TPU v7x, 32 devices: a whole 2x2x4 slice. The times are simulated.
32 devices in a mesh: seq: 16 (over z, y, x), mp: 2 (over core).
Axes of the slice: x: 2, y: 2, z: 4, core: 2. Of those that a mesh axis runs over, the one named last changes fastest.
Arguments:
- tokens: bfloat16 [2, 6144, 768], P(None, 'seq'), may hold values from -6 to 6
- out_grad: bfloat16 [2, 6144, 768], P(None, 'seq'), may hold values from -6 to 6
- gains: float32 [768, 2], replicated, may hold values from 0.5 to 1.5
- routers: float32 [768, 3], replicated, may hold values from -0.21875 to 0.21875
- light_query_key_value_weight: bfloat16 [768, 3, 768], P(None, None, 'mp'), may hold values from -0.21875 to 0.21875
- light_attention_output_weight: bfloat16 [768, 768], P(None, 'mp'), may hold values from -1.75 to 1.75
- heavy_qkv: bfloat16 [768, 3, 768], P(None, None, 'mp'), may hold values from -0.21875 to 0.21875
- heavy_out: bfloat16 [768, 768], P(None, 'mp'), may hold values from -6 to 6
- light_feedforward_input_weight: bfloat16 [768, 2, 1024], P(None, None, 'mp'), may hold values from -0.21875 to 0.21875
- light_feedforward_output_weight: bfloat16 [768, 1024], P(None, 'mp'), may hold values from -0.1875 to 0.1875
- heavy_mlp_in: bfloat16 [768, 2, 4096], P(None, None, 'mp'), may hold values from -0.21875 to 0.21875
- heavy_mlp_out: bfloat16 [768, 4096], P(None, 'mp'), may hold values from -0.09375 to 0.09375
- routed_queries: int32 [2, 1536], P(None, 'seq'), may hold values from 0 to 6143, as said below
- routed_keys: int32 [2, 1536], P(None, 'seq'), may hold values from 0 to 6143, as said below
- routed_mlp: int32 [2, 1536], P(None, 'seq'), may hold values from 0 to 6143, as said below
- block_counts: int32 [2, 16, 3], P(None, 'seq'), may hold values from 1 to 96, as said below
Outputs:
- mixed: bfloat16 [2, 6144, 768], P(None, 'seq')
- input_grad: float32 [2, 6144, 768], P(None, 'seq')
- light_qkv_grad: float32 [768, 3, 768], P(None, None, 'mp')
- light_out_grad: float32 [768, 768], P(None, 'mp')
- heavy_qkv_grad: float32 [768, 3, 768], P(None, None, 'mp')
- heavy_out_grad: float32 [768, 768], P(None, 'mp')
- light_mlp_in_grad: float32 [768, 2, 1024], P(None, None, 'mp')
- light_mlp_out_grad: float32 [768, 1024], P(None, 'mp')
- heavy_mlp_in_grad: float32 [768, 2, 4096], P(None, None, 'mp')
- heavy_mlp_out_grad: float32 [768, 4096], P(None, 'mp')
- gains_grad: float32 [768, 2], replicated
- routers_grad: float32 [768, 3], replicated
Inputs may be any that keep to these rules, and one draw needn't show every extreme that they name: block_counts[s,b,k] slots of block b of sequence s are used for kind k; in every draw some block of each kind uses all 96 slots and some uses one. `routed_queries`: slots c * 96 to c * 96 + 95 belong to block c, positions c * 384 to c * 384 + 383 of the sequence; used slots hold distinct positions in rising order, unused slots repeat the block's first slot. `routed_keys`: as for routed_queries, with kind 1 of block_counts. `routed_mlp`: as for routed_queries, with kind 2 of block_counts.
All inputs are finite; a program needn't handle non-finite values.
Results may differ from a plain program's by a relative error of at most 0.022.
Values may be sent and summed in bfloat16 or wider, within the bound.
No kernel may reach another device: no remote copies, remote signals or barrier semaphores. Data moves between devices by JAX's collectives and lax.ppermute only.
A program may use at most 512 MiB of HBM per device.

v0:
```python
import math

import jax
import jax.numpy as jnp
from jax import lax
from jax.sharding import PartitionSpec as P

LHD = 96
HHD = 64
WIN = 128


EPSILON = 1e-06
MASKED = -1e30
TOP_PRECISION = lax.Precision.HIGHEST


def padded(value, sides, width):
    for axis, dim in sides:
        peers, length = (lax.axis_size(axis), value.shape[dim])
        up = [(i, (i + 1) % peers) for i in range(peers - 1)]
        down = [(j, i) for i, j in up]
        last = lax.slice_in_dim(value, length - width, length, axis=dim)
        leading = lax.slice_in_dim(value, 0, width, axis=dim)
        before = lax.ppermute(last, axis, up)
        after = lax.ppermute(leading, axis, down)
        value = jnp.concatenate([before, value, after], axis=dim)
    return value


def norm_rows(values, gain_vec):
    factor = lax.rsqrt(jnp.mean(values * values, axis=-1, keepdims=True) + EPSILON)
    return (values * factor * gain_vec, factor)


def norm_back(values, factor, gain_vec, grad_in):
    weighted = grad_in * gain_vec
    inner = jnp.mean(weighted * values, axis=-1, keepdims=True)
    return factor * weighted - values * (factor * factor * factor) * inner


def gated_gelu(gate_in, up_in):
    return jax.nn.gelu(gate_in, approximate=True) * up_in


def pick_rows(source, where_rows):
    seq_ids = jnp.arange(source.shape[0], dtype=jnp.int32)[:, None]
    return source[seq_ids, where_rows]


def add_rows(target, where_rows, values):
    seq_ids = jnp.arange(target.shape[0], dtype=jnp.int32)[:, None]
    return target.at[seq_ids, where_rows].add(values)


def windows(extended, blocks, tile_width):
    dims_in = extended.shape
    tile_view = extended.reshape((dims_in[0], blocks + 2, tile_width) + dims_in[2:])
    return jnp.concatenate([tile_view[:, :-2], tile_view[:, 1:-1], tile_view[:, 2:]], axis=2)


def unwindows(tiled, tile_width):
    first_part = tiled[:, :, :tile_width]
    second_part = tiled[:, :, tile_width : 2 * tile_width]
    third_part = tiled[:, :, 2 * tile_width :]
    zero_tile = jnp.zeros_like(first_part[:, :1])
    summed_tiles = (
        jnp.concatenate([first_part, zero_tile, zero_tile], axis=1)
        + jnp.concatenate([zero_tile, second_part, zero_tile], axis=1)
        + jnp.concatenate([zero_tile, zero_tile, third_part], axis=1)
    )
    dims_in = summed_tiles.shape
    return summed_tiles.reshape((dims_in[0], dims_in[1] * dims_in[2]) + dims_in[3:])


def window_mask(blocks, tile_width, row_base, length):
    row_ids = jnp.arange(tile_width, dtype=jnp.int32)
    col_ids = jnp.arange(3 * tile_width, dtype=jnp.int32)
    tile_ids = jnp.arange(blocks, dtype=jnp.int32)
    within = jnp.abs(col_ids[None, :] - tile_width - row_ids[:, None]) < tile_width
    key_place = row_base + tile_ids[:, None] * tile_width + col_ids[None, :] - tile_width
    inside = (key_place >= 0) & (key_place < length)
    return within[None, :, :] & inside[:, None, :]


def heavy_scores(queries, key_heads, key_flags, scale_value):
    plain = (
        jnp.einsum("sqhd,skhd->shqk", queries, key_heads, preferred_element_type=jnp.float32)
        * scale_value
    )
    return jnp.where(key_flags[:, None, None, :] > 0, plain, MASKED)


def shards(
    tokens,
    out_grad,
    gains,
    routers,
    light_query_key_value_weight,
    light_attention_output_weight,
    heavy_qkv,
    heavy_out,
    light_feedforward_input_weight,
    light_feedforward_output_weight,
    heavy_mlp_in,
    heavy_mlp_out,
    routed_queries,
    routed_keys,
    routed_mlp,
    block_counts,
):
    seq_count, local_len, model_width = tokens.shape
    seq_devices = lax.axis_size("seq")
    row_base = lax.axis_index("seq") * local_len
    full_len = seq_devices * local_len
    blocks = local_len // WIN
    light_cols = light_query_key_value_weight.shape[2]
    light_heads = light_cols // LHD
    heavy_cols = heavy_qkv.shape[2]
    heavy_heads = heavy_cols // HHD
    capacity = routed_queries.shape[1]
    light_scale = 1.0 / math.sqrt(LHD)
    heavy_scale = 1.0 / math.sqrt(HHD)
    inputs = tokens.astype(jnp.float32)
    normed, factor_one = norm_rows(inputs, gains[:, 0])
    normalized_lower_precision = normed.astype(jnp.bfloat16)
    light_projected_rows = jnp.einsum(
        "std,djc->stjc",
        normalized_lower_precision,
        light_query_key_value_weight,
        preferred_element_type=jnp.float32,
    ).astype(jnp.bfloat16)
    extended = padded(light_projected_rows[:, :, 1:], (("seq", 1),), WIN)
    query_tiles = light_projected_rows[:, :, 0].reshape(seq_count, blocks, WIN, light_heads, LHD)
    key_tiles = windows(extended[:, :, 0], blocks, WIN).reshape(
        seq_count, blocks, 3 * WIN, light_heads, LHD
    )
    value_tiles = windows(extended[:, :, 1], blocks, WIN).reshape(
        seq_count, blocks, 3 * WIN, light_heads, LHD
    )
    allowed = window_mask(blocks, WIN, row_base, full_len)[None, :, None]
    light_scores = (
        jnp.einsum("sbihd,sbjhd->sbhij", query_tiles, key_tiles, preferred_element_type=jnp.float32)
        * light_scale
    )
    light_scores = jnp.where(allowed, light_scores, MASKED)
    top_light = jnp.max(light_scores, axis=-1, keepdims=True)
    expo_light = jnp.exp(light_scores - top_light)
    sum_light = jnp.sum(expo_light, axis=-1, keepdims=True)
    light_probs = expo_light / sum_light
    light_lse = top_light + jnp.log(sum_light)
    light_blended_rows = jnp.einsum(
        "sbhij,sbjhd->sbihd",
        light_probs.astype(jnp.bfloat16),
        value_tiles,
        preferred_element_type=jnp.float32,
    )
    light_blended_rows = light_blended_rows.astype(jnp.bfloat16).reshape(
        seq_count, local_len, light_cols
    )
    attn_part = jnp.einsum(
        "stc,dc->std",
        light_blended_rows,
        light_attention_output_weight,
        preferred_element_type=jnp.float32,
    )
    counts_here = block_counts[:, 0, :]
    slot_ids = jnp.arange(capacity, dtype=jnp.int32)[None, :]
    valid_query = slot_ids < counts_here[:, 0:1]
    valid_key = slot_ids < counts_here[:, 1:2]
    valid_mlp = slot_ids < counts_here[:, 2:3]
    query_rows = routed_queries - row_base
    key_rows = routed_keys - row_base
    mlp_rows = routed_mlp - row_base
    query_in = pick_rows(normalized_lower_precision, query_rows)
    query_norm = pick_rows(normed, query_rows)
    query_gate = jax.nn.sigmoid(
        jnp.einsum("scd,d->sc", query_norm, routers[:, 0], precision=TOP_PRECISION)
    )
    heavy_query = jnp.einsum(
        "scd,dk->sck", query_in, heavy_qkv[:, 0], preferred_element_type=jnp.float32
    ).astype(jnp.bfloat16)
    key_in = pick_rows(normalized_lower_precision, key_rows)
    key_norm = pick_rows(normed, key_rows)
    key_gate = jax.nn.sigmoid(
        jnp.einsum("scd,d->sc", key_norm, routers[:, 1], precision=TOP_PRECISION)
    )
    key_both = jnp.einsum(
        "scd,djk->scjk", key_in, heavy_qkv[:, 1:], preferred_element_type=jnp.float32
    )
    heavy_key = key_both[:, :, 0].astype(jnp.bfloat16)
    raw_value = key_both[:, :, 1]
    heavy_value = (key_gate[..., None] * raw_value).astype(jnp.bfloat16)
    key_flag = valid_key.astype(jnp.bfloat16)
    all_keys, all_values, all_flags = (
        lax.all_gather(heavy_key, "seq", axis=1, tiled=True),
        lax.all_gather(heavy_value, "seq", axis=1, tiled=True),
        lax.all_gather(key_flag, "seq", axis=1, tiled=True),
    )
    key_heads = all_keys.reshape(seq_count, -1, heavy_heads, HHD)
    value_heads = all_values.reshape(seq_count, -1, heavy_heads, HHD)
    query_heads = heavy_query.reshape(seq_count, capacity, heavy_heads, HHD)
    scores_heavy = heavy_scores(query_heads, key_heads, all_flags, heavy_scale)
    top_heavy = jnp.max(scores_heavy, axis=-1, keepdims=True)
    expo_heavy = jnp.exp(scores_heavy - top_heavy)
    sum_heavy = jnp.sum(expo_heavy, axis=-1, keepdims=True)
    heavy_probs = expo_heavy / sum_heavy
    heavy_lse = (top_heavy + jnp.log(sum_heavy))[..., 0]
    heavy_mix = jnp.einsum(
        "shqk,skhd->sqhd",
        heavy_probs.astype(jnp.bfloat16),
        value_heads,
        preferred_element_type=jnp.float32,
    )
    heavy_mix = heavy_mix.reshape(seq_count, capacity, heavy_cols).astype(jnp.bfloat16)
    heavy_rows = jnp.einsum("sck,dk->scd", heavy_mix, heavy_out, preferred_element_type=jnp.float32)
    query_weight = jnp.where(valid_query, query_gate, 0.0)
    attn_part = add_rows(attn_part, query_rows, query_weight[..., None] * heavy_rows)
    attention_layer = lax.psum(attn_part.astype(jnp.bfloat16), "mp").astype(jnp.float32)
    middle = inputs + attention_layer
    normed_two, factor_two = norm_rows(middle, gains[:, 1])
    lower_precision_second = normed_two.astype(jnp.bfloat16)
    paired_gate_values = jnp.einsum(
        "std,dkf->stkf",
        lower_precision_second,
        light_feedforward_input_weight,
        preferred_element_type=jnp.float32,
    )
    hidden_activations = gated_gelu(
        paired_gate_values[:, :, 0], paired_gate_values[:, :, 1]
    ).astype(jnp.bfloat16)
    feedforward_portion = jnp.einsum(
        "stf,df->std",
        hidden_activations,
        light_feedforward_output_weight,
        preferred_element_type=jnp.float32,
    )
    mlp_in = pick_rows(lower_precision_second, mlp_rows)
    mlp_norm = pick_rows(normed_two, mlp_rows)
    mlp_gate = jax.nn.sigmoid(
        jnp.einsum("scd,d->sc", mlp_norm, routers[:, 2], precision=TOP_PRECISION)
    )
    heavy_gates = jnp.einsum(
        "scd,dkf->sckf", mlp_in, heavy_mlp_in, preferred_element_type=jnp.float32
    )
    heavy_hidden = gated_gelu(heavy_gates[:, :, 0], heavy_gates[:, :, 1]).astype(jnp.bfloat16)
    heavy_mlp_rows = jnp.einsum(
        "scf,df->scd", heavy_hidden, heavy_mlp_out, preferred_element_type=jnp.float32
    )
    mlp_weight = jnp.where(valid_mlp, mlp_gate, 0.0)
    feedforward_portion = add_rows(
        feedforward_portion, mlp_rows, mlp_weight[..., None] * heavy_mlp_rows
    )
    mlp_total = lax.psum(feedforward_portion.astype(jnp.bfloat16), "mp").astype(jnp.float32)
    result = (middle + mlp_total).astype(jnp.bfloat16)
    upstream = out_grad.astype(jnp.float32)
    hidden_grad = jnp.einsum(
        "std,df->stf", out_grad, light_feedforward_output_weight, preferred_element_type=jnp.float32
    )
    unused_light, pull_light = jax.vjp(
        gated_gelu, paired_gate_values[:, :, 0], paired_gate_values[:, :, 1]
    )
    gate_grad, up_grad = pull_light(hidden_grad)
    gates_grad = jnp.stack([gate_grad, up_grad], axis=2).astype(jnp.bfloat16)
    light_mlp_out_grad = jnp.einsum(
        "std,stf->df", out_grad, hidden_activations, preferred_element_type=jnp.float32
    )
    light_mlp_in_grad = jnp.einsum(
        "std,stkf->dkf", lower_precision_second, gates_grad, preferred_element_type=jnp.float32
    )
    low_two_grad = jnp.einsum(
        "stkf,dkf->std",
        gates_grad,
        light_feedforward_input_weight,
        preferred_element_type=jnp.float32,
    )
    mlp_upstream = pick_rows(out_grad, mlp_rows).astype(jnp.float32)
    slot_mlp_grad = (mlp_weight[..., None] * mlp_upstream).astype(jnp.bfloat16)
    mlp_gate_grad = jnp.sum(mlp_upstream * heavy_mlp_rows, axis=-1)
    heavy_mlp_out_grad = jnp.einsum(
        "scd,scf->df", slot_mlp_grad, heavy_hidden, preferred_element_type=jnp.float32
    )
    heavy_hidden_grad = jnp.einsum(
        "scd,df->scf", slot_mlp_grad, heavy_mlp_out, preferred_element_type=jnp.float32
    )
    unused_heavy, pull_heavy = jax.vjp(gated_gelu, heavy_gates[:, :, 0], heavy_gates[:, :, 1])
    heavy_gate_grad, heavy_up_grad = pull_heavy(heavy_hidden_grad)
    heavy_gates_grad = jnp.stack([heavy_gate_grad, heavy_up_grad], axis=2).astype(jnp.bfloat16)
    heavy_mlp_in_grad = jnp.einsum(
        "scd,sckf->dkf", mlp_in, heavy_gates_grad, preferred_element_type=jnp.float32
    )
    low_two_grad = add_rows(
        low_two_grad,
        mlp_rows,
        jnp.einsum(
            "sckf,dkf->scd", heavy_gates_grad, heavy_mlp_in, preferred_element_type=jnp.float32
        ),
    )
    normed_two_grad, mlp_gate_sum = (
        lax.psum(low_two_grad.astype(jnp.bfloat16), "mp").astype(jnp.float32),
        lax.psum(mlp_gate_grad.astype(jnp.bfloat16), "mp").astype(jnp.float32),
    )
    mlp_logit_grad = jnp.where(valid_mlp, mlp_gate_sum * mlp_gate * (1.0 - mlp_gate), 0.0)
    normed_two_grad = add_rows(normed_two_grad, mlp_rows, mlp_logit_grad[..., None] * routers[:, 2])
    router_mlp_grad = jnp.einsum("sc,scd->d", mlp_logit_grad, mlp_norm, precision=TOP_PRECISION)
    gain_mlp_grad = jnp.sum(normed_two_grad * middle * factor_two, axis=(0, 1))
    middle_grad = upstream + norm_back(middle, factor_two, gains[:, 1], normed_two_grad)
    attn_low = middle_grad.astype(jnp.bfloat16)
    light_out_grad = jnp.einsum(
        "std,stc->dc", attn_low, light_blended_rows, preferred_element_type=jnp.float32
    )
    mix_grad = jnp.einsum(
        "std,dc->stc", attn_low, light_attention_output_weight, preferred_element_type=jnp.float32
    ).astype(jnp.bfloat16)
    mix_grad = mix_grad.reshape(seq_count, blocks, WIN, light_heads, LHD)
    probs_light = jnp.exp(light_scores - light_lse)
    light_prob_grad = jnp.einsum(
        "sbihd,sbjhd->sbhij", mix_grad, value_tiles, preferred_element_type=jnp.float32
    )
    light_delta = jnp.sum(probs_light * light_prob_grad, axis=-1, keepdims=True)
    light_score_grad = (probs_light * (light_prob_grad - light_delta)).astype(jnp.bfloat16)
    light_query_grad = (
        jnp.einsum(
            "sbhij,sbjhd->sbihd", light_score_grad, key_tiles, preferred_element_type=jnp.float32
        )
        * light_scale
    )
    light_query_grad = light_query_grad.reshape(seq_count, local_len, light_cols)
    light_key_win = (
        jnp.einsum(
            "sbhij,sbihd->sbjhd", light_score_grad, query_tiles, preferred_element_type=jnp.float32
        )
        * light_scale
    )
    light_value_win = jnp.einsum(
        "sbhij,sbihd->sbjhd",
        probs_light.astype(jnp.bfloat16),
        mix_grad,
        preferred_element_type=jnp.float32,
    )
    pair_win = jnp.stack(
        [
            light_key_win.reshape(seq_count, blocks, 3 * WIN, light_cols),
            light_value_win.reshape(seq_count, blocks, 3 * WIN, light_cols),
        ],
        axis=3,
    )
    pair_rows = unwindows(pair_win, WIN)
    rim_rows = jnp.concatenate([pair_rows[:, :WIN], pair_rows[:, local_len + WIN :]], axis=1)
    rim_back = padded(rim_rows.astype(jnp.bfloat16), (("seq", 1),), WIN).astype(rim_rows.dtype)
    pair_grad = pair_rows[:, WIN : WIN + local_len]
    pair_grad = pair_grad.at[:, :WIN].add(rim_back[:, :WIN])
    pair_grad = pair_grad.at[:, local_len - WIN :].add(rim_back[:, 3 * WIN :])
    light_grad = jnp.concatenate(
        [light_query_grad.astype(jnp.bfloat16)[:, :, None], pair_grad.astype(jnp.bfloat16)], axis=2
    )
    light_qkv_grad = jnp.einsum(
        "std,stjc->djc", normalized_lower_precision, light_grad, preferred_element_type=jnp.float32
    )
    input_low_grad = jnp.einsum(
        "stjc,djc->std",
        light_grad,
        light_query_key_value_weight,
        preferred_element_type=jnp.float32,
    )
    attn_upstream = pick_rows(attn_low, query_rows).astype(jnp.float32)
    slot_attn_grad = (query_weight[..., None] * attn_upstream).astype(jnp.bfloat16)
    query_gate_grad = jnp.sum(attn_upstream * heavy_rows, axis=-1)
    heavy_out_grad = jnp.einsum(
        "scd,sck->dk", slot_attn_grad, heavy_mix, preferred_element_type=jnp.float32
    )
    heavy_mix_grad = jnp.einsum(
        "scd,dk->sck", slot_attn_grad, heavy_out, preferred_element_type=jnp.float32
    ).astype(jnp.bfloat16)
    grad_heads = heavy_mix_grad.reshape(seq_count, capacity, heavy_heads, HHD)
    probs_again = jnp.exp(scores_heavy - heavy_lse[..., None])
    prob_grad = jnp.einsum(
        "sqhd,skhd->shqk", grad_heads, value_heads, preferred_element_type=jnp.float32
    )
    heavy_delta = jnp.sum(probs_again * prob_grad, axis=-1)
    score_grad = (probs_again * (prob_grad - heavy_delta[..., None])).astype(jnp.bfloat16)
    query_grad = (
        jnp.einsum("shqk,skhd->sqhd", score_grad, key_heads, preferred_element_type=jnp.float32)
        * heavy_scale
    )
    query_grad = query_grad.reshape(seq_count, capacity, heavy_cols).astype(jnp.bfloat16)
    every_query, every_grad = (
        lax.all_gather(heavy_query, "seq", axis=1, tiled=True),
        lax.all_gather(heavy_mix_grad, "seq", axis=1, tiled=True),
    )
    every_lse, every_delta = (
        lax.all_gather(heavy_lse, "seq", axis=2, tiled=True),
        lax.all_gather(heavy_delta, "seq", axis=2, tiled=True),
    )
    query_all = every_query.reshape(seq_count, -1, heavy_heads, HHD)
    grad_all = every_grad.reshape(seq_count, -1, heavy_heads, HHD)
    own_keys = heavy_key.reshape(seq_count, capacity, heavy_heads, HHD)
    own_values = heavy_value.reshape(seq_count, capacity, heavy_heads, HHD)
    own_probs = jnp.exp(
        heavy_scores(query_all, own_keys, key_flag, heavy_scale) - every_lse[..., None]
    )
    own_prob_grad = jnp.einsum(
        "sqhd,skhd->shqk", grad_all, own_values, preferred_element_type=jnp.float32
    )
    own_score_grad = (own_probs * (own_prob_grad - every_delta[..., None])).astype(jnp.bfloat16)
    key_grad = (
        jnp.einsum("shqk,sqhd->skhd", own_score_grad, query_all, preferred_element_type=jnp.float32)
        * heavy_scale
    )
    key_grad = key_grad.reshape(seq_count, capacity, heavy_cols)
    value_grad = jnp.einsum(
        "shqk,sqhd->skhd",
        own_probs.astype(jnp.bfloat16),
        grad_all,
        preferred_element_type=jnp.float32,
    )
    value_grad = value_grad.reshape(seq_count, capacity, heavy_cols)
    key_grad_low = key_grad.astype(jnp.bfloat16)
    value_grad_low = value_grad.astype(jnp.bfloat16).astype(jnp.float32)
    raw_grad = (key_gate[..., None] * value_grad_low).astype(jnp.bfloat16)
    key_gate_grad = jnp.sum(value_grad_low * raw_value, axis=-1)
    key_pair_grad = jnp.stack([key_grad_low, raw_grad], axis=2)
    heavy_qkv_grad = jnp.concatenate(
        [
            jnp.einsum("scd,sck->dk", query_in, query_grad, preferred_element_type=jnp.float32)[
                :, None
            ],
            jnp.einsum("scd,scjk->djk", key_in, key_pair_grad, preferred_element_type=jnp.float32),
        ],
        axis=1,
    )
    input_low_grad = add_rows(
        input_low_grad,
        query_rows,
        jnp.einsum("sck,dk->scd", query_grad, heavy_qkv[:, 0], preferred_element_type=jnp.float32),
    )
    input_low_grad = add_rows(
        input_low_grad,
        key_rows,
        jnp.einsum(
            "scjk,djk->scd", key_pair_grad, heavy_qkv[:, 1:], preferred_element_type=jnp.float32
        ),
    )
    normed_grad, query_gate_sum, key_gate_sum = (
        lax.psum(input_low_grad.astype(jnp.bfloat16), "mp").astype(jnp.float32),
        lax.psum(query_gate_grad.astype(jnp.bfloat16), "mp").astype(jnp.float32),
        lax.psum(key_gate_grad.astype(jnp.bfloat16), "mp").astype(jnp.float32),
    )
    query_logit_grad = jnp.where(valid_query, query_gate_sum * query_gate * (1.0 - query_gate), 0.0)
    key_logit_grad = jnp.where(valid_key, key_gate_sum * key_gate * (1.0 - key_gate), 0.0)
    normed_grad = add_rows(normed_grad, query_rows, query_logit_grad[..., None] * routers[:, 0])
    normed_grad = add_rows(normed_grad, key_rows, key_logit_grad[..., None] * routers[:, 1])
    router_query_grad = jnp.einsum(
        "sc,scd->d", query_logit_grad, query_norm, precision=TOP_PRECISION
    )
    router_key_grad = jnp.einsum("sc,scd->d", key_logit_grad, key_norm, precision=TOP_PRECISION)
    gain_attn_grad = jnp.sum(normed_grad * inputs * factor_one, axis=(0, 1))
    input_grad = middle_grad + norm_back(inputs, factor_one, gains[:, 0], normed_grad)
    gains_grad = jnp.stack([gain_attn_grad, gain_mlp_grad], axis=1)
    routers_grad = jnp.stack([router_query_grad, router_key_grad, router_mlp_grad], axis=1)
    (
        sum_light_qkv,
        sum_light_out,
        sum_heavy_qkv,
        sum_heavy_out,
        sum_light_in,
        sum_light_down,
        sum_heavy_in,
        sum_heavy_down,
        sum_gains,
        sum_routers,
    ) = (
        lax.psum_scatter(light_qkv_grad, "seq", scatter_dimension=0, tiled=True),
        lax.psum_scatter(light_out_grad, "seq", scatter_dimension=0, tiled=True),
        lax.psum_scatter(heavy_qkv_grad, "seq", scatter_dimension=0, tiled=True),
        lax.psum_scatter(heavy_out_grad, "seq", scatter_dimension=0, tiled=True),
        lax.psum_scatter(light_mlp_in_grad, "seq", scatter_dimension=0, tiled=True),
        lax.psum_scatter(light_mlp_out_grad, "seq", scatter_dimension=0, tiled=True),
        lax.psum_scatter(heavy_mlp_in_grad, "seq", scatter_dimension=0, tiled=True),
        lax.psum_scatter(heavy_mlp_out_grad, "seq", scatter_dimension=0, tiled=True),
        lax.psum_scatter(gains_grad, "seq", scatter_dimension=0, tiled=True),
        lax.psum_scatter(routers_grad, "seq", scatter_dimension=0, tiled=True),
    )
    shared = (
        lax.all_gather(sum_light_qkv.astype(jnp.bfloat16), "seq", axis=0, tiled=True).astype(
            sum_light_qkv.dtype
        ),
        lax.all_gather(sum_light_out.astype(jnp.bfloat16), "seq", axis=0, tiled=True).astype(
            sum_light_out.dtype
        ),
        lax.all_gather(sum_heavy_qkv.astype(jnp.bfloat16), "seq", axis=0, tiled=True).astype(
            sum_heavy_qkv.dtype
        ),
        lax.all_gather(sum_heavy_out.astype(jnp.bfloat16), "seq", axis=0, tiled=True).astype(
            sum_heavy_out.dtype
        ),
        lax.all_gather(sum_light_in.astype(jnp.bfloat16), "seq", axis=0, tiled=True).astype(
            sum_light_in.dtype
        ),
        lax.all_gather(sum_light_down.astype(jnp.bfloat16), "seq", axis=0, tiled=True).astype(
            sum_light_down.dtype
        ),
        lax.all_gather(sum_heavy_in.astype(jnp.bfloat16), "seq", axis=0, tiled=True).astype(
            sum_heavy_in.dtype
        ),
        lax.all_gather(sum_heavy_down.astype(jnp.bfloat16), "seq", axis=0, tiled=True).astype(
            sum_heavy_down.dtype
        ),
        lax.all_gather(sum_gains.astype(jnp.bfloat16), "seq", axis=0, tiled=True).astype(
            sum_gains.dtype
        ),
        lax.all_gather(sum_routers.astype(jnp.bfloat16), "seq", axis=0, tiled=True).astype(
            sum_routers.dtype
        ),
    )
    return (
        result,
        input_grad,
        shared[0],
        shared[1],
        shared[2],
        shared[3],
        shared[4],
        shared[5],
        shared[6],
        shared[7],
        shared[8],
        shared[9],
    )


def solution(mesh):
    placed = (
        P(None, "seq", None),
        P(None, "seq", None),
        P(),
        P(),
        P(None, None, "mp"),
        P(None, "mp"),
        P(None, None, "mp"),
        P(None, "mp"),
        P(None, None, "mp"),
        P(None, "mp"),
        P(None, None, "mp"),
        P(None, "mp"),
        P(None, "seq"),
        P(None, "seq"),
        P(None, "seq"),
        P(None, "seq", None),
    )
    return jax.shard_map(
        shards,
        mesh=mesh,
        in_specs=placed,
        out_specs=(
            P(None, "seq", None),
            P(None, "seq", None),
            P(None, None, "mp"),
            P(None, "mp"),
            P(None, None, "mp"),
            P(None, "mp"),
            P(None, None, "mp"),
            P(None, "mp"),
            P(None, None, "mp"),
            P(None, "mp"),
            P(),
            P(),
        ),
        check_vma=False,
    )
```

profile of v0, /device:TPU:0, one launch (start us, length us, event | category | flops | bytes accessed | tf_op | source)
XLA Modules:
  0.0 2379.2 jit_solution(8223036079652446552)
XLA Ops:
  15.1 6.1 gather_fusion.1
  23.5 5.3 gather_fusion.2
  39.9 7.2 collective-permute-start
  47.7 8.1 gather_fusion.3
  63.3 11.5 gather_fusion
  83.2 35.3 %all-gather.1 = bf16[16,96,2]{1,2,0:T(2,128)(2,1)S(1)} all-gather(bf16[1,96,2]{1,2,0:T(2,128)(2,1)S(1)} %get-tuple-element.164), channel_id=1, replica_groups=mesh['seq'=16,'mp'=2] {'seq'}, dimensions={0}, use_global_device_ids=true | all-gather | bytes 6528 | tf_op jit(solution)/shard_map/all_gather | solution.py:198
  155.6 15.1 all-gather.30.cloned.1.call-done
  184.7 32.9 %scatter_fusion = f32[2,384,768]{2,1,0:T(8,128)} fusion(f32[2,384,768]{2,1,0:T(8,128)} %fusion.113, s32[192]{0:T(256)S(1)} %reshape.401, f32[192,768]{1,0:T(8,128)} %bitcast.422), kind=kCustom, calls=%fused_computation.8 | custom fusion | flops 147456 | bytes 1771008 | tf_op jit(solution)/shard_map/scatter-add | solution.py:53
  229.5 51.6 %all_gather.55 = f32[2,6,1536]{1,0,2:T(2,128)} all-gather(f32[2,6,96]{1,0,2:T(2,128)} %copy.276), channel_id=1, replica_groups=mesh['seq'=16,'mp'=2] {'seq'}, dimensions={2}, use_global_device_ids=true | all-gather | bytes 78336 | tf_op jit(solution)/shard_map/all_gather | solution.py:392
  293.0 5.9 gather_fusion.5
  303.8 6.9 fusion.2
  334.9 11.7 scatter_fusion.2
  348.3 5.8 fusion.177
  355.0 11.7 scatter_fusion.1
  371.2 11.7 scatter_fusion.3
  396.3 6.3 multiply_reduce_fusion.1
  421.6 5.6 copy.270
  431.1 5.3 collective-permute-start.2
  454.4 65.8 %all_gather.57 = f32[2,6,1536]{1,0,2:T(2,128)} all-gather(f32[2,6,96]{1,0,2:T(2,128)} %copy.280), channel_id=1, replica_groups=mesh['seq'=16,'mp'=2] {'seq'}, dimensions={2}, use_global_device_ids=true | all-gather | bytes 78336 | tf_op jit(solution)/shard_map/all_gather | solution.py:393
  532.0 11.8 scatter_fusion.4
  548.1 5.6 fusion.86
  554.6 7.7 fusion.81
  565.1 11.7 scatter_fusion.5
  599.7 6.6 convolution_bitcast_fusion
  625.7 11.8 scatter_fusion.6
  637.5 18.2 scatter_fusion.7
  658.9 75.1 %reduce-scatter.25.cloned.1.call-done = f32[48,2,512]{2,0,1:T(8,128)} async-done(((f32[768,2,512]{2,0,1:T(8,128)}), f32[48,2,512]{2,0,1:T(8,128)}) %reduce-scatter.25.cloned.1.call-update) | async-done | bytes 196624 | tf_op jit(solution)/shard_map/reduce_scatter | solution.py:477
  735.7 137.3 %reduce-scatter.17.cloned.1.call-done = f32[48,3,384]{2,0,1:T(8,128)} async-done(((f32[768,3,384]{2,0,1:T(8,128)}), f32[48,3,384]{2,0,1:T(8,128)}) %reduce-scatter.17.cloned.1.call-update) | async-done | bytes 221200 | tf_op jit(solution)/shard_map/reduce_scatter | solution.py:473
  874.7 137.6 %reduce-scatter.21.cloned.1.call-done = f32[48,3,384]{2,0,1:T(8,128)} async-done(((f32[768,3,384]{2,0,1:T(8,128)}), f32[48,3,384]{2,0,1:T(8,128)}) %reduce-scatter.21.cloned.1.call-update) | async-done | bytes 221200 | tf_op jit(solution)/shard_map/reduce_scatter | solution.py:475
  1013.9 149.7 %reduce-scatter.29.cloned.1.call-done = f32[48,2048]{1,0:T(8,128)} async-done(((f32[768,2048]{1,0:T(8,128)}), f32[48,2048]{1,0:T(8,128)}) %reduce-scatter.29.cloned.1.call-update) | async-done | bytes 393232 | tf_op jit(solution)/shard_map/reduce_scatter | solution.py:480
  1165.3 208.5 %reduce-scatter.27.cloned.1.call-done = f32[48,2,2048]{2,0,1:T(8,128)} async-done(((f32[768,2,2048]{2,0,1:T(8,128)}), f32[48,2,2048]{2,0,1:T(8,128)}) %reduce-scatter.27.cloned.1.call-update) | async-done | bytes 786448 | tf_op jit(solution)/shard_map/reduce_scatter | solution.py:479
  1375.8 127.6 %reduce-scatter.31.cloned.1.call-done = f32[48,512]{1,0:T(8,128)} async-done(((f32[768,512]{1,0:T(8,128)}), f32[48,512]{1,0:T(8,128)}) %reduce-scatter.31.cloned.1.call-update) | async-done | bytes 98320 | tf_op jit(solution)/shard_map/reduce_scatter | solution.py:478
  1504.2 44.1 %all_gather.63 = bf16[768,512]{1,0:T(8,128)(2,1)S(1)} all-gather(bf16[48,512]{1,0:T(8,128)(2,1)S(1)} %convert_element_type.383), channel_id=1, replica_groups=mesh['seq'=16,'mp'=2] {'seq'}, dimensions={0}, use_global_device_ids=true | all-gather | bytes 835584 | tf_op jit(solution)/shard_map/all_gather | solution.py:500
  1549.7 81.5 %reduce-scatter.19.cloned.1.call-done = f32[48,384]{1,0:T(8,128)} async-done(((f32[768,384]{1,0:T(8,128)}), f32[48,384]{1,0:T(8,128)}) %reduce-scatter.19.cloned.1.call-update) | async-done | bytes 73744 | tf_op jit(solution)/shard_map/reduce_scatter | solution.py:474
  1632.1 42.9 %all_gather.59 = bf16[768,384]{1,0:T(8,128)(2,1)S(1)} all-gather(bf16[48,384]{1,0:T(8,128)(2,1)S(1)} %convert_element_type.375), channel_id=1, replica_groups=mesh['seq'=16,'mp'=2] {'seq'}, dimensions={0}, use_global_device_ids=true | all-gather | bytes 626688 | tf_op jit(solution)/shard_map/all_gather | solution.py:488
  1676.1 83.2 %reduce-scatter.23.cloned.1.call-done = f32[48,384]{1,0:T(8,128)} async-done(((f32[768,384]{1,0:T(8,128)}), f32[48,384]{1,0:T(8,128)}) %reduce-scatter.23.cloned.1.call-update) | async-done | bytes 73744 | tf_op jit(solution)/shard_map/reduce_scatter | solution.py:476
  1760.1 42.5 %all_gather.61 = bf16[768,384]{1,0:T(8,128)(2,1)S(1)} all-gather(bf16[48,384]{1,0:T(8,128)(2,1)S(1)} %convert_element_type.379), channel_id=1, replica_groups=mesh['seq'=16,'mp'=2] {'seq'}, dimensions={0}, use_global_device_ids=true | all-gather | bytes 626688 | tf_op jit(solution)/shard_map/all_gather | solution.py:494
  1803.7 80.8 %reduce-scatter.35.cloned.1.call-done = f32[48,3]{1,0:T(8,128)} async-done(((f32[768,3]{1,0:T(8,128)}), f32[48,3]{1,0:T(8,128)}) %reduce-scatter.35.cloned.1.call-update) | async-done | bytes 592
  1885.3 38.8 %all-gather.3 = bf16[16,48,3]{1,2,0:T(4,128)(2,1)S(1)} all-gather(bf16[1,48,3]{1,2,0:T(4,128)(2,1)S(1)} %bitcast.458), channel_id=1, replica_groups=mesh['seq'=16,'mp'=2] {'seq'}, dimensions={0}, use_global_device_ids=true | all-gather | bytes 4896 | tf_op jit(solution)/shard_map/all_gather | solution.py:512
  1929.8 80.6 %reduce-scatter.33.cloned.1.call-done = f32[48,2]{1,0:T(8,128)} async-done(((f32[768,2]{1,0:T(8,128)}), f32[48,2]{1,0:T(8,128)}) %reduce-scatter.33.cloned.1.call-update) | async-done | bytes 400
  2011.3 38.6 %all-gather.2 = bf16[16,48,2]{1,2,0:T(2,128)(2,1)S(1)} all-gather(bf16[1,48,2]{1,2,0:T(2,128)(2,1)S(1)} %bitcast.459), channel_id=1, replica_groups=mesh['seq'=16,'mp'=2] {'seq'}, dimensions={0}, use_global_device_ids=true | all-gather | bytes 3264 | tf_op jit(solution)/shard_map/all_gather | solution.py:509
  2050.5 20.0 all-gather.24.cloned.1.call-done
  2075.2 56.3 %all-gather.20.cloned.1.call-done = bf16[768,3,384]{2,0,1:T(8,128)(2,1)} async-done(((bf16[48,3,384]{2,0,1:T(8,128)(2,1)}), bf16[768,3,384]{2,0,1:T(8,128)(2,1)}) %all-gather.20.cloned.1.call-update) | async-done | bytes 1769488 | tf_op jit(solution)/shard_map/all_gather | solution.py:485
  2135.0 56.8 %all-gather.22.cloned.1.call-done = bf16[768,3,384]{2,0,1:T(8,128)(2,1)} async-done(((bf16[48,3,384]{2,0,1:T(8,128)(2,1)}), bf16[768,3,384]{2,0,1:T(8,128)(2,1)}) %all-gather.22.cloned.1.call-update) | async-done | bytes 1769488 | tf_op jit(solution)/shard_map/all_gather | solution.py:491
  2195.3 66.8 %all-gather.28.cloned.1.call-done = bf16[768,2048]{1,0:T(8,128)(2,1)} async-done(((bf16[48,2048]{1,0:T(8,128)(2,1)}), bf16[768,2048]{1,0:T(8,128)(2,1)}) %all-gather.28.cloned.1.call-update) | async-done | bytes 3145744 | tf_op jit(solution)/shard_map/all_gather | solution.py:506
  2262.1 5.4 convert_element_type.388
  2267.6 90.5 %all-gather.26.cloned.1.call-done = bf16[768,2,2048]{2,0,1:T(8,128)(2,1)} async-done(((bf16[48,2,2048]{2,0,1:T(8,128)(2,1)}), bf16[768,2,2048]{2,0,1:T(8,128)(2,1)}) %all-gather.26.cloned.1.call-update) | async-done | bytes 6291472 | tf_op jit(solution)/shard_map/all_gather | solution.py:503
  2358.1 13.8 copy.297
  (465 shorter events, 301.5 us)
Async XLA Ops:
  7.2 304.1 %copy-start = (bf16[768,2048]{1,0:T(8,128)(2,1)S(1)}, bf16[768,2048]{1,0:T(8,128)(2,1)}, u32[]{:S(2)}) copy-start(bf16[768,2048]{1,0:T(8,128)(2,1)} %param.31) | copy-start | bytes 9437188
  7.2 144.3 %all-gather.14.cloned.1.call-start = ((), (), s32[]{:S(2)}) async-start(), calls=%async_computation.10 | async-start | bytes 2506752 | tf_op jit(solution)/shard_map/all_gather | solution.py:197
  8.1 7.0 copy-start.78
  23.5 7.1 copy-start.85
  28.8 8.8 copy-start.40
  32.2 138.6 %all-gather.30.cloned.1.call-start = ((), (), s32[]{:S(2)}) async-start(), calls=%async_computation.27 | async-start | bytes 2506752 | tf_op jit(solution)/shard_map/all_gather | solution.py:196
  33.9 13.2 copy-start.100
  33.9 250.2 %all-gather.16.cloned.1.call-start = ((), (), s32[]{:S(2)}) async-start(), calls=%async_computation.13 | async-start | bytes 2506752 | tf_op jit(solution)/shard_map/all_gather | solution.py:388
  37.5 10.1 copy-start.38
  38.6 81.4 %collective-permute-start.1 = (bf16[2,128,2,384]{3,1,2,0:T(8,128)(2,1)}, bf16[2,128,2,384]{3,1,2,0:T(8,128)(2,1)}, u32[]{:S(2)}, u32[]{:S(2)}) collective-permute-start(bf16[2,128,2,384]{3,1,2,0:T(8,128)(2,1)} %get-tuple-element.144), channel_id=1, source_target_pairs={{2,0},{4,2},{6,4},{8,6},{10,8},{12,10},{14,12},{16,14},{18,16},{20... | collective-permute-start | bytes 1179656 | tf_op jit(solution)/shard_map/ppermute | solution.py:26
  39.9 80.1 %collective-permute-start = (bf16[2,128,2,384]{3,1,2,0:T(8,128)(2,1)}, bf16[2,128,2,384]{3,1,2,0:T(8,128)(2,1)}, u32[]{:S(2)}, u32[]{:S(2)}) collective-permute-start(bf16[2,128,2,384]{3,1,2,0:T(8,128)(2,1)} %get-tuple-element.143), channel_id=1, source_target_pairs={{0,2},{2,4},{4,6},{6,8},{8,10},{10,12},{12,14},{14,16},{16,18},{18... | collective-permute-start | bytes 1179656 | tf_op jit(solution)/shard_map/ppermute | solution.py:25
  58.0 230.4 %all-reduce.8.cloned.1.call-start = ((), (), s32[]{:S(2)}) async-start(), calls=%async_computation.11 | async-start | bytes 2359296 | tf_op jit(solution)/shard_map/psum | solution.py:219
  63.3 11.5 copy-start.71
  75.0 44.8 %copy-start.101 = (s32[3]{0:T(128)S(1)}, s32[3]{0:T(128)}, u32[]{:S(2)}) copy-start(s32[3]{0:T(128)} %multiply_add_fusion) | copy-start | bytes 40
  80.8 39.0 %copy-start.90 = (s32[2]{0:T(128)}, s32[2]{0:T(128)S(1)}, u32[]{:S(2)}) copy-start(s32[2]{0:T(128)S(1)} %get-tuple-element.119) | copy-start | bytes 28
  80.8 39.0 %copy-start.98 = (s32[2]{0:T(128)}, s32[2]{0:T(128)S(1)}, u32[]{:S(2)}) copy-start(s32[2]{0:T(128)S(1)} %get-tuple-element.118) | copy-start | bytes 28
  155.6 19.4 copy-start.80
  220.5 7.5 copy-start.76
  220.5 149.3 %all-reduce.10.cloned.1.call-start = ((), (), s32[]{:S(2)}) async-start(), calls=%async_computation.12 | async-start | bytes 2359296 | tf_op jit(solution)/shard_map/psum | solution.py:300
  228.0 95.1 %copy-start.36 = (bf16[192,768]{1,0:T(8,128)(2,1)}, bf16[192,768]{1,0:T(8,128)(2,1)S(1)}, u32[]{:S(2)}) copy-start(bf16[192,768]{1,0:T(8,128)(2,1)S(1)} %gather_fusion.6) | copy-start | bytes 884740
  323.1 8.2 slice-start.3
  347.8 196.0 %all-gather.18.cloned.1.call-start = ((), (), s32[]{:S(2)}) async-start(), calls=%async_computation.14 | async-start | bytes 2506752 | tf_op jit(solution)/shard_map/all_gather | solution.py:389
  406.7 217.5 %all-reduce.12.cloned.1.call-start = ((), (), s32[]{:S(2)}) async-start(), calls=%async_computation.31 | async-start | bytes 4718592 | tf_op jit(solution)/shard_map/psum | solution.py:254
  427.3 9.2 copy-start.24
  427.3 9.2 copy-start.57
  429.8 95.8 %collective-permute-start.3 = (bf16[2,128,2,384]{3,1,2,0:T(8,128)(2,1)S(1)}, bf16[2,128,2,384]{3,1,2,0:T(8,128)(2,1)}, u32[]{:S(2)}, u32[]{:S(2)}) collective-permute-start(bf16[2,128,2,384]{3,1,2,0:T(8,128)(2,1)S(1)} %get-tuple-element.140), channel_id=1, source_target_pairs={{2,0},{4,2},{6,4},{8,6},{10,8},{12,10},{14,12},{16,14},{18,16},{20... | collective-permute-start | bytes 1179656 | tf_op jit(solution)/shard_map/ppermute | solution.py:26
  431.1 94.5 %collective-permute-start.2 = (bf16[2,128,2,384]{3,1,2,0:T(8,128)(2,1)S(1)}, bf16[2,128,2,384]{3,1,2,0:T(8,128)(2,1)}, u32[]{:S(2)}, u32[]{:S(2)}) collective-permute-start(bf16[2,128,2,384]{3,1,2,0:T(8,128)(2,1)S(1)} %get-tuple-element.139), channel_id=1, source_target_pairs={{0,2},{2,4},{4,6},{6,8},{8,10},{10,12},{12,14},{14,16},{16,18},{18... | collective-permute-start | bytes 1179656 | tf_op jit(solution)/shard_map/ppermute | solution.py:25
  553.7 8.7 copy-start.51
  554.6 8.5 copy-start.69
  578.0 156.0 %reduce-scatter.25.cloned.1.call-start = ((), (), s32[]{:S(2)}) async-start(), calls=%async_computation.21 | async-start | bytes 3342336 | tf_op jit(solution)/shard_map/reduce_scatter | solution.py:477
  582.6 290.4 %reduce-scatter.17.cloned.1.call-start = ((), (), s32[]{:S(2)}) async-start(), calls=%async_computation.15 | async-start | bytes 3760128 | tf_op jit(solution)/shard_map/reduce_scatter | solution.py:473
  588.1 424.1 %reduce-scatter.21.cloned.1.call-start = ((), (), s32[]{:S(2)}) async-start(), calls=%async_computation.18 | async-start | bytes 3760128 | tf_op jit(solution)/shard_map/reduce_scatter | solution.py:475
  593.1 570.4 %reduce-scatter.29.cloned.1.call-start = ((), (), s32[]{:S(2)}) async-start(), calls=%async_computation.25 | async-start | bytes 6684672 | tf_op jit(solution)/shard_map/reduce_scatter | solution.py:480
  598.3 775.5 %reduce-scatter.27.cloned.1.call-start = ((), (), s32[]{:S(2)}) async-start(), calls=%async_computation.23 | async-start | bytes 13369344 | tf_op jit(solution)/shard_map/reduce_scatter | solution.py:479
  606.4 897.0 %reduce-scatter.31.cloned.1.call-start = ((), (), s32[]{:S(2)}) async-start(), calls=%async_computation.28 | async-start | bytes 1671168 | tf_op jit(solution)/shard_map/reduce_scatter | solution.py:478
  613.1 1018.1 %reduce-scatter.19.cloned.1.call-start = ((), (), s32[]{:S(2)}) async-start(), calls=%async_computation.17 | async-start | bytes 1253376 | tf_op jit(solution)/shard_map/reduce_scatter | solution.py:474
  615.0 1144.2 %reduce-scatter.23.cloned.1.call-start = ((), (), s32[]{:S(2)}) async-start(), calls=%async_computation.20 | async-start | bytes 1253376 | tf_op jit(solution)/shard_map/reduce_scatter | solution.py:476
  616.7 1267.8 %reduce-scatter.35.cloned.1.call-start = ((), (), s32[]{:S(2)}) async-start(), calls=%async_computation.30 | async-start | bytes 417792
  624.1 1386.3 %reduce-scatter.33.cloned.1.call-start = ((), (), s32[]{:S(2)}) async-start(), calls=%async_computation.29 | async-start | bytes 417792
  637.5 18.3 copy-start.79
  637.5 18.3 copy-start.82
  658.9 1411.7 %all-gather.24.cloned.1.call-start = ((), (), s32[]{:S(2)}) async-start(), calls=%async_computation.22 | async-start | bytes 1671168 | tf_op jit(solution)/shard_map/all_gather | solution.py:497
  735.6 1395.9 %all-gather.20.cloned.1.call-start = ((), (), s32[]{:S(2)}) async-start(), calls=%async_computation.16 | async-start | bytes 1880064 | tf_op jit(solution)/shard_map/all_gather | solution.py:485
  874.6 1317.2 %all-gather.22.cloned.1.call-start = ((), (), s32[]{:S(2)}) async-start(), calls=%async_computation.19 | async-start | bytes 1880064 | tf_op jit(solution)/shard_map/all_gather | solution.py:491
  1013.8 1248.3 %all-gather.28.cloned.1.call-start = ((), (), s32[]{:S(2)}) async-start(), calls=%async_computation.26 | async-start | bytes 3342336 | tf_op jit(solution)/shard_map/all_gather | solution.py:506
  1165.3 1192.8 %all-gather.26.cloned.1.call-start = ((), (), s32[]{:S(2)}) async-start(), calls=%async_computation.24 | async-start | bytes 6684672 | tf_op jit(solution)/shard_map/all_gather | solution.py:503
  1675.0 249.8 %copy-start.84 = (f32[2,384]{1,0:T(2,128)S(1)}, f32[2,384]{1,0:T(2,128)}, u32[]{:S(2)}) copy-start(f32[2,384]{1,0:T(2,128)} %get-tuple-element.153) | copy-start | bytes 9220
  2358.1 13.8 copy-start.1
  (93 other events, 301.8 us)
Sparse Core Ops, SparseCore 0:
  32.3 74.5 all-gather.13
  109.6 61.1 all-gather.29
  173.5 61.8 all-gather.15
  238.1 18.6 all-reduce.7
  347.9 21.8 all-reduce.9
  406.8 80.8 all-gather.17
  578.1 17.5 all-reduce.11
  602.0 131.9 reduce-scatter.24
  740.5 132.4 reduce-scatter.16
  879.3 132.8 reduce-scatter.20
  1018.9 144.6 reduce-scatter.28
  1170.6 203.1 reduce-scatter.26
  1379.2 124.1 reduce-scatter.30
  1508.5 122.6 reduce-scatter.18
  1635.8 123.4 reduce-scatter.22
  1763.8 120.6 reduce-scatter.34
  1889.7 120.7 reduce-scatter.32
  2013.5 56.9 all-gather.23
  2073.8 57.6 all-gather.19
  2134.1 57.7 all-gather.21
  2195.2 66.8 all-gather.27
  2265.4 92.6 all-gather.25
where the time goes:
time: 2390 us; the launch traced here: 2380 us
  waiting for transfers between devices  1470 us (62%)
  blocking collectives  365 us (15%)
  other arithmetic  213 us (9%)
  local copies, waits for them, and re-layouts  169 us (7%)
  matrix products  129 us (5%)
    reduce_scatter x1, waiting for transfers between devices, shards(): lax.psum_scatter(heavy_mlp_in_grad, 'seq', scatter_dimension=0, tiled=True)  208 us
    unnamed x24, waiting for transfers between devices  162 us
    reduce_scatter x1, waiting for transfers between devices, shards(): lax.psum_scatter(heavy_mlp_out_grad, 'seq', scatter_dimension=0, tiled=True)  150 us
    reduce_scatter x1, waiting for transfers between devices, shards(): lax.psum_scatter(heavy_qkv_grad, 'seq', scatter_dimension=0, tiled=True)  138 us
    reduce_scatter x1, waiting for transfers between devices, shards(): lax.psum_scatter(light_qkv_grad, 'seq', scatter_dimension=0, tiled=True)  137 us
    reduce_scatter x1, waiting for transfers between devices, shards(): lax.psum_scatter(light_mlp_out_grad, 'seq', scatter_dimension=0, tiled=True)  128 us
    scatter-add x8, other arithmetic, add_rows(): return target.at[seq_ids, where_rows].add(values)  121 us
    all_gather x1, waiting for transfers between devices, shards(): lax.all_gather(sum_heavy_in.astype(jnp.bfloat16), 'seq', axis=0, tiled=True)  90.5 us
  transfers between devices with their start and end apart: 26, of which 17 were waited for; matrix products, arithmetic and copies ran while one was open for 14% of the time, Pallas kernels for 0%

commit v1 on v0

--- a/solution.py
+++ b/solution.py
@@ -3,6 +3,8 @@
 import jax
 import jax.numpy as jnp
 from jax import lax
+from jax.experimental import pallas as pl
+from jax.experimental.pallas import tpu as pltpu
 from jax.sharding import PartitionSpec as P
 
 LHD = 96
@@ -43,14 +45,164 @@
     return jax.nn.gelu(gate_in, approximate=True) * up_in
 
 
-def pick_rows(source, where_rows):
-    seq_ids = jnp.arange(source.shape[0], dtype=jnp.int32)[:, None]
-    return source[seq_ids, where_rows]
-
-
-def add_rows(target, where_rows, values):
-    seq_ids = jnp.arange(target.shape[0], dtype=jnp.int32)[:, None]
-    return target.at[seq_ids, where_rows].add(values)
+def one_hot_rows(where_rows, length):
+    places = jnp.arange(length, dtype=jnp.int32)
+    return (where_rows[:, :, None] == places[None, None, :]).astype(jnp.bfloat16)
+
+
+def pick_rows(source, hot):
+    return jnp.einsum("sct,std->scd", hot, source, preferred_element_type=jnp.float32).astype(
+        source.dtype
+    )
+
+
+def pick_values(source, hot):
+    return jnp.sum(hot.astype(jnp.float32) * source[:, None, :], axis=-1)
+
+
+def place_values(values, hot):
+    return jnp.sum(hot.astype(jnp.float32) * values[:, :, None], axis=1)
+
+
+def add_rows(target, hot, values):
+    high = values.astype(jnp.bfloat16)
+    rest = (values - high.astype(jnp.float32)).astype(jnp.bfloat16)
+    return target + jnp.einsum(
+        "sct,scd->std",
+        jnp.concatenate([hot, hot], axis=1),
+        jnp.concatenate([high, rest], axis=1),
+        preferred_element_type=jnp.float32,
+    )
+
+
+def other_core(value):
+    return lax.ppermute(value, "mp", [(0, 1), (1, 0)])
+
+
+def core_sum(value):
+    low_value = value.astype(jnp.bfloat16)
+    return low_value.astype(jnp.float32) + other_core(low_value).astype(jnp.float32)
+
+
+def lanes_of(shape):
+    return lax.broadcasted_iota(jnp.int32, shape, len(shape) - 1)
+
+
+def rows_dot(a, b):
+    return lax.dot_general(a, b, (((1,), (1,)), ((), ())), preferred_element_type=jnp.float32)
+
+
+def cols_dot(a, b):
+    return lax.dot_general(a, b, (((0,), (0,)), ((), ())), preferred_element_type=jnp.float32)
+
+
+def key_operand(pair, extra):
+    lane = lanes_of(pair.shape)
+    moved = pltpu.roll(pair.astype(jnp.float32), HHD, 1)
+    bias = extra[:, HHD : HHD + 1].astype(jnp.float32)
+    return jnp.where(lane < HHD, moved, jnp.where(lane == HHD, bias, 0.0)).astype(jnp.bfloat16)
+
+
+def query_operand(pair, scale):
+    lane = lanes_of(pair.shape)
+    scaled = pair.astype(jnp.float32) * scale
+    return jnp.where(lane < HHD, scaled, jnp.where(lane == HHD, 1.0, 0.0)).astype(jnp.bfloat16)
+
+
+def heavy_forward_kernel(tile, scale, pair_ref, extra_ref, kept_ref, key_ref):
+    @pl.when(pl.program_id(1) == 0)
+    def _():
+        key_ref[...] = key_operand(pair_ref[0], extra_ref[0])
+
+    start = pl.multiple_of(pl.program_id(1) * tile, tile)
+    query = query_operand(pair_ref[0, pl.ds(start, tile), :], scale)
+    scores = rows_dot(query, key_ref[...])
+    top = jnp.max(scores, axis=-1, keepdims=True)
+    expo = jnp.exp(scores - top)
+    total = jnp.sum(expo, axis=-1, keepdims=True)
+    mix = jnp.dot(
+        expo.astype(jnp.bfloat16), extra_ref[0], preferred_element_type=jnp.float32
+    ) / total
+    lane = lanes_of(mix.shape)
+    kept_ref[0] = jnp.where(lane < HHD, mix, top + jnp.log(total))
+
+
+def heavy_backward_kernel(
+    tile, scale, pair_ref, extra_ref, kept_ref, grad_ref, both_ref, value_ref, key_ref, dk_ref, dv_ref
+):
+    step = pl.program_id(1)
+
+    @pl.when(step == 0)
+    def _():
+        key_ref[...] = key_operand(pair_ref[0], extra_ref[0])
+        dk_ref[...] = jnp.zeros_like(dk_ref)
+        dv_ref[...] = jnp.zeros_like(dv_ref)
+
+    start = pl.multiple_of(step * tile, tile)
+    query = query_operand(pair_ref[0, pl.ds(start, tile), :], scale)
+    lane = lanes_of(query.shape)
+    kept = kept_ref[0]
+    grad = grad_ref[0]
+    lse = kept[:, HHD : HHD + 1]
+    delta = jnp.sum(
+        kept[:, :HHD] * grad[:, :HHD].astype(jnp.float32), axis=-1, keepdims=True
+    )
+    probs = jnp.exp(rows_dot(query, key_ref[...]) - lse)
+    prob_grad = rows_dot(grad, extra_ref[0])
+    score_grad = (probs * (prob_grad - delta)).astype(jnp.bfloat16)
+    query_grad = jnp.dot(score_grad, key_ref[...], preferred_element_type=jnp.float32) * scale
+    both_ref[0, pl.ds(start, tile), :] = jnp.where(lane < HHD, query_grad, 0.0).astype(jnp.bfloat16)
+    dk_ref[...] += cols_dot(score_grad, query)
+    dv_ref[...] += cols_dot(probs.astype(jnp.bfloat16), grad)
+
+    @pl.when(step == pl.num_programs(1) - 1)
+    def _():
+        spot = lanes_of(dk_ref.shape)
+        moved = pltpu.roll(dk_ref[...], HHD, 1)
+        query_part = both_ref[0].astype(jnp.float32)
+        both_ref[0] = jnp.where(spot < HHD, query_part, moved).astype(jnp.bfloat16)
+        value_ref[0] = dv_ref[...].astype(jnp.bfloat16)
+
+
+def query_tile(length):
+    return 256 if length % 256 == 0 else 96
+
+
+def heavy_forward(pair, extra, scale):
+    pairs, length, lanes = pair.shape
+    tile = query_tile(length)
+    whole = pl.BlockSpec((1, length, lanes), lambda p, i: (p, 0, 0))
+    return pl.pallas_call(
+        lambda *refs: heavy_forward_kernel(tile, scale, *refs),
+        grid=(pairs, length // tile),
+        in_specs=[whole, whole],
+        out_specs=pl.BlockSpec((1, tile, lanes), lambda p, i: (p, i, 0)),
+        out_shape=jax.ShapeDtypeStruct(pair.shape, jnp.float32),
+        scratch_shapes=[pltpu.VMEM((length, lanes), jnp.bfloat16)],
+        compiler_params=pltpu.CompilerParams(vmem_limit_bytes=60 * 2**20),
+        name="heavy_forward",
+    )(pair, extra)
+
+
+def heavy_backward(pair, extra, kept, grad, scale):
+    pairs, length, lanes = pair.shape
+    tile = query_tile(length)
+    whole = pl.BlockSpec((1, length, lanes), lambda p, i: (p, 0, 0))
+    rows = pl.BlockSpec((1, tile, lanes), lambda p, i: (p, i, 0))
+    return pl.pallas_call(
+        lambda *refs: heavy_backward_kernel(tile, scale, *refs),
+        grid=(pairs, length // tile),
+        in_specs=[whole, whole, rows, rows],
+        out_specs=[whole, whole],
+        out_shape=[jax.ShapeDtypeStruct(pair.shape, jnp.bfloat16)] * 2,
+        scratch_shapes=[
+            pltpu.VMEM((length, lanes), jnp.bfloat16),
+            pltpu.VMEM((length, lanes), jnp.float32),
+            pltpu.VMEM((length, lanes), jnp.float32),
+        ],
+        compiler_params=pltpu.CompilerParams(vmem_limit_bytes=60 * 2**20),
+        name="heavy_backward",
+    )(pair, extra, kept, grad)
 
 
 def windows(extended, blocks, tile_width):
@@ -81,14 +233,6 @@
     key_place = row_base + tile_ids[:, None] * tile_width + col_ids[None, :] - tile_width
     inside = (key_place >= 0) & (key_place < length)
     return within[None, :, :] & inside[:, None, :]
-
-
-def heavy_scores(queries, key_heads, key_flags, scale_value):
-    plain = (
-        jnp.einsum("sqhd,skhd->shqk", queries, key_heads, preferred_element_type=jnp.float32)
-        * scale_value
-    )
-    return jnp.where(key_flags[:, None, None, :] > 0, plain, MASKED)
 
 
 def shards(
@@ -172,51 +316,58 @@
     query_rows = routed_queries - row_base
     key_rows = routed_keys - row_base
     mlp_rows = routed_mlp - row_base
-    query_in = pick_rows(normalized_lower_precision, query_rows)
-    query_norm = pick_rows(normed, query_rows)
-    query_gate = jax.nn.sigmoid(
-        jnp.einsum("scd,d->sc", query_norm, routers[:, 0], precision=TOP_PRECISION)
-    )
+    query_hot = one_hot_rows(query_rows, local_len)
+    key_hot = one_hot_rows(key_rows, local_len)
+    mlp_hot = one_hot_rows(mlp_rows, local_len)
+    logits_one = jnp.einsum("std,dk->kst", normed, routers[:, :2], precision=TOP_PRECISION)
+    query_in = pick_rows(normalized_lower_precision, query_hot)
+    query_gate = jax.nn.sigmoid(pick_values(logits_one[0], query_hot))
     heavy_query = jnp.einsum(
         "scd,dk->sck", query_in, heavy_qkv[:, 0], preferred_element_type=jnp.float32
     ).astype(jnp.bfloat16)
-    key_in = pick_rows(normalized_lower_precision, key_rows)
-    key_norm = pick_rows(normed, key_rows)
-    key_gate = jax.nn.sigmoid(
-        jnp.einsum("scd,d->sc", key_norm, routers[:, 1], precision=TOP_PRECISION)
-    )
+    key_in = pick_rows(normalized_lower_precision, key_hot)
+    key_gate = jax.nn.sigmoid(pick_values(logits_one[1], key_hot))
     key_both = jnp.einsum(
         "scd,djk->scjk", key_in, heavy_qkv[:, 1:], preferred_element_type=jnp.float32
     )
     heavy_key = key_both[:, :, 0].astype(jnp.bfloat16)
     raw_value = key_both[:, :, 1]
     heavy_value = (key_gate[..., None] * raw_value).astype(jnp.bfloat16)
-    key_flag = valid_key.astype(jnp.bfloat16)
-    all_keys, all_values, all_flags = (
-        lax.all_gather(heavy_key, "seq", axis=1, tiled=True),
-        lax.all_gather(heavy_value, "seq", axis=1, tiled=True),
-        lax.all_gather(key_flag, "seq", axis=1, tiled=True),
-    )
-    key_heads = all_keys.reshape(seq_count, -1, heavy_heads, HHD)
-    value_heads = all_values.reshape(seq_count, -1, heavy_heads, HHD)
-    query_heads = heavy_query.reshape(seq_count, capacity, heavy_heads, HHD)
-    scores_heavy = heavy_scores(query_heads, key_heads, all_flags, heavy_scale)
-    top_heavy = jnp.max(scores_heavy, axis=-1, keepdims=True)
-    expo_heavy = jnp.exp(scores_heavy - top_heavy)
-    sum_heavy = jnp.sum(expo_heavy, axis=-1, keepdims=True)
-    heavy_probs = expo_heavy / sum_heavy
-    heavy_lse = (top_heavy + jnp.log(sum_heavy))[..., 0]
-    heavy_mix = jnp.einsum(
-        "shqk,skhd->sqhd",
-        heavy_probs.astype(jnp.bfloat16),
-        value_heads,
-        preferred_element_type=jnp.float32,
-    )
-    heavy_mix = heavy_mix.reshape(seq_count, capacity, heavy_cols).astype(jnp.bfloat16)
+    key_bias = jnp.where(valid_key, 0.0, MASKED).astype(jnp.bfloat16)
+
+    def to_pairs(parts):
+        split = jnp.concatenate(
+            [p.reshape(seq_count, capacity, heavy_heads, HHD) for p in parts], axis=-1
+        )
+        pairs = split.transpose(0, 2, 1, 3).reshape(
+            seq_count * heavy_heads, capacity, HHD * len(parts)
+        )
+        return pairs
+
+    def across(pairs):
+        spare = pairs_here * seq_devices - pairs.shape[0]
+        sent = jnp.pad(pairs, ((0, spare), (0, 0), (0, 0)))
+        return lax.all_to_all(sent, "seq", split_axis=0, concat_axis=1, tiled=True)
+
+    def back(per_pair):
+        got = lax.all_to_all(per_pair, "seq", split_axis=1, concat_axis=0, tiled=True)
+        return got[: seq_count * heavy_heads].reshape(seq_count, heavy_heads, capacity, -1)
+
+    pairs_here = -(-(seq_count * heavy_heads) // seq_devices)
+    bias_column = jnp.broadcast_to(
+        key_bias[:, None, :, None], (seq_count, heavy_heads, capacity, HHD)
+    ).reshape(seq_count * heavy_heads, capacity, HHD)
+    pair_in = across(
+        jnp.concatenate([to_pairs([heavy_query, heavy_key, heavy_value]), bias_column], axis=-1)
+    )
+    pair_both, pair_extra = pair_in[:, :, : 2 * HHD], pair_in[:, :, 2 * HHD :]
+    pair_kept = heavy_forward(pair_both, pair_extra, heavy_scale)
+    heavy_mix = back(pair_kept[:, :, :HHD].astype(jnp.bfloat16))
+    heavy_mix = heavy_mix.transpose(0, 2, 1, 3).reshape(seq_count, capacity, heavy_cols)
     heavy_rows = jnp.einsum("sck,dk->scd", heavy_mix, heavy_out, preferred_element_type=jnp.float32)
     query_weight = jnp.where(valid_query, query_gate, 0.0)
-    attn_part = add_rows(attn_part, query_rows, query_weight[..., None] * heavy_rows)
-    attention_layer = lax.psum(attn_part.astype(jnp.bfloat16), "mp").astype(jnp.float32)
+    attn_part = add_rows(attn_part, query_hot, query_weight[..., None] * heavy_rows)
+    attention_layer = core_sum(attn_part)
     middle = inputs + attention_layer
     normed_two, factor_two = norm_rows(middle, gains[:, 1])
     lower_precision_second = normed_two.astype(jnp.bfloat16)
@@ -235,11 +386,9 @@
         light_feedforward_output_weight,
         preferred_element_type=jnp.float32,
     )
-    mlp_in = pick_rows(lower_precision_second, mlp_rows)
-    mlp_norm = pick_rows(normed_two, mlp_rows)
-    mlp_gate = jax.nn.sigmoid(
-        jnp.einsum("scd,d->sc", mlp_norm, routers[:, 2], precision=TOP_PRECISION)
-    )
+    mlp_in = pick_rows(lower_precision_second, mlp_hot)
+    logits_two = jnp.einsum("std,d->st", normed_two, routers[:, 2], precision=TOP_PRECISION)
+    mlp_gate = jax.nn.sigmoid(pick_values(logits_two, mlp_hot))
     heavy_gates = jnp.einsum(
         "scd,dkf->sckf", mlp_in, heavy_mlp_in, preferred_element_type=jnp.float32
     )
@@ -249,9 +398,9 @@
     )
     mlp_weight = jnp.where(valid_mlp, mlp_gate, 0.0)
     feedforward_portion = add_rows(
-        feedforward_portion, mlp_rows, mlp_weight[..., None] * heavy_mlp_rows
-    )
-    mlp_total = lax.psum(feedforward_portion.astype(jnp.bfloat16), "mp").astype(jnp.float32)
+        feedforward_portion, mlp_hot, mlp_weight[..., None] * heavy_mlp_rows
+    )
+    mlp_total = core_sum(feedforward_portion)
     result = (middle + mlp_total).astype(jnp.bfloat16)
     upstream = out_grad.astype(jnp.float32)
     hidden_grad = jnp.einsum(
@@ -274,35 +423,56 @@
         light_feedforward_input_weight,
         preferred_element_type=jnp.float32,
     )
-    mlp_upstream = pick_rows(out_grad, mlp_rows).astype(jnp.float32)
+    mlp_upstream = pick_rows(out_grad, mlp_hot).astype(jnp.float32)
     slot_mlp_grad = (mlp_weight[..., None] * mlp_upstream).astype(jnp.bfloat16)
     mlp_gate_grad = jnp.sum(mlp_upstream * heavy_mlp_rows, axis=-1)
-    heavy_mlp_out_grad = jnp.einsum(
-        "scd,scf->df", slot_mlp_grad, heavy_hidden, preferred_element_type=jnp.float32
-    )
     heavy_hidden_grad = jnp.einsum(
         "scd,df->scf", slot_mlp_grad, heavy_mlp_out, preferred_element_type=jnp.float32
     )
     unused_heavy, pull_heavy = jax.vjp(gated_gelu, heavy_gates[:, :, 0], heavy_gates[:, :, 1])
     heavy_gate_grad, heavy_up_grad = pull_heavy(heavy_hidden_grad)
     heavy_gates_grad = jnp.stack([heavy_gate_grad, heavy_up_grad], axis=2).astype(jnp.bfloat16)
+    all_slots = seq_count * capacity * seq_devices
+    gather_heavy = 2 * all_slots * model_width < 4 * (heavy_mlp_in.size + heavy_mlp_out.size)
+    if gather_heavy:
+        first_core = lax.axis_index("mp") == 0
+        here = lax.all_gather(
+            jnp.where(first_core, mlp_in, slot_mlp_grad), "seq", axis=1, tiled=True
+        )
+        there = other_core(here)
+        slot_in = jnp.where(first_core, here, there)
+        slot_grad_all = jnp.where(first_core, there, here)
+        gates_all = jnp.einsum(
+            "scd,dkf->sckf", slot_in, heavy_mlp_in, preferred_element_type=jnp.float32
+        )
+        hidden_grad_all = jnp.einsum(
+            "scd,df->scf", slot_grad_all, heavy_mlp_out, preferred_element_type=jnp.float32
+        )
+        hidden_all, pull_all = jax.vjp(gated_gelu, gates_all[:, :, 0], gates_all[:, :, 1])
+        gate_grad_all, up_grad_all = pull_all(hidden_grad_all)
+        hidden_all = hidden_all.astype(jnp.bfloat16)
+        gates_grad_all = jnp.stack([gate_grad_all, up_grad_all], axis=2).astype(jnp.bfloat16)
+    else:
+        slot_in, slot_grad_all, hidden_all = mlp_in, slot_mlp_grad, heavy_hidden
+        gates_grad_all = heavy_gates_grad
+    heavy_mlp_out_grad = jnp.einsum(
+        "scd,scf->df", slot_grad_all, hidden_all, preferred_element_type=jnp.float32
+    )
     heavy_mlp_in_grad = jnp.einsum(
-        "scd,sckf->dkf", mlp_in, heavy_gates_grad, preferred_element_type=jnp.float32
+        "scd,sckf->dkf", slot_in, gates_grad_all, preferred_element_type=jnp.float32
     )
     low_two_grad = add_rows(
         low_two_grad,
-        mlp_rows,
+        mlp_hot,
         jnp.einsum(
             "sckf,dkf->scd", heavy_gates_grad, heavy_mlp_in, preferred_element_type=jnp.float32
         ),
     )
-    normed_two_grad, mlp_gate_sum = (
-        lax.psum(low_two_grad.astype(jnp.bfloat16), "mp").astype(jnp.float32),
-        lax.psum(mlp_gate_grad.astype(jnp.bfloat16), "mp").astype(jnp.float32),
-    )
+    normed_two_grad, mlp_gate_sum = core_sum(low_two_grad), core_sum(mlp_gate_grad)
     mlp_logit_grad = jnp.where(valid_mlp, mlp_gate_sum * mlp_gate * (1.0 - mlp_gate), 0.0)
-    normed_two_grad = add_rows(normed_two_grad, mlp_rows, mlp_logit_grad[..., None] * routers[:, 2])
-    router_mlp_grad = jnp.einsum("sc,scd->d", mlp_logit_grad, mlp_norm, precision=TOP_PRECISION)
+    mlp_token_grad = place_values(mlp_logit_grad, mlp_hot)
+    normed_two_grad = normed_two_grad + mlp_token_grad[..., None] * routers[:, 2]
+    router_mlp_grad = jnp.einsum("st,std->d", mlp_token_grad, normed_two, precision=TOP_PRECISION)
     gain_mlp_grad = jnp.sum(normed_two_grad * middle * factor_two, axis=(0, 1))
     middle_grad = upstream + norm_back(middle, factor_two, gains[:, 1], normed_two_grad)
     attn_low = middle_grad.astype(jnp.bfloat16)
@@ -363,7 +533,7 @@
         light_query_key_value_weight,
         preferred_element_type=jnp.float32,
     )
-    attn_upstream = pick_rows(attn_low, query_rows).astype(jnp.float32)
+    attn_upstream = pick_rows(attn_low, query_hot).astype(jnp.float32)
     slot_attn_grad = (query_weight[..., None] * attn_upstream).astype(jnp.bfloat16)
     query_gate_grad = jnp.sum(attn_upstream * heavy_rows, axis=-1)
     heavy_out_grad = jnp.einsum(
@@ -372,49 +542,16 @@
     heavy_mix_grad = jnp.einsum(
         "scd,dk->sck", slot_attn_grad, heavy_out, preferred_element_type=jnp.float32
     ).astype(jnp.bfloat16)
-    grad_heads = heavy_mix_grad.reshape(seq_count, capacity, heavy_heads, HHD)
-    probs_again = jnp.exp(scores_heavy - heavy_lse[..., None])
-    prob_grad = jnp.einsum(
-        "sqhd,skhd->shqk", grad_heads, value_heads, preferred_element_type=jnp.float32
-    )
-    heavy_delta = jnp.sum(probs_again * prob_grad, axis=-1)
-    score_grad = (probs_again * (prob_grad - heavy_delta[..., None])).astype(jnp.bfloat16)
-    query_grad = (
-        jnp.einsum("shqk,skhd->sqhd", score_grad, key_heads, preferred_element_type=jnp.float32)
-        * heavy_scale
-    )
-    query_grad = query_grad.reshape(seq_count, capacity, heavy_cols).astype(jnp.bfloat16)
-    every_query, every_grad = (
-        lax.all_gather(heavy_query, "seq", axis=1, tiled=True),
-        lax.all_gather(heavy_mix_grad, "seq", axis=1, tiled=True),
-    )
-    every_lse, every_delta = (
-        lax.all_gather(heavy_lse, "seq", axis=2, tiled=True),
-        lax.all_gather(heavy_delta, "seq", axis=2, tiled=True),
-    )
-    query_all = every_query.reshape(seq_count, -1, heavy_heads, HHD)
-    grad_all = every_grad.reshape(seq_count, -1, heavy_heads, HHD)
-    own_keys = heavy_key.reshape(seq_count, capacity, heavy_heads, HHD)
-    own_values = heavy_value.reshape(seq_count, capacity, heavy_heads, HHD)
-    own_probs = jnp.exp(
-        heavy_scores(query_all, own_keys, key_flag, heavy_scale) - every_lse[..., None]
-    )
-    own_prob_grad = jnp.einsum(
-        "sqhd,skhd->shqk", grad_all, own_values, preferred_element_type=jnp.float32
-    )
-    own_score_grad = (own_probs * (own_prob_grad - every_delta[..., None])).astype(jnp.bfloat16)
-    key_grad = (
-        jnp.einsum("shqk,sqhd->skhd", own_score_grad, query_all, preferred_element_type=jnp.float32)
-        * heavy_scale
-    )
-    key_grad = key_grad.reshape(seq_count, capacity, heavy_cols)
-    value_grad = jnp.einsum(
-        "shqk,sqhd->skhd",
-        own_probs.astype(jnp.bfloat16),
-        grad_all,
-        preferred_element_type=jnp.float32,
-    )
-    value_grad = value_grad.reshape(seq_count, capacity, heavy_cols)
+    pair_grad_in = across(to_pairs([heavy_mix_grad]))
+    pair_grad_in = jnp.pad(pair_grad_in, ((0, 0), (0, 0), (0, HHD)))
+    pair_both_grad, pair_value_grad = heavy_backward(
+        pair_both, pair_extra, pair_kept, pair_grad_in, heavy_scale
+    )
+    triple = back(
+        jnp.concatenate([pair_both_grad, pair_value_grad[:, :, :HHD]], axis=-1)
+    ).reshape(seq_count, heavy_heads, capacity, 3, HHD)
+    triple = triple.transpose(3, 0, 2, 1, 4).reshape(3, seq_count, capacity, heavy_cols)
+    query_grad, key_grad, value_grad = triple[0], triple[1], triple[2]
     key_grad_low = key_grad.astype(jnp.bfloat16)
     value_grad_low = value_grad.astype(jnp.bfloat16).astype(jnp.float32)
     raw_grad = (key_gate[..., None] * value_grad_low).astype(jnp.bfloat16)
@@ -431,34 +568,63 @@
     )
     input_low_grad = add_rows(
         input_low_grad,
-        query_rows,
+        query_hot,
         jnp.einsum("sck,dk->scd", query_grad, heavy_qkv[:, 0], preferred_element_type=jnp.float32),
     )
     input_low_grad = add_rows(
         input_low_grad,
-        key_rows,
+        key_hot,
         jnp.einsum(
             "scjk,djk->scd", key_pair_grad, heavy_qkv[:, 1:], preferred_element_type=jnp.float32
         ),
     )
     normed_grad, query_gate_sum, key_gate_sum = (
-        lax.psum(input_low_grad.astype(jnp.bfloat16), "mp").astype(jnp.float32),
-        lax.psum(query_gate_grad.astype(jnp.bfloat16), "mp").astype(jnp.float32),
-        lax.psum(key_gate_grad.astype(jnp.bfloat16), "mp").astype(jnp.float32),
+        core_sum(input_low_grad),
+        core_sum(query_gate_grad),
+        core_sum(key_gate_grad),
     )
     query_logit_grad = jnp.where(valid_query, query_gate_sum * query_gate * (1.0 - query_gate), 0.0)
     key_logit_grad = jnp.where(valid_key, key_gate_sum * key_gate * (1.0 - key_gate), 0.0)
-    normed_grad = add_rows(normed_grad, query_rows, query_logit_grad[..., None] * routers[:, 0])
-    normed_grad = add_rows(normed_grad, key_rows, key_logit_grad[..., None] * routers[:, 1])
-    router_query_grad = jnp.einsum(
-        "sc,scd->d", query_logit_grad, query_norm, precision=TOP_PRECISION
-    )
-    router_key_grad = jnp.einsum("sc,scd->d", key_logit_grad, key_norm, precision=TOP_PRECISION)
+    token_logit_grad = jnp.stack(
+        [place_values(query_logit_grad, query_hot), place_values(key_logit_grad, key_hot)], axis=0
+    )
+    normed_grad = (
+        normed_grad
+        + token_logit_grad[0][..., None] * routers[:, 0]
+        + token_logit_grad[1][..., None] * routers[:, 1]
+    )
+    router_attn_grad = jnp.einsum(
+        "kst,std->dk", token_logit_grad, normed, precision=TOP_PRECISION
+    )
     gain_attn_grad = jnp.sum(normed_grad * inputs * factor_one, axis=(0, 1))
     input_grad = middle_grad + norm_back(inputs, factor_one, gains[:, 0], normed_grad)
-    gains_grad = jnp.stack([gain_attn_grad, gain_mlp_grad], axis=1)
-    routers_grad = jnp.stack([router_query_grad, router_key_grad, router_mlp_grad], axis=1)
-    (
+    small_grads = jnp.concatenate(
+        [gain_attn_grad[:, None], gain_mlp_grad[:, None], router_attn_grad, router_mlp_grad[:, None]],
+        axis=1,
+    )
+
+    def summed(parts):
+        widths = [math.prod(p.shape[1:]) for p in parts]
+        joined = jnp.concatenate(
+            [p.reshape(model_width, -1).astype(jnp.bfloat16) for p in parts], axis=1
+        )
+        total = lax.psum(joined, "seq").astype(jnp.float32)
+        marks = [sum(widths[:i]) for i in range(len(widths) + 1)]
+        return [
+            total[:, marks[i] : marks[i + 1]].reshape(p.shape) for i, p in enumerate(parts)
+        ]
+
+    sum_light_in, sum_light_down = summed([light_mlp_in_grad, light_mlp_out_grad])
+    sum_light_qkv, sum_heavy_qkv, sum_light_out, sum_heavy_out, sum_small = summed(
+        [light_qkv_grad, heavy_qkv_grad, light_out_grad, heavy_out_grad, small_grads]
+    )
+    if gather_heavy:
+        sum_heavy_in, sum_heavy_down = heavy_mlp_in_grad, heavy_mlp_out_grad
+    else:
+        sum_heavy_in, sum_heavy_down = summed([heavy_mlp_in_grad, heavy_mlp_out_grad])
+    return (
+        result,
+        input_grad,
         sum_light_qkv,
         sum_light_out,
         sum_heavy_qkv,
@@ -467,65 +633,8 @@
         sum_light_down,
         sum_heavy_in,
         sum_heavy_down,
-        sum_gains,
-        sum_routers,
-    ) = (
-        lax.psum_scatter(light_qkv_grad, "seq", scatter_dimension=0, tiled=True),
-        lax.psum_scatter(light_out_grad, "seq", scatter_dimension=0, tiled=True),
-        lax.psum_scatter(heavy_qkv_grad, "seq", scatter_dimension=0, tiled=True),
-        lax.psum_scatter(heavy_out_grad, "seq", scatter_dimension=0, tiled=True),
-        lax.psum_scatter(light_mlp_in_grad, "seq", scatter_dimension=0, tiled=True),
-        lax.psum_scatter(light_mlp_out_grad, "seq", scatter_dimension=0, tiled=True),
-        lax.psum_scatter(heavy_mlp_in_grad, "seq", scatter_dimension=0, tiled=True),
-        lax.psum_scatter(heavy_mlp_out_grad, "seq", scatter_dimension=0, tiled=True),
-        lax.psum_scatter(gains_grad, "seq", scatter_dimension=0, tiled=True),
-        lax.psum_scatter(routers_grad, "seq", scatter_dimension=0, tiled=True),
-    )
-    shared = (
-        lax.all_gather(sum_light_qkv.astype(jnp.bfloat16), "seq", axis=0, tiled=True).astype(
-            sum_light_qkv.dtype
-        ),
-        lax.all_gather(sum_light_out.astype(jnp.bfloat16), "seq", axis=0, tiled=True).astype(
-            sum_light_out.dtype
-        ),
-        lax.all_gather(sum_heavy_qkv.astype(jnp.bfloat16), "seq", axis=0, tiled=True).astype(
-            sum_heavy_qkv.dtype
-        ),
-        lax.all_gather(sum_heavy_out.astype(jnp.bfloat16), "seq", axis=0, tiled=True).astype(
-            sum_heavy_out.dtype
-        ),
-        lax.all_gather(sum_light_in.astype(jnp.bfloat16), "seq", axis=0, tiled=True).astype(
-            sum_light_in.dtype
-        ),
-        lax.all_gather(sum_light_down.astype(jnp.bfloat16), "seq", axis=0, tiled=True).astype(
-            sum_light_down.dtype
-        ),
-        lax.all_gather(sum_heavy_in.astype(jnp.bfloat16), "seq", axis=0, tiled=True).astype(
-            sum_heavy_in.dtype
-        ),
-        lax.all_gather(sum_heavy_down.astype(jnp.bfloat16), "seq", axis=0, tiled=True).astype(
-            sum_heavy_down.dtype
-        ),
-        lax.all_gather(sum_gains.astype(jnp.bfloat16), "seq", axis=0, tiled=True).astype(
-            sum_gains.dtype
-        ),
-        lax.all_gather(sum_routers.astype(jnp.bfloat16), "seq", axis=0, tiled=True).astype(
-            sum_routers.dtype
-        ),
-    )
-    return (
-        result,
-        input_grad,
-        shared[0],
-        shared[1],
-        shared[2],
-        shared[3],
-        shared[4],
-        shared[5],
-        shared[6],
-        shared[7],
-        shared[8],
-        shared[9],
+        sum_small[:, :2],
+        sum_small[:, 2:],
     )
 
 

time: 2390 us -> 801 us (0.34)
  waiting for transfers between devices: 1470 us -> 227 us
  blocking collectives: 365 us -> 0 us
  other arithmetic: 213 us -> 69.8 us
  matrix products: 129 us -> 216 us
  local copies, waits for them, and re-layouts: 169 us -> 201 us
  starting transfers between devices: 17.2 us -> 44.6 us
    reduce_scatter x8 -> x0, waiting for transfers between devices: 1000 us -> none  [the longest x1 208 us: shards(): lax.psum_scatter(heavy_mlp_in_grad, 'seq', scatter_dimension=0, tiled=True)]
    all_gather x8 -> x0, blocking collectives: 360 us -> none  [the longest x1 65.8 us: shards(): lax.all_gather(heavy_delta, 'seq', axis=2, tiled=True)]
    all_gather x9 -> x1, waiting for transfers between devices: 306 us -> 0.02 us  [shards(): lax.all_gather(jnp.where(first_core, mlp_in, slot_mlp_grad), 'seq', axis=...]
    psum x3 -> x1, waiting for transfers between devices: 1.78 us -> 224 us  [summed(): total = lax.psum(joined, 'seq').astype(jnp.float32)]
    unnamed x24 -> x2, waiting for transfers between devices: 162 us -> 0.03 us
    scatter-add x8 -> x0, other arithmetic: 121 us -> none  [add_rows(): return target.at[seq_ids, where_rows].add(values)]
    dot_general x15 -> x18, matrix products: 48 us -> 136 us  [the longest x1 36.7 us: shards(): jnp.einsum('scd,df->scf', slot_grad_all, heavy_mlp_out, preferred_element...]
    gather x8 -> x0, local copies, waits for them, and re-layouts: 49.6 us -> none  [pick_rows(): return source[seq_ids, where_rows]]
  transfers between devices with their start and end apart: 26 -> 18, of which waited for: 17 -> 2; matrix products, arithmetic and copies ran while one was open for 14% -> 35% of each run, Pallas kernels for 0% -> 1%
where the time goes in v1:
time: 801 us; the launch traced here: 791 us
  waiting for transfers between devices  227 us (28%)
  matrix products  216 us (27%)
  local copies, waits for them, and re-layouts  201 us (25%)
  other arithmetic  69.8 us (9%)
  starting transfers between devices  44.6 us (6%)
  Pallas kernels  17.8 us (2%)
  between operations  15.5 us (2%)
    psum x1, waiting for transfers between devices, summed(): total = lax.psum(joined, 'seq').astype(jnp.float32)  224 us
    unnamed x194, local copies, waits for them, and re-layouts  54.8 us
    dot_general x1, matrix products, shards(): jnp.einsum('scd,df->scf', slot_grad_all, heavy_mlp_out, preferred_element...  36.7 us
    dot_general x1, matrix products, shards(): jnp.einsum('scd,dkf->sckf', slot_in, heavy_mlp_in, preferred_element_type...  30.4 us
    dot_general x1, matrix products, shards(): jnp.einsum('scd,sckf->dkf', slot_in, gates_grad_all, preferred_element_ty...  25.5 us
    concatenate x1, local copies, waits for them, and re-layouts, summed(): jnp.concatenate([p.reshape(model_width, -1).astype(jnp.bfloat16) for p in...  24.3 us
    dot_general x1, matrix products, shards(): jnp.einsum('scd,scf->df', slot_grad_all, hidden_all, preferred_element_ty...  22.2 us
    unnamed x4, other arithmetic  20.6 us
  transfers between devices with their start and end apart: 18, of which 2 were waited for; matrix products, arithmetic and copies ran while one was open for 35% of the time, Pallas kernels for 1%

profile of v1, /device:TPU:0, one launch (start us, length us, event | category | flops | bytes accessed | tf_op | source)
XLA Modules:
  0.0 791.2 jit_solution(1995282015247494218)
XLA Ops:
  10.4 3.6 fusion.65
  16.1 5.6 collective-permute-start
  30.0 3.6 fusion.124
  52.8 8.2 %all-to-all-start = ((bf16[16,96,256]{2,1,0:T(8,128)(2,1)}), bf16[16,96,256]{2,1,0:T(8,128)(2,1)}, u32[]{:S(2)}, u32[]{:S(2)}) async-start(bf16[16,96,256]{2,1,0:T(8,128)(2,1)} %fusion.138), calls=%async_computation | async-start | bytes 1572864 | tf_op jit(solution)/shard_map/all_to_all | solution.py:350
  66.1 2.8 reshape_squeeze.10
  75.7 3.9 copy.214
  82.6 3.9 copy.213
  95.4 7.3 heavy_forward.1.refs_2_
  103.9 6.9 copy.332
  111.2 9.9 %reduce.22 = bf16[1536,64]{1,0:T(8,128)(2,1)S(1)} reduce(bf16[1536,1,64]{2,1,0:T(2,128)(2,1)} %bitcast.398, bf16[]{:T(256)} %broadcast.518), dimensions={1}, to_apply=%bitcast.373.reduce_sub_computation | reduce | bytes 393218
  122.1 7.0 all-to-all-start.1
  129.1 5.0 fusion.98
  138.7 3.4 fusion.170
  163.0 3.0 fusion.146
  171.3 4.3 fusion.14
  177.9 3.0 fusion.145
  181.0 4.3 bitcast_convert_fusion.1
  190.7 3.5 fusion.87
  194.2 6.4 subtract_convert_fusion.2
  217.4 7.3 all-to-all-start.2
  224.8 2.8 reshape.416
  229.7 5.5 multiply_reduce_fusion
  235.2 3.1 multiply_convert_fusion.3
  244.0 5.5 copy.235
  251.9 3.4 fusion.93
  258.6 4.6 collective-permute-start.6
  276.0 10.5 %heavy_backward.1 = (bf16[1,1536,128]{2,1,0:T(8,128)(2,1)}, bf16[1,1536,128]{2,1,0:T(8,128)(2,1)}) custom-call(bf16[1,1536,128]{2,1,0:T(8,128)(2,1)} %get-tuple-element.150.refs_0_, bf16[1,1536,128]{2,1,0:T(8,128)(2,1)} %get-tuple-element.149.refs_1_, f32[1,1536,128]{2,1,0:T(8,128)} %heavy_forward.1.refs_2_, bf16[1,1536,128]{2,1,0:T(8,128)(2,1)} %pad.20.refs_3_), custom_call_target="tpu_custom_call" | custom-call | tf_op jit(solution)/shard_map/heavy_backward/pallas_call | solution.py:192
  287.8 9.9 %copy.331 = bf16[1,1536,192]{2,0,1:T(2,128)(2,1)} copy(bf16[1,1536,192]{2,1,0:T(8,128)(2,1)S(1)} %pad_maximum_fusion.11) | data formatting | bytes 1179648 | tf_op jit(solution)/shard_map/concatenate | solution.py:551
  297.7 10.7 %reduce.23 = bf16[1536,192]{1,0:T(8,128)(2,1)} reduce(bf16[1536,1,192]{2,1,0:T(2,128)(2,1)} %bitcast.394, bf16[]{:T(256)} %broadcast.518), dimensions={1}, to_apply=%bitcast.372.reduce_sub_computation | reduce | bytes 1179650
  308.4 3.1 reshape.474
  311.4 7.7 all-to-all-start.3
  326.0 3.1 fusion.61
  329.1 2.9 bitcast_convert_fusion
  334.3 6.1 reshape.475
  340.4 4.6 copy.240
  364.5 24.3 %concatenate.99 = bf16[768,3077]{0,1:T(8,128)(2,1)} concatenate(bf16[768,1152]{0,1:T(8,128)(2,1)} %bitcast.405, bf16[768,1152]{0,1:T(8,128)(2,1)} %bitcast.393, bf16[768,384]{0,1:T(8,128)(2,1)} %fusion.93, bf16[768,384]{0,1:T(8,128)(2,1)} %fusion.96, bf16[768,1]{0,1:T(2,128)(2,1)S(1)} %broadcast_in_dim.55, bf16[768,1]{0,1:T(2,128)(2,1)S(1)} %copy-done.67, ...), dimensions={1} | concatenate | bytes 9452544 | tf_op jit(solution)/shard_map/concatenate | solution.py:608
  389.6 4.3 fusion.47
  393.9 224.3 %all-reduce.8.cloned.1.call-done = (bf16[768,3077]{0,1:T(8,128)(2,1)}, bf16[768,1536]{1,0:T(8,128)(2,1)}) async-done(((bf16[768,3077]{0,1:T(8,128)(2,1)}, bf16[768,1536]{1,0:T(8,128)(2,1)}), (bf16[768,3077]{0,1:T(8,128)(2,1)}, bf16[768,1536]{1,0:T(8,128)(2,1)})) %all-reduce.8.cloned.1.call-update) | async-done | bytes 7085584 | tf_op jit(solution)/shard_map/psum | solution.py:611
  618.2 3.6 slice.365
  625.5 3.5 fusion.236
  629.0 5.2 copy.260
  634.1 5.2 copy.262
  639.3 5.6 reshape.422
  653.0 30.4 %fusion.17 = f32[2,1536,2,2048]{3,1,0,2:T(8,128)} fusion(bf16[768,2,2048,1]{2,1,0,3:T(2,128)(2,1)} %bitcast.425, bf16[2,1536,768]{2,1,0:T(8,128)(2,1)} %all-gather.2.cloned.1.call-done, bf16[2,1536,768]{2,1,0:T(8,128)(2,1)} %collective-permute-done.11, pred[]{:T(512)S(6)} %eq.51), kind=kOutput, calls=%fused_computation.28 | convolution fusion | flops 19329712128 | bytes 66060288 | tf_op jit(solution)/shard_map/scd,dkf->sckf/dot_general | solution.py:445
  683.3 36.7 %fusion.13 = (bf16[2,1536,1,2048]{3,1,0,2:T(8,128)(2,1)}, bf16[2,1536,1,2048]{3,1,0,2:T(8,128)(2,1)}) fusion(f32[2,1536,2,2048]{3,1,0,2:T(8,128)} %fusion.17, bf16[768,2048]{1,0:T(8,128)(2,1)S(1)} %copy-done, bf16[2,1536,768]{2,1,0:T(8,128)(2,1)} %collective-permute-done.11, bf16[2,1536,768]{2,1,0:T(8,128)(2,1)} %all-gather.2.cloned.1.call-done, pred[]{:T(512)S(6)} %eq.51), kind=kOutput, calls=%fused_computation.20 | convolution fusion | flops 9817030656 | bytes 88080384 | tf_op jit(solution)/shard_map/scd,df->scf/dot_general | solution.py:448
  720.1 25.5 %fusion.21 = f32[768,2,2048]{2,0,1:T(8,128)S(1)} fusion(bf16[2,1536,1,2048]{3,1,0,2:T(8,128)(2,1)} %get-tuple-element.123, bf16[2,1536,1,2048]{3,1,0,2:T(8,128)(2,1)} %get-tuple-element.122, bf16[2,1536,768]{2,1,0:T(8,128)(2,1)} %all-gather.2.cloned.1.call-done, bf16[2,1536,768]{2,1,0:T(8,128)(2,1)} %collective-permute-done.11, pred[]{:T(512)S(6)} %eq.51), kind=kOutput, calls=%fused_computation.32 | convolution fusion | flops 19380043776 | bytes 47185920 | tf_op jit(solution)/shard_map/scd,sckf->dkf/dot_general | solution.py:461
  745.6 16.4 %copy.264 = f32[768,2,2048]{2,1,0:T(2,128)} copy(f32[768,2,2048]{2,0,1:T(8,128)S(1)} %fusion.21) | data formatting | bytes 25165824
  761.9 22.2 %fusion.28 = f32[768,2048]{1,0:T(8,128)} fusion(f32[2,1536,2,2048]{3,1,0,2:T(8,128)} %fusion.17, bf16[2,1536,768]{2,1,0:T(8,128)(2,1)} %collective-permute-done.11, bf16[2,1536,768]{2,1,0:T(8,128)(2,1)} %all-gather.2.cloned.1.call-done, pred[]{:T(512)S(6)} %eq.51), kind=kOutput, calls=%fused_computation.54 | convolution fusion | flops 9728950272 | bytes 66060288 | tf_op jit(solution)/shard_map/scd,scf->df/dot_general | solution.py:458
  (359 shorter events, 182.2 us)
Async XLA Ops:
  7.2 168.4 %copy-start = (bf16[768,2048]{1,0:T(8,128)(2,1)S(1)}, bf16[768,2048]{1,0:T(8,128)(2,1)}, u32[]{:S(2)}) copy-start(bf16[768,2048]{1,0:T(8,128)(2,1)} %param.31) | copy-start | bytes 9437188
  9.5 14.1 %copy-start.57 = (f32[2,384]{1,0:T(2,128)}, f32[2,384]{1,0:T(2,128)S(1)}, u32[]{:S(2)}) copy-start(f32[2,384]{1,0:T(2,128)S(1)} %get-tuple-element.162) | copy-start | bytes 9220
  10.3 13.3 %copy-start.52 = (f32[768]{0:T(1024)}, f32[768]{0:T(1024)S(1)}, u32[]{:S(2)}) copy-start(f32[768]{0:T(1024)S(1)} %get-tuple-element.108) | copy-start | bytes 9220
  10.3 12.7 %copy-start.81 = (s32[2,96]{1,0:T(2,128)S(1)}, s32[2,96]{1,0:T(2,128)}, u32[]{:S(2)}) copy-start(s32[2,96]{1,0:T(2,128)} %param.34) | copy-start | bytes 2308
  10.3 12.7 %copy-start.82 = (s32[2,96]{1,0:T(2,128)S(1)}, s32[2,96]{1,0:T(2,128)}, u32[]{:S(2)}) copy-start(s32[2,96]{1,0:T(2,128)} %param.33) | copy-start | bytes 2308
  16.1 55.1 %collective-permute-start = (bf16[2,128,2,384]{3,1,2,0:T(8,128)(2,1)}, bf16[2,128,2,384]{3,1,2,0:T(8,128)(2,1)}, u32[]{:S(2)}, u32[]{:S(2)}) collective-permute-start(bf16[2,128,2,384]{3,1,2,0:T(8,128)(2,1)} %get-tuple-element.141), channel_id=1, source_target_pairs={{0,2},{2,4},{4,6},{6,8},{8,10},{10,12},{12,14},{14,16},{16,18},{18... | collective-permute-start | bytes 1179656 | tf_op jit(solution)/shard_map/ppermute | solution.py:27
  21.7 49.5 %collective-permute-start.1 = (bf16[2,128,2,384]{3,1,2,0:T(8,128)(2,1)}, bf16[2,128,2,384]{3,1,2,0:T(8,128)(2,1)}, u32[]{:S(2)}, u32[]{:S(2)}) collective-permute-start(bf16[2,128,2,384]{3,1,2,0:T(8,128)(2,1)} %get-tuple-element.142), channel_id=1, source_target_pairs={{2,0},{4,2},{6,4},{8,6},{10,8},{12,10},{14,12},{16,14},{18,16},{20... | collective-permute-start | bytes 1179656 | tf_op jit(solution)/shard_map/ppermute | solution.py:28
  23.6 4.5 copy-start.63
  25.5 4.5 copy-start.50
  35.1 10.8 %copy-start.69 = (f32[2,96]{1,0:T(2,128)}, f32[2,96]{1,0:T(2,128)S(1)}, u32[]{:S(2)}) copy-start(f32[2,96]{1,0:T(2,128)S(1)} %add_divide_fusion.1) | copy-start | bytes 2308
  37.5 27.9 %copy-start.59 = (s32[2,96]{1,0:T(2,128)}, s32[2,96]{1,0:T(2,128)S(1)}, u32[]{:S(2)}) copy-start(s32[2,96]{1,0:T(2,128)S(1)} %broadcast_subtract_fusion.2) | copy-start | bytes 2308
  52.8 40.5 %all-to-all-start = ((bf16[16,96,256]{2,1,0:T(8,128)(2,1)}), bf16[16,96,256]{2,1,0:T(8,128)(2,1)}, u32[]{:S(2)}, u32[]{:S(2)}) async-start(bf16[16,96,256]{2,1,0:T(8,128)(2,1)} %fusion.138), calls=%async_computation | async-start | bytes 1572864 | tf_op jit(solution)/shard_map/all_to_all | solution.py:350
  89.2 39.9 %copy-start.47 = (f32[2,3,4,128]{3,2,1,0:T(4,128)}, f32[2,3,4,128]{3,2,1,0:T(4,128)S(1)}, u32[]{:S(2)}) copy-start(f32[2,3,4,128]{3,2,1,0:T(4,128)S(1)} %get-tuple-element.165) | copy-start | bytes 36868
  122.1 20.1 %all-to-all-start.1 = ((bf16[16,2,3072]{2,1,0:T(2,128)(2,1)}), bf16[16,2,3072]{2,1,0:T(2,128)(2,1)S(1)}, u32[]{:S(2)}, u32[]{:S(2)}) async-start(bf16[16,2,3072]{2,1,0:T(2,128)(2,1)} %reshape.472), calls=%async_computation.1 | async-start | bytes 393216 | tf_op jit(solution)/shard_map/all_to_all | solution.py:353
  129.1 259.9 %all-gather.2.cloned.1.call-start = ((), (), s32[]{:S(2)}) async-start(), calls=%async_computation.4 | async-start | bytes 5013504 | tf_op jit(solution)/shard_map/all_gather | solution.py:439
  138.7 9.2 %copy-start.61 = (f32[2,96]{1,0:T(2,128)S(1)}, f32[2,96]{1,0:T(2,128)}, u32[]{:S(2)}) copy-start(f32[2,96]{1,0:T(2,128)} %get-tuple-element.177) | copy-start | bytes 2308
  142.2 8.0 %copy-start.34 = (bf16[2,96,384]{2,1,0:T(8,128)(2,1)S(1)}, bf16[2,96,384]{2,1,0:T(8,128)(2,1)}, u32[]{:S(2)}) copy-start(bf16[2,96,384]{2,1,0:T(8,128)(2,1)} %fusion.191) | copy-start | bytes 442372
  150.2 4.7 copy-start.48
  150.3 4.7 copy-start.49
  151.8 3.2 collective-permute-start.2
  161.0 9.1 %copy-start.23 = (bf16[2,384,768]{2,1,0:T(8,128)(2,1)}, bf16[2,384,768]{2,1,0:T(8,128)(2,1)S(1)}, u32[]{:S(2)}) copy-start(bf16[2,384,768]{2,1,0:T(8,128)(2,1)S(1)} %fusion.60) | copy-start | bytes 3538948
  161.0 10.2 %slice-start.2 = ((s8[6291456]{0:T(1024)(128)(4,1)}), s8[4194304]{0:T(1024)(128)(4,1)S(1)}, s32[]{:S(2)}) async-start(s8[6291456]{0:T(1024)(128)(4,1)} %bitcast.426), calls=%async_computation.8 | async-start | bytes 8388608
  163.0 8.3 %slice-start.3 = ((s8[6291456]{0:T(1024)(128)(4,1)}), s8[2097152]{0:T(1024)(128)(4,1)S(1)}, s32[]{:S(2)}) async-start(s8[6291456]{0:T(1024)(128)(4,1)} %bitcast.426), calls=%async_computation.9 | async-start | bytes 4194304
  190.2 14.6 %collective-permute-start.5 = (bf16[2,96]{1,0:T(2,128)(2,1)S(1)}, bf16[2,96]{1,0:T(2,128)(2,1)S(1)}, u32[]{:S(2)}, u32[]{:S(2)}) collective-permute-start(bf16[2,96]{1,0:T(2,128)(2,1)S(1)} %get-tuple-element.158), channel_id=1, source_target_pairs={{0,1},{1,0},{2,3},{3,2},{4,5},{5,4},{6,7},{7,6},{8,9},{9,8},{10,11... | collective-permute-start | bytes 1160 | tf_op jit(solution)/shard_map/ppermute | solution.py:79
  190.7 3.5 copy-start.86
  201.2 6.1 collective-permute-start.4
  202.9 6.0 collective-permute-start.3
  213.7 57.7 %collective-permute-start.9 = (bf16[2,96]{1,0:T(2,128)(2,1)}, bf16[2,96]{1,0:T(2,128)(2,1)}, u32[]{:S(2)}, u32[]{:S(2)}) collective-permute-start(bf16[2,96]{1,0:T(2,128)(2,1)} %get-tuple-element.168), channel_id=1, source_target_pairs={{0,1},{1,0},{2,3},{3,2},{4,5},{5,4},{6,7},{7,6},{8,9},{9,8},{10,11... | collective-permute-start | bytes 1160 | tf_op jit(solution)/shard_map/ppermute | solution.py:79
  217.4 54.9 %all-to-all-start.2 = ((bf16[16,96,64]{1,2,0:T(8,128)(2,1)}), bf16[16,96,64]{1,2,0:T(8,128)(2,1)}, u32[]{:S(2)}, u32[]{:S(2)}) async-start(bf16[16,96,64]{1,2,0:T(8,128)(2,1)} %pad.19), calls=%async_computation.2 | async-start | bytes 524288 | tf_op jit(solution)/shard_map/all_to_all | solution.py:350
  229.7 10.0 %slice-start = ((s8[4718592]{0:T(1024)(128)(4,1)}), s8[524288]{0:T(1024)(128)(4,1)S(1)}, s32[]{:S(2)}) async-start(s8[4718592]{0:T(1024)(128)(4,1)} %bitcast.377), calls=%async_computation.6 | async-start | bytes 1048576
  235.2 4.6 slice-start.1
  244.0 5.5 copy-start.62
  249.5 5.8 copy-start.7
  249.5 5.8 copy-start.12
  258.6 60.6 %collective-permute-start.6 = (bf16[2,128,2,384]{3,1,2,0:T(8,128)(2,1)S(1)}, bf16[2,128,2,384]{3,1,2,0:T(8,128)(2,1)}, u32[]{:S(2)}, u32[]{:S(2)}) collective-permute-start(bf16[2,128,2,384]{3,1,2,0:T(8,128)(2,1)S(1)} %get-tuple-element.137), channel_id=1, source_target_pairs={{0,2},{2,4},{4,6},{6,8},{8,10},{10,12},{12,14},{14,16},{16,18},{18... | collective-permute-start | bytes 1179656 | tf_op jit(solution)/shard_map/ppermute | solution.py:27
  263.2 56.0 %collective-permute-start.7 = (bf16[2,128,2,384]{3,1,2,0:T(8,128)(2,1)}, bf16[2,128,2,384]{3,1,2,0:T(8,128)(2,1)}, u32[]{:S(2)}, u32[]{:S(2)}) collective-permute-start(bf16[2,128,2,384]{3,1,2,0:T(8,128)(2,1)} %get-tuple-element.138), channel_id=1, source_target_pairs={{2,0},{4,2},{6,4},{8,6},{10,8},{12,10},{14,12},{16,14},{18,16},{20... | collective-permute-start | bytes 1179656 | tf_op jit(solution)/shard_map/ppermute | solution.py:28
  266.0 4.8 copy-start.75
  266.0 5.4 copy-start.72
  266.0 5.4 copy-start.79
  311.4 22.9 %all-to-all-start.3 = ((bf16[16,2,9216]{2,1,0:T(2,128)(2,1)}), bf16[16,2,9216]{2,1,0:T(2,128)(2,1)}, u32[]{:S(2)}, u32[]{:S(2)}) async-start(bf16[16,2,9216]{2,1,0:T(2,128)(2,1)} %reshape.474), calls=%async_computation.3 | async-start | bytes 1179648 | tf_op jit(solution)/shard_map/all_to_all | solution.py:353
  319.1 299.0 %all-reduce.8.cloned.1.call-start = ((), (), s32[]{:S(2)}) async-start(), calls=%async_computation.5 | async-start | bytes 14180352 | tf_op jit(solution)/shard_map/psum | solution.py:611
  351.3 5.1 copy-start.37
  351.3 5.1 copy-start.70
  357.8 5.0 copy-start.13
  357.8 5.0 collective-permute-start.8
  358.4 2.5 collective-permute-start.10
  388.9 264.0 %collective-permute-start.11 = (bf16[2,1536,768]{2,1,0:T(8,128)(2,1)}, bf16[2,1536,768]{2,1,0:T(8,128)(2,1)}, u32[]{:S(2)}, u32[]{:S(2)}) collective-permute-start(bf16[2,1536,768]{2,1,0:T(8,128)(2,1)} %all-gather.2.cloned.1.call-done), channel_id=1, source_target_pairs={{0,1},{1,0},{2,3},{3,2},{4,5},{5,4},{6,7},{7,6},{8,9},{9,8},{10,11... | collective-permute-start | bytes 14155784 | tf_op jit(solution)/shard_map/ppermute | solution.py:79
  618.1 6.1 copy-start.8
  (61 other events, 126.8 us)
Sparse Core Ops, SparseCore 0:
  181.1 81.9 all-gather.1
  389.0 229.0 all-reduce.7

commit v2 on v0

v2 whole, which is shorter than its diff:
```python
import math

import jax
import jax.numpy as jnp
from jax import lax
from jax.experimental import pallas as pl
from jax.experimental.pallas import tpu as pltpu
from jax.sharding import PartitionSpec as P

LHD = 96
HHD = 64
WIN = 128
LANES = 128

EPSILON = 1e-06
MASKED = -1e30
EXACT = lax.Precision.HIGHEST
LOW = jnp.bfloat16
WIDE = jnp.float32

ROW_QUERY, ROW_KEY, ROW_MLP, OK_QUERY, OK_KEY, OK_MLP = range(6)


def lanes_of(shape):
    return lax.broadcasted_iota(jnp.int32, shape, len(shape) - 1)


def dot(a, b):
    return jnp.dot(a, b, preferred_element_type=WIDE)


def rows_dot(a, b):
    return lax.dot_general(a, b, (((1,), (1,)), ((), ())), preferred_element_type=WIDE)


def cols_dot(a, b):
    return lax.dot_general(a, b, (((0,), (0,)), ((), ())), preferred_element_type=WIDE)


def rms_of(values):
    return lax.rsqrt(jnp.mean(values * values, axis=-1, keepdims=True) + EPSILON)


def column(values, index):
    return values[:, index : index + 1]


def columns(shape, *parts):
    lane = lanes_of(shape)
    out = jnp.zeros(shape, WIDE)
    for index, part in enumerate(parts):
        out = jnp.where(lane == index, part, out)
    return out


def hot_rows(slots, index, length):
    rows = column(slots, index)
    return (lanes_of((rows.shape[0], length)) == rows).astype(WIDE)


def place_rows(hot, values):
    high = values.astype(LOW)
    rest = (values - high.astype(WIDE)).astype(LOW)
    return cols_dot(hot, high) + cols_dot(hot, rest)


def exact_place(hot, values):
    return lax.dot_general(
        hot, values, (((0,), (0,)), ((), ())), precision=EXACT, preferred_element_type=WIDE
    )


def exact_pick(hot, values):
    return jnp.dot(hot, values, precision=EXACT, preferred_element_type=WIDE)


def row_dots(values, vector):
    return jnp.sum(values * vector, axis=-1, keepdims=True)


def norm_back(values, factor, weighted):
    inner = jnp.mean(weighted * values, axis=-1, keepdims=True)
    return factor * weighted - values * (factor * factor * factor) * inner


def gelu_parts(gate, up, hidden_grad):
    root = math.sqrt(2.0 / math.pi)
    cube = 0.044715 * root
    square = gate * gate
    bend = jnp.tanh(gate * (root + cube * square))
    half = 0.5 + 0.5 * bend
    value = gate * half
    slope = half + gate * (1.0 - bend * bend) * (0.5 * root + (1.5 * cube) * square)
    return value * up, slope * up * hidden_grad, value * hidden_grad


def merge_heads(ref, offset, heads):
    tiles = []
    for head in range(0, heads, 2):
        first = ref[head, :, offset : offset + LANES].astype(WIDE)
        second = ref[head + 1, :, offset : offset + LANES].astype(WIDE)
        lane = lanes_of(first.shape)
        tiles.append(jnp.where(lane < HHD, first, pltpu.roll(second, HHD, 1)))
    return jnp.concatenate(tiles, axis=1)


def merge_upper(ref, heads):
    tiles = []
    for head in range(0, heads, 2):
        first = ref[head, :, :LANES].astype(WIDE)
        second = ref[head + 1, :, :LANES].astype(WIDE)
        lane = lanes_of(first.shape)
        tiles.append(jnp.where(lane < HHD, pltpu.roll(first, HHD, 1), second))
    return jnp.concatenate(tiles, axis=1)


def head_low(values, head):
    tile = values[:, head // 2 * LANES : (head // 2 + 1) * LANES]
    return tile if head % 2 == 0 else pltpu.roll(tile, HHD, 1)


def head_high(values, head):
    tile = values[:, head // 2 * LANES : (head // 2 + 1) * LANES]
    return tile if head % 2 == 1 else pltpu.roll(tile, HHD, 1)


def spread_matrix(heads):
    row = lax.broadcasted_iota(jnp.int32, (heads * LHD, heads * LANES), 0)
    lane = lanes_of((heads * LHD, heads * LANES))
    inner = lane & (LANES - 1)
    hit = (row == (lane >> 7) * LHD + inner) & (inner < LHD)
    return hit.astype(WIDE).astype(LOW)


def params(mib=56):
    return pltpu.CompilerParams(vmem_limit_bytes=mib * 2**20)


def whole(array):
    zeros = (0,) * array.ndim
    return pl.BlockSpec(array.shape, lambda *_: zeros, pipeline_mode=pl.Buffered(1))


def each(array):
    rest = (0,) * (array.ndim - 1)
    return pl.BlockSpec((1,) + array.shape[1:], lambda s: (s,) + rest)


def like(shape, kind):
    return jax.ShapeDtypeStruct(shape, kind)


def front_kernel(
    tokens_ref, gains_ref, routers_ref, slots_ref, light_ref, heavy_ref,
    low_ref, qkv_ref, pair_ref, raw_ref, gate_ref,
):
    inputs = tokens_ref[0].astype(WIDE)
    length = inputs.shape[0]
    normed = inputs * rms_of(inputs) * gains_ref[0:1, :]
    low = normed.astype(LOW)
    low_ref[0] = low
    slots = slots_ref[0]
    hot_query = hot_rows(slots, ROW_QUERY, length)
    hot_key = hot_rows(slots, ROW_KEY, length)
    logits = columns(
        (length, LANES),
        row_dots(normed, routers_ref[0:1, :]),
        row_dots(normed, routers_ref[1:2, :]),
    )
    query_gate = jax.nn.sigmoid(column(exact_pick(hot_query, logits), 0))
    key_gate = jax.nn.sigmoid(column(exact_pick(hot_key, logits), 1))
    gate_ref[0] = columns((slots.shape[0], LANES), query_gate, key_gate)
    query_in = dot(hot_query.astype(LOW), low).astype(LOW)
    key_in = dot(hot_key.astype(LOW), low).astype(LOW)
    query = dot(query_in, heavy_ref[0]).astype(LOW).astype(WIDE)
    key = dot(key_in, heavy_ref[1]).astype(LOW).astype(WIDE)
    raw = dot(key_in, heavy_ref[2])
    raw_ref[0] = raw
    value = (key_gate * raw).astype(LOW).astype(WIDE)
    bias = jnp.where(column(slots, OK_KEY) > 0, 0.0, MASKED)
    lane = lanes_of((slots.shape[0], LANES))
    for head in range(raw.shape[1] // HHD):
        both = jnp.where(lane < HHD, head_low(query, head), head_high(key, head))
        extra = jnp.where(lane < HHD, head_low(value, head), bias)
        pair_ref[head, :, :LANES] = both.astype(LOW)
        pair_ref[head, :, LANES:] = extra.astype(LOW)
    for kind in range(3):
        qkv_ref[0, kind] = dot(low, light_ref[kind]).astype(LOW)


def front(tokens, gains, routers, slots, light, heavy, seq_devices):
    seqs, length, width = tokens.shape
    cap = slots.shape[1]
    light_cols, heavy_cols = light.shape[2], heavy.shape[2]
    heads = heavy_cols // HHD
    shapes = [
        like(tokens.shape, LOW),
        like((seqs, 3, length, light_cols), LOW),
        like((seq_devices, cap, 2 * LANES), LOW),
        like((seqs, cap, heavy_cols), WIDE),
        like((seqs, cap, LANES), WIDE),
    ]
    specs = [each(s) for s in shapes]
    specs[2] = pl.BlockSpec((heads, cap, 2 * LANES), lambda s: (s, 0, 0))
    return pl.pallas_call(
        front_kernel,
        grid=(seqs,),
        in_specs=[each(tokens), whole(gains), whole(routers), each(slots), whole(light), whole(heavy)],
        out_specs=specs,
        out_shape=shapes,
        compiler_params=params(),
        name="front",
    )(tokens, gains, routers, slots, light, heavy)


def window_bias(block, length, base, total):
    row = lax.broadcasted_iota(jnp.int32, (WIN, 3 * WIN), 0)
    col = lanes_of((WIN, 3 * WIN))
    place = base + (block - 1) * WIN + col
    near = jnp.abs(col - WIN - row) < WIN
    return jnp.where(near & (place >= 0) & (place < total), 0.0, MASKED)


def light_forward_kernel(
    scale, place_ref, qkv_ref, before_ref, after_ref, gains_ref, weight_ref, out_ref,
    mix_ref, attn_ref, lse_ref, query_ref, window_ref, wide_ref,
):
    length, light_cols = qkv_ref.shape[2:]
    heads = light_cols // LHD
    spread = spread_matrix(heads)
    query_ref[0] = dot(qkv_ref[0, 0], spread).astype(LOW)
    edges = ((before_ref, slice(0, WIN)), (after_ref, slice(WIN + length, 2 * WIN + length)))
    for ref, rows in edges:
        inputs = ref[0].astype(WIDE)
        low = (inputs * rms_of(inputs) * gains_ref[0:1, :]).astype(LOW)
        for kind in range(2):
            edge = dot(low, weight_ref[1 + kind]).astype(LOW)
            window_ref[0, kind, rows, :] = dot(edge, spread).astype(LOW)
    for kind in range(2):
        window_ref[0, kind, WIN : WIN + length, :] = dot(qkv_ref[0, 1 + kind], spread).astype(LOW)
    for block in range(length // WIN):
        rows = slice(block * WIN, (block + 1) * WIN)
        near = slice(block * WIN, (block + 3) * WIN)
        bias = window_bias(block, length, place_ref[0, 0], place_ref[0, 1])
        kept = []
        for head in range(heads):
            lanes = slice(head * LANES, (head + 1) * LANES)
            scores = rows_dot(query_ref[0, rows, lanes], window_ref[0, 0, near, lanes]) * scale + bias
            top = jnp.max(scores, axis=-1, keepdims=True)
            expo = jnp.exp(scores - top)
            total = jnp.sum(expo, axis=-1, keepdims=True)
            mixed = dot(expo.astype(LOW), window_ref[0, 1, near, lanes]) / total
            wide_ref[rows, lanes] = mixed.astype(LOW)
            kept.append(top + jnp.log(total))
        lse_ref[0, rows, :] = columns((WIN, LANES), *kept)
    mix = rows_dot(wide_ref[...], spread).astype(LOW)
    mix_ref[0] = mix
    attn_ref[0] = rows_dot(mix, out_ref[...])


def light_forward(place, qkv, before, after, gains, weight, weight_out):
    seqs, _, length, light_cols = qkv.shape
    heads = light_cols // LHD
    shapes = [
        like((seqs, length, light_cols), LOW),
        like((seqs, length, weight_out.shape[0]), WIDE),
        like((seqs, length, LANES), WIDE),
        like((seqs, length, heads * LANES), LOW),
        like((seqs, 2, length + 2 * WIN, heads * LANES), LOW),
    ]
    return pl.pallas_call(
        lambda *refs: light_forward_kernel(1.0 / math.sqrt(LHD), *refs),
        grid=(seqs,),
        in_specs=[
            pl.BlockSpec(memory_space=pltpu.SMEM),
            each(qkv),
            each(before),
            each(after),
            whole(gains),
            whole(weight),
            whole(weight_out),
        ],
        out_specs=[each(s) for s in shapes],
        out_shape=shapes,
        scratch_shapes=[pltpu.VMEM((length, heads * LANES), LOW)],
        compiler_params=params(),
        name="light_forward",
    )(place, qkv, before, after, gains, weight, weight_out)


def light_backward_kernel(
    scale, place_ref, query_ref, window_ref, lse_ref, grad_ref, local_ref, early_ref, late_ref, *scratch
):
    wide_ref, dkey_ref, dvalue_ref = scratch
    length, light_cols = grad_ref.shape[1:]
    heads = light_cols // LHD
    spread = spread_matrix(heads)
    grad = dot(grad_ref[0], spread).astype(LOW)
    dkey_ref[...] = jnp.zeros_like(dkey_ref)
    dvalue_ref[...] = jnp.zeros_like(dvalue_ref)
    for block in range(length // WIN):
        rows = slice(block * WIN, (block + 1) * WIN)
        near = slice(block * WIN, (block + 3) * WIN)
        bias = window_bias(block, length, place_ref[0, 0], place_ref[0, 1])
        lse = lse_ref[0, rows, :]
        for head in range(heads):
            lanes = slice(head * LANES, (head + 1) * LANES)
            key = window_ref[0, 0, near, lanes]
            part = grad[rows, lanes]
            mine = query_ref[0, rows, lanes]
            probs = jnp.exp(rows_dot(mine, key) * scale + bias - column(lse, head))
            prob_grad = rows_dot(part, window_ref[0, 1, near, lanes])
            delta = jnp.sum(probs * prob_grad, axis=-1, keepdims=True)
            score_grad = (probs * (prob_grad - delta)).astype(LOW)
            wide_ref[rows, lanes] = (dot(score_grad, key) * scale).astype(LOW)
            dkey_ref[near, lanes] += cols_dot(score_grad, mine) * scale
            dvalue_ref[near, lanes] += cols_dot(probs.astype(LOW), part)
    local_ref[0, 0] = rows_dot(wide_ref[...], spread).astype(LOW)
    for kind, ref in ((1, dkey_ref), (2, dvalue_ref)):
        all_rows = rows_dot(ref[...].astype(LOW), spread).astype(LOW)
        early_ref[0, kind - 1] = all_rows[:WIN]
        local_ref[0, kind] = all_rows[WIN : WIN + length]
        late_ref[0, kind - 1] = all_rows[WIN + length :]


def light_backward(place, query, window, lse, grad):
    seqs, length, light_cols = grad.shape
    edge = like((seqs, 2, WIN, light_cols), LOW)
    shapes = [like((seqs, 3, length, light_cols), LOW), edge, edge]
    return pl.pallas_call(
        lambda *refs: light_backward_kernel(1.0 / math.sqrt(LHD), *refs),
        grid=(seqs,),
        in_specs=[
            pl.BlockSpec(memory_space=pltpu.SMEM),
            each(query),
            each(window),
            each(lse),
            each(grad),
        ],
        out_specs=[each(s) for s in shapes],
        out_shape=shapes,
        scratch_shapes=[
            pltpu.VMEM(query.shape[1:], LOW),
            pltpu.VMEM(window.shape[2:], WIDE),
            pltpu.VMEM(window.shape[2:], WIDE),
        ],
        compiler_params=params(),
        name="light_backward",
    )(place, query, window, lse, grad)


def key_operand(pair, extra):
    lane = lanes_of(pair.shape)
    moved = pltpu.roll(pair.astype(WIDE), HHD, 1)
    bias = column(extra, HHD).astype(WIDE)
    return jnp.where(lane < HHD, moved, jnp.where(lane == HHD, bias, 0.0)).astype(LOW)


def query_operand(pair, scale):
    lane = lanes_of(pair.shape)
    scaled = pair.astype(WIDE) * scale
    return jnp.where(lane < HHD, scaled, jnp.where(lane == HHD, 1.0, 0.0)).astype(LOW)


def heavy_forward_kernel(tile, scale, pair_ref, kept_ref, mix_ref, key_ref):
    @pl.when(pl.program_id(0) == 0)
    def _():
        key_ref[...] = key_operand(pair_ref[:, :LANES], pair_ref[:, LANES:])

    start = pl.multiple_of(pl.program_id(0) * tile, tile)
    query = query_operand(pair_ref[pl.ds(start, tile), :LANES], scale)
    scores = rows_dot(query, key_ref[...])
    top = jnp.max(scores, axis=-1, keepdims=True)
    expo = jnp.exp(scores - top)
    total = jnp.sum(expo, axis=-1, keepdims=True)
    mix = dot(expo.astype(LOW), pair_ref[:, LANES:]) / total
    lane = lanes_of(mix.shape)
    kept_ref[...] = jnp.where(lane < HHD, mix, top + jnp.log(total))
    mix_ref[...] = jnp.where(lane < HHD, mix, 0.0).astype(LOW)


def heavy_backward_kernel(
    tile, scale, pair_ref, kept_ref, grad_ref, both_ref, key_ref, dk_ref, dv_ref
):
    step = pl.program_id(0)

    @pl.when(step == 0)
    def _():
        key_ref[...] = key_operand(pair_ref[:, :LANES], pair_ref[:, LANES:])
        dk_ref[...] = jnp.zeros_like(dk_ref)
        dv_ref[...] = jnp.zeros_like(dv_ref)

    start = pl.multiple_of(step * tile, tile)
    query = query_operand(pair_ref[pl.ds(start, tile), :LANES], scale)
    lane = lanes_of(query.shape)
    kept = kept_ref[...]
    grad = grad_ref[...]
    lse = column(kept, HHD)
    delta = jnp.sum(
        jnp.where(lane < HHD, kept * grad.astype(WIDE), 0.0), axis=-1, keepdims=True
    )
    probs = jnp.exp(rows_dot(query, key_ref[...]) - lse)
    prob_grad = rows_dot(grad, pair_ref[:, LANES:])
    score_grad = (probs * (prob_grad - delta)).astype(LOW)
    query_grad = dot(score_grad, key_ref[...]) * scale
    both_ref[pl.ds(start, tile), :LANES] = jnp.where(lane < HHD, query_grad, 0.0).astype(LOW)
    dk_ref[...] += cols_dot(score_grad, query)
    dv_ref[...] += cols_dot(probs.astype(LOW), grad)

    @pl.when(step == pl.num_programs(0) - 1)
    def _():
        spot = lanes_of(dk_ref.shape)
        moved = pltpu.roll(dk_ref[...], HHD, 1)
        query_part = both_ref[:, :LANES].astype(WIDE)
        both_ref[:, :LANES] = jnp.where(spot < HHD, query_part, moved).astype(LOW)
        both_ref[:, LANES:] = dv_ref[...].astype(LOW)


def query_tile(length):
    return 256 if length % 256 == 0 else length


def heavy_forward(pair):
    length = pair.shape[0]
    tile = query_tile(length)
    rows = pl.BlockSpec((tile, LANES), lambda i: (i, 0))
    return pl.pallas_call(
        lambda *refs: heavy_forward_kernel(tile, 1.0 / math.sqrt(HHD), *refs),
        grid=(length // tile,),
        in_specs=[whole(pair)],
        out_specs=[rows, rows],
        out_shape=[like((length, LANES), WIDE), like((length, LANES), LOW)],
        scratch_shapes=[pltpu.VMEM((length, LANES), LOW)],
        compiler_params=params(60),
        name="heavy_forward",
    )(pair)


def heavy_backward(pair, kept, grad):
    length = pair.shape[0]
    tile = query_tile(length)
    rows = pl.BlockSpec((tile, LANES), lambda i: (i, 0))
    return pl.pallas_call(
        lambda *refs: heavy_backward_kernel(tile, 1.0 / math.sqrt(HHD), *refs),
        grid=(length // tile,),
        in_specs=[whole(pair), rows, rows],
        out_specs=whole(pair),
        out_shape=like(pair.shape, LOW),
        scratch_shapes=[
            pltpu.VMEM((length, LANES), LOW),
            pltpu.VMEM((length, LANES), WIDE),
            pltpu.VMEM((length, LANES), WIDE),
        ],
        compiler_params=params(60),
        name="heavy_backward",
    )(pair, kept, grad)


def combine_kernel(pairs_ref, attn_ref, out_ref, slots_ref, gate_ref, part_ref, mix_ref):
    slots = slots_ref[0]
    mix = merge_heads(pairs_ref, 0, pairs_ref.shape[0]).astype(LOW)
    mix_ref[0] = mix
    rows = rows_dot(mix, out_ref[...])
    weight = jnp.where(column(slots, OK_QUERY) > 0, column(gate_ref[0], 0), 0.0)
    hot = hot_rows(slots, ROW_QUERY, attn_ref.shape[1]).astype(LOW)
    part_ref[0] = (attn_ref[0] + place_rows(hot, weight * rows)).astype(LOW)


def pair_spec(pairs, heads):
    return pl.BlockSpec((heads,) + pairs.shape[1:], lambda s: (s, 0, 0))


def combine(pairs, attn, weight_out, slots, gate):
    seqs, cap = slots.shape[:2]
    heavy_cols = weight_out.shape[1]
    shapes = [like(attn.shape, LOW), like((seqs, cap, heavy_cols), LOW)]
    return pl.pallas_call(
        combine_kernel,
        grid=(seqs,),
        in_specs=[
            pair_spec(pairs, heavy_cols // HHD),
            each(attn),
            whole(weight_out),
            each(slots),
            each(gate),
        ],
        out_specs=[each(s) for s in shapes],
        out_shape=shapes,
        compiler_params=params(),
        name="combine",
    )(pairs, attn, weight_out, slots, gate)


def slots_kernel(
    core_ref, tokens_ref, own_ref, other_ref, up_ref, gains_ref, routers_ref, slots_ref,
    low_ref, rows_ref, slot_ref, ship_ref, gate_ref,
):
    middle = tokens_ref[0].astype(WIDE) + own_ref[0].astype(WIDE) + other_ref[0].astype(WIDE)
    length = middle.shape[0]
    normed = middle * rms_of(middle) * gains_ref[1:2, :]
    low = normed.astype(LOW)
    low_ref[0] = low
    slots = slots_ref[0]
    hot = hot_rows(slots, ROW_MLP, length)
    logits = columns((length, LANES), row_dots(normed, routers_ref[2:3, :]))
    gate = jax.nn.sigmoid(column(exact_pick(hot, logits), 0))
    weight = jnp.where(column(slots, OK_MLP) > 0, gate, 0.0)
    hot = hot.astype(LOW)
    rows = dot(hot, low)
    slot = weight * dot(hot, up_ref[0])
    rows_ref[0] = rows.astype(LOW)
    slot_ref[0] = slot.astype(LOW)
    ship_ref[0] = jnp.where(core_ref[0, 0] == 0, rows, slot).astype(LOW)
    gate_ref[0] = columns((slots.shape[0], LANES), gate, weight)


def mlp_slots(core, tokens, own, other, up, gains, routers, slots):
    seqs, length, width = tokens.shape
    cap = slots.shape[1]
    shapes = [like(tokens.shape, LOW)]
    shapes += [like((seqs, cap, width), LOW)] * 3 + [like((seqs, cap, LANES), WIDE)]
    return pl.pallas_call(
        slots_kernel,
        grid=(seqs,),
        in_specs=[
            pl.BlockSpec(memory_space=pltpu.SMEM),
            each(tokens), each(own), each(other), each(up), whole(gains), whole(routers), each(slots),
        ],
        out_specs=[each(s) for s in shapes],
        out_shape=shapes,
        compiler_params=params(),
        name="mlp_slots",
    )(core, tokens, own, other, up, gains, routers, slots)


def feed_kernel(
    low_ref, rows_ref, slot_ref, kept_ref, up_ref, slots_ref, in_ref, out_ref, heavy_in_ref,
    heavy_out_ref, part_ref, weights_ref, gate_ref, heavy_acc, back_acc, hidden_ref, dgate_ref, dup_ref,
):
    step = pl.program_id(0)
    seqs, length, width = up_ref.shape
    cap = slots_ref.shape[1]

    @pl.when(step == 0)
    def _():
        heavy_acc[...] = jnp.zeros_like(heavy_acc)
        back_acc[...] = jnp.zeros_like(back_acc)

    first, second, last = heavy_in_ref[0], heavy_in_ref[1], heavy_out_ref[...]
    rows = rows_ref[...]
    hidden, gate_grad, up_grad = gelu_parts(
        dot(rows, first), dot(rows, second), dot(slot_ref[...], last)
    )
    heavy_acc[...] += rows_dot(hidden.astype(LOW), last)
    back_acc[...] += rows_dot(gate_grad.astype(LOW), first) + rows_dot(up_grad.astype(LOW), second)

    @pl.when(step == pl.num_programs(0) - 1)
    def _():
        for s in range(seqs):
            here = slice(s * length, (s + 1) * length)
            mine = slice(s * cap, (s + 1) * cap)
            low = low_ref[s]
            hidden, gate_grad, up_grad = gelu_parts(
                dot(low, in_ref[0]), dot(low, in_ref[1]), dot(up_ref[s], out_ref[...])
            )
            hidden, gate_grad, up_grad = (
                hidden.astype(LOW),
                gate_grad.astype(LOW),
                up_grad.astype(LOW),
            )
            hidden_ref[here, :] = hidden
            dgate_ref[here, :] = gate_grad
            dup_ref[here, :] = up_grad
            hot = hot_rows(slots_ref[s], ROW_MLP, length).astype(LOW)
            kept = kept_ref[s]
            heavy_rows = heavy_acc[mine, :]
            part_ref[0, s] = (
                rows_dot(hidden, out_ref[...]) + place_rows(hot, column(kept, 1) * heavy_rows)
            ).astype(LOW)
            part_ref[1, s] = (
                rows_dot(gate_grad, in_ref[0])
                + rows_dot(up_grad, in_ref[1])
                + place_rows(hot, back_acc[mine, :])
            ).astype(LOW)
            gate_part = jnp.sum(dot(hot, up_ref[s]) * heavy_rows, axis=-1, keepdims=True)
            gate_ref[s] = columns((cap, LANES), column(kept, 0), gate_part)
        low = low_ref[...].reshape(seqs * length, width)
        up = up_ref[...].reshape(seqs * length, width)
        weights_ref[0] = cols_dot(low, dgate_ref[...]).astype(LOW)
        weights_ref[1] = cols_dot(low, dup_ref[...]).astype(LOW)
        weights_ref[2] = cols_dot(up, hidden_ref[...]).astype(LOW)


def feed(low, rows, slot, kept, up, slots, light_in, light_out, heavy_in, heavy_out):
    seqs, length, width = up.shape
    cap = slots.shape[1]
    hidden = light_out.shape[1]
    cols = 256
    rows, slot = rows.reshape(-1, width), slot.reshape(-1, width)
    shapes = [
        like((2, seqs, length, width), LOW),
        like((3, width, hidden), LOW),
        like((seqs, cap, LANES), WIDE),
    ]
    return pl.pallas_call(
        feed_kernel,
        grid=(heavy_out.shape[1] // cols,),
        in_specs=[
            whole(low),
            whole(rows),
            whole(slot),
            whole(kept),
            whole(up),
            whole(slots),
            whole(light_in),
            whole(light_out),
            pl.BlockSpec((2, width, cols), lambda i: (0, 0, i)),
            pl.BlockSpec((width, cols), lambda i: (0, i)),
        ],
        out_specs=[whole(s) for s in shapes],
        out_shape=shapes,
        scratch_shapes=[pltpu.VMEM((seqs * cap, width), WIDE)] * 2
        + [pltpu.VMEM((seqs * length, hidden), LOW)] * 3,
        compiler_params=params(),
        name="feed",
    )(low, rows, slot, kept, up, slots, light_in, light_out, heavy_in, heavy_out)


def middle_kernel(
    tokens_ref, own_ref, other_ref, part_ref, beyond_ref, up_ref, gains_ref, routers_ref, slots_ref,
    gate_ref, mlp_ref, mlp_other_ref, mix_ref, heavy_mix_ref, light_out_ref, heavy_out_ref,
    mixed_ref, middle_ref, grad_ref, pair_ref, weights_ref, small_ref, logit_ref, weights_acc,
):
    step = pl.program_id(0)

    @pl.when(step == 0)
    def _():
        weights_acc[...] = jnp.zeros_like(weights_acc)
        small_ref[...] = jnp.zeros_like(small_ref)

    slots = slots_ref[0]
    cap = slots.shape[0]
    middle = tokens_ref[0].astype(WIDE) + own_ref[0].astype(WIDE) + other_ref[0].astype(WIDE)
    length = middle.shape[0]
    factor = rms_of(middle)
    scaled = middle * factor
    normed = scaled * gains_ref[1:2, :]
    mixed = middle + (part_ref[0, 0].astype(WIDE) + beyond_ref[0, 0].astype(WIDE))
    mixed_ref[0] = mixed.astype(LOW)
    gate = column(mlp_ref[0], 0)
    gate_grad = column(mlp_ref[0], 1) + column(mlp_other_ref[0], 1)
    logit_grad = jnp.where(column(slots, OK_MLP) > 0, gate_grad * gate * (1.0 - gate), 0.0)
    token_grad = column(
        exact_place(hot_rows(slots, ROW_MLP, length), columns((cap, LANES), logit_grad)), 0
    )
    normed_grad = (
        part_ref[1, 0].astype(WIDE) + beyond_ref[1, 0].astype(WIDE)
    ) + token_grad * routers_ref[2:3, :]
    small_ref[0:1, :] += jnp.sum(normed_grad * scaled, axis=0, keepdims=True)
    small_ref[1:2, :] += jnp.sum(token_grad * normed, axis=0, keepdims=True)
    middle_grad = up_ref[0].astype(WIDE) + norm_back(middle, factor, normed_grad * gains_ref[1:2, :])
    middle_ref[0] = middle_grad
    low = middle_grad.astype(LOW)
    hot = hot_rows(slots, ROW_QUERY, length).astype(LOW)
    up_rows = dot(hot, low)
    weight = jnp.where(column(slots, OK_QUERY) > 0, column(gate_ref[0], 0), 0.0)
    slot = (weight * up_rows).astype(LOW)
    heavy_rows = rows_dot(heavy_mix_ref[0], heavy_out_ref[...])
    logit_ref[0] = columns(
        (cap, LANES), jnp.sum(up_rows * heavy_rows, axis=-1, keepdims=True)
    )
    mix_grad = dot(slot, heavy_out_ref[...]).astype(LOW).astype(WIDE)
    lane = lanes_of((cap, LANES))
    for head in range(mix_grad.shape[1] // HHD):
        pair_ref[head] = jnp.where(lane < HHD, head_low(mix_grad, head), 0.0).astype(LOW)
    grad_ref[0] = dot(low, light_out_ref[...]).astype(LOW)
    weights_acc[0] += cols_dot(low, mix_ref[0])
    weights_acc[1] += cols_dot(slot, heavy_mix_ref[0])

    @pl.when(step == pl.num_programs(0) - 1)
    def _():
        weights_ref[...] = weights_acc[...].astype(LOW)


def middle_back(
    tokens, own, other, part, beyond, up, gains, routers, slots, gate, mlp, mlp_other,
    mix, heavy_mix, light_out, heavy_out, seq_devices,
):
    seqs, length, width = tokens.shape
    cap = slots.shape[1]
    cols = light_out.shape[1]
    heads = heavy_out.shape[1] // HHD
    shapes = [
        like(tokens.shape, LOW),
        like(tokens.shape, WIDE),
        like((seqs, length, cols), LOW),
        like((seq_devices, cap, LANES), LOW),
        like((2, width, cols), LOW),
        like((8, width), WIDE),
        like((seqs, cap, LANES), WIDE),
    ]
    specs = [
        each(shapes[0]), each(shapes[1]), each(shapes[2]), pair_spec(shapes[3], heads),
        whole(shapes[4]), whole(shapes[5]), each(shapes[6]),
    ]
    both = pl.BlockSpec((2, 1, length, width), lambda s: (0, s, 0, 0))
    return pl.pallas_call(
        middle_kernel,
        grid=(seqs,),
        in_specs=[
            each(tokens), each(own), each(other), both, both, each(up), whole(gains),
            whole(routers), each(slots), each(gate), each(mlp), each(mlp_other), each(mix),
            each(heavy_mix), whole(light_out), whole(heavy_out),
        ],
        out_specs=specs,
        out_shape=shapes,
        scratch_shapes=[pltpu.VMEM((2, width, cols), WIDE)],
        compiler_params=params(),
        name="middle_back",
    )(
        tokens, own, other, part, beyond, up, gains, routers, slots, gate, mlp, mlp_other,
        mix, heavy_mix, light_out, heavy_out,
    )


def light_project_kernel(
    local_ref, lead_ref, tail_ref, low_ref, light_ref, grad_ref, part_ref, grad_acc
):
    step = pl.program_id(0)

    @pl.when(step == 0)
    def _():
        grad_acc[...] = jnp.zeros_like(grad_acc)

    low = low_ref[0]
    length = low.shape[0]
    part = jnp.zeros((length, low.shape[1]), WIDE)
    for kind in range(3):
        rows = local_ref[0, kind]
        if kind > 0:
            lead = rows[:WIN].astype(WIDE) + lead_ref[0, kind - 1].astype(WIDE)
            tail = rows[length - WIN :].astype(WIDE) + tail_ref[0, kind - 1].astype(WIDE)
            rows = jnp.concatenate(
                [lead.astype(LOW), rows[WIN : length - WIN], tail.astype(LOW)], axis=0
            )
        grad_acc[kind] += cols_dot(low, rows)
        part = part + rows_dot(rows, light_ref[kind])
    part_ref[0] = part

    @pl.when(step == pl.num_programs(0) - 1)
    def _():
        grad_ref[...] = grad_acc[...].astype(LOW)


def light_project(local, lead, tail, low, light):
    shapes = [like(light.shape, LOW), like(low.shape, WIDE)]
    return pl.pallas_call(
        light_project_kernel,
        grid=(low.shape[0],),
        in_specs=[each(local), each(lead), each(tail), each(low), whole(light)],
        out_specs=[whole(shapes[0]), each(shapes[1])],
        out_shape=shapes,
        scratch_shapes=[pltpu.VMEM(light.shape, WIDE)],
        compiler_params=params(),
        name="light_project",
    )(local, lead, tail, low, light)


def heavy_project_kernel(
    light_part_ref, low_ref, pairs_ref, heavy_ref, slots_ref, gate_ref, raw_ref, logit_ref,
    grad_ref, part_ref, both_logit_ref, grad_acc,
):
    step = pl.program_id(0)

    @pl.when(step == 0)
    def _():
        grad_acc[...] = jnp.zeros_like(grad_acc)

    low = low_ref[0]
    length = low.shape[0]
    slots = slots_ref[0]
    cap = slots.shape[0]
    heads = raw_ref.shape[2] // HHD
    key_gate = column(gate_ref[0], 1)
    query_grad = merge_heads(pairs_ref, 0, heads).astype(LOW)
    key_grad = merge_upper(pairs_ref, heads).astype(LOW)
    value_grad = merge_heads(pairs_ref, LANES, heads)
    raw_grad = (key_gate * value_grad).astype(LOW)
    key_logit = jnp.sum(value_grad * raw_ref[0], axis=-1, keepdims=True)
    both_logit_ref[0] = columns((cap, LANES), column(logit_ref[0], 0), key_logit)
    hot_query = hot_rows(slots, ROW_QUERY, length).astype(LOW)
    hot_key = hot_rows(slots, ROW_KEY, length).astype(LOW)
    query_in = dot(hot_query, low).astype(LOW)
    key_in = dot(hot_key, low).astype(LOW)
    grad_acc[0] += cols_dot(query_in, query_grad)
    grad_acc[1] += cols_dot(key_in, key_grad)
    grad_acc[2] += cols_dot(key_in, raw_grad)
    part = light_part_ref[0] + place_rows(hot_query, rows_dot(query_grad, heavy_ref[0]))
    part = part + place_rows(
        hot_key, rows_dot(key_grad, heavy_ref[1]) + rows_dot(raw_grad, heavy_ref[2])
    )
    part_ref[0] = part.astype(LOW)

    @pl.when(step == pl.num_programs(0) - 1)
    def _():
        grad_ref[...] = grad_acc[...].astype(LOW)


def heavy_project(light_part, low, pairs, heavy, slots, gate, raw, logit):
    heads = heavy.shape[2] // HHD
    shapes = [like(heavy.shape, LOW), like(low.shape, LOW), like(logit.shape, WIDE)]
    return pl.pallas_call(
        heavy_project_kernel,
        grid=(low.shape[0],),
        in_specs=[
            each(light_part), each(low), pair_spec(pairs, heads), whole(heavy), each(slots),
            each(gate), each(raw), each(logit),
        ],
        out_specs=[whole(shapes[0]), each(shapes[1]), each(shapes[2])],
        out_shape=shapes,
        scratch_shapes=[pltpu.VMEM(heavy.shape, WIDE)],
        compiler_params=params(),
        name="heavy_project",
    )(light_part, low, pairs, heavy, slots, gate, raw, logit)


def input_kernel(
    part_ref, other_ref, logit_ref, logit_other_ref, gate_ref, slots_ref, tokens_ref, gains_ref,
    routers_ref, middle_ref, small_in_ref, grad_ref, small_ref,
):
    @pl.when(pl.program_id(0) == 0)
    def _():
        small_ref[...] = small_in_ref[...]

    slots = slots_ref[0]
    cap = slots.shape[0]
    inputs = tokens_ref[0].astype(WIDE)
    length = inputs.shape[0]
    factor = rms_of(inputs)
    scaled = inputs * factor
    normed = scaled * gains_ref[0:1, :]
    gates = gate_ref[0]
    grads = (logit_ref[0] + logit_other_ref[0]) * gates * (1.0 - gates)
    query_logit = jnp.where(column(slots, OK_QUERY) > 0, column(grads, 0), 0.0)
    key_logit = jnp.where(column(slots, OK_KEY) > 0, column(grads, 1), 0.0)
    query_token = column(
        exact_place(hot_rows(slots, ROW_QUERY, length), columns((cap, LANES), query_logit)), 0
    )
    key_token = column(
        exact_place(hot_rows(slots, ROW_KEY, length), columns((cap, LANES), key_logit)), 0
    )
    normed_grad = (
        (part_ref[0].astype(WIDE) + other_ref[0].astype(WIDE))
        + query_token * routers_ref[0:1, :]
        + key_token * routers_ref[1:2, :]
    )
    small_ref[2:3, :] += jnp.sum(normed_grad * scaled, axis=0, keepdims=True)
    small_ref[3:4, :] += jnp.sum(query_token * normed, axis=0, keepdims=True)
    small_ref[4:5, :] += jnp.sum(key_token * normed, axis=0, keepdims=True)
    grad_ref[0] = middle_ref[0] + norm_back(inputs, factor, normed_grad * gains_ref[0:1, :])


def input_back(part, other, logit, logit_other, gate, slots, tokens, gains, routers, middle, small):
    shapes = [like(middle.shape, WIDE), like(small.shape, WIDE)]
    return pl.pallas_call(
        input_kernel,
        grid=(tokens.shape[0],),
        in_specs=[
            each(part), each(other), each(logit), each(logit_other), each(gate), each(slots),
            each(tokens), whole(gains), whole(routers), each(middle), whole(small),
        ],
        out_specs=[each(shapes[0]), whole(shapes[1])],
        out_shape=shapes,
        compiler_params=params(),
        name="input_back",
    )(part, other, logit, logit_other, gate, slots, tokens, gains, routers, middle, small)


def heavy_weights_kernel(tile, core_ref, here_ref, there_ref, in_ref, out_ref, *refs):
    din_ref, dout_ref, rows_ref, grad_ref, hidden_ref, gate_ref, up_ref, sems = refs[-8:]

    starts = range(0, rows_ref.shape[0], tile)
    first = pl.program_id(0) == 0

    def copies(rows_from, grad_from, index):
        part = pl.ds(index * tile, tile)
        return [
            pltpu.make_async_copy(rows_from.at[part, :], rows_ref.at[part, :], sems.at[0, index]),
            pltpu.make_async_copy(grad_from.at[part, :], grad_ref.at[part, :], sems.at[1, index]),
        ]

    def fetch(rows_from, grad_from):
        for index in range(len(starts)):
            for copy in copies(rows_from, grad_from, index):
                copy.start()

    @pl.when(first & (core_ref[0, 0] == 0))
    def _():
        fetch(here_ref, there_ref)

    @pl.when(first & (core_ref[0, 0] != 0))
    def _():
        fetch(there_ref, here_ref)

    for index, start in enumerate(starts):

        @pl.when(first)
        def _():
            for copy in copies(here_ref, there_ref, index):
                copy.wait()

        part = pl.ds(start, tile)
        rows = rows_ref[part, :]
        hidden, gate_grad, up_grad = gelu_parts(
            dot(rows, in_ref[0]), dot(rows, in_ref[1]), dot(grad_ref[part, :], out_ref[...])
        )
        hidden_ref[part, :] = hidden.astype(LOW)
        gate_ref[part, :] = gate_grad.astype(LOW)
        up_ref[part, :] = up_grad.astype(LOW)
    dout_ref[...] = cols_dot(grad_ref[...], hidden_ref[...])
    din_ref[:, 0, :] = cols_dot(rows_ref[...], gate_ref[...])
    din_ref[:, 1, :] = cols_dot(rows_ref[...], up_ref[...])


def heavy_weights(core, here, there, weight_in, weight_out, piece, pieces, done):
    count, width = here.shape
    hidden = weight_out.shape[1]
    cols = 256
    tile = 512 if count % 512 == 0 else count
    steps = hidden // cols // pieces
    out_block = pl.BlockSpec((width, cols), lambda i: (0, piece * steps + i))
    in_block = pl.BlockSpec((width, 2, cols), lambda i: (0, 0, piece * steps + i))
    return pl.pallas_call(
        lambda *refs: heavy_weights_kernel(tile, *refs),
        grid=(steps,),
        in_specs=[
            pl.BlockSpec(memory_space=pltpu.SMEM),
            pl.BlockSpec(memory_space=pl.ANY),
            pl.BlockSpec(memory_space=pl.ANY),
            pl.BlockSpec((2, width, cols), lambda i: (0, 0, piece * steps + i)),
            out_block,
        ]
        + [pl.BlockSpec(memory_space=pl.ANY)] * len(done),
        out_specs=[in_block, out_block],
        out_shape=[like((width, 2, hidden), WIDE), like((width, hidden), WIDE)],
        scratch_shapes=[pltpu.VMEM((count, width), LOW)] * 2
        + [pltpu.VMEM((count, cols), LOW)] * 3
        + [pltpu.SemaphoreType.DMA((2, count // tile))],
        input_output_aliases={5 + i: i for i in range(len(done))},
        compiler_params=params(60),
        cost_estimate=pl.CostEstimate(
            flops=12 * count * width * hidden // pieces, bytes_accessed=2**24, transcendentals=0
        ),
        name="heavy_weights",
    )(core, here, there, weight_in, weight_out, *done)


def bit_pairs(bit):
    return [(i, i ^ (1 << bit)) for i in range(lax.axis_size("seq"))]


def bit_here(bit):
    return (lax.axis_index("seq") >> bit) & 1


def scatter_stage(value, bit):
    halves = value.reshape(2, value.shape[0] // 2, value.shape[1])
    mine = bit_here(bit)
    sent = lax.dynamic_index_in_dim(halves, 1 - mine, 0, keepdims=False)
    kept = lax.dynamic_index_in_dim(halves, mine, 0, keepdims=False)
    got = lax.ppermute(sent, "seq", bit_pairs(bit))
    return (kept.astype(WIDE) + got.astype(WIDE)).astype(LOW)


def gather_stage(value, bit):
    got = lax.ppermute(value, "seq", bit_pairs(bit))
    return jnp.where(
        bit_here(bit) == 0,
        jnp.concatenate([value, got], axis=0),
        jnp.concatenate([got, value], axis=0),
    )


def stage_orders():
    bits = list(range((lax.axis_size("seq") - 1).bit_length()))
    return [
        bits,
        [bits[1], bits[0]] + bits[2:],
        [bits[2], bits[0], bits[1]] + bits[3:],
    ]


def scatter_all(parts, step):
    return [scatter_stage(p, order[step]) for p, order in zip(parts, stage_orders())]


def gather_all(parts, step):
    return [gather_stage(p, order[step]) for p, order in zip(parts, stage_orders())]


def after(value, *others):
    return lax.optimization_barrier((value,) + others)[0]


def widen_kernel(bit_ref, mine_ref, got_ref, out_ref):
    half = mine_ref.shape[0]

    @pl.when(bit_ref[0, 0] == 0)
    def _():
        out_ref[:half, :] = mine_ref[...].astype(WIDE)
        out_ref[half:, :] = got_ref[...].astype(WIDE)

    @pl.when(bit_ref[0, 0] != 0)
    def _():
        out_ref[:half, :] = got_ref[...].astype(WIDE)
        out_ref[half:, :] = mine_ref[...].astype(WIDE)


def widen(bit, mine, got):
    rows, cols = mine.shape
    half = pl.BlockSpec((rows, LANES), lambda i: (0, i))
    return pl.pallas_call(
        widen_kernel,
        grid=(cols // LANES,),
        in_specs=[pl.BlockSpec(memory_space=pltpu.SMEM), half, half],
        out_specs=pl.BlockSpec((2 * rows, LANES), lambda i: (0, i)),
        out_shape=like((2 * rows, cols), WIDE),
        compiler_params=params(24),
        name="widen",
    )(bit.astype(jnp.int32).reshape(1, 1), mine, got)


def split_kernel(sum_ref, in_ref, out_ref):
    width = out_ref.shape[0]
    in_ref[:, 0, :] = sum_ref[:width, :].astype(WIDE)
    in_ref[:, 1, :] = sum_ref[width : 2 * width, :].astype(WIDE)
    out_ref[...] = sum_ref[2 * width :, :].astype(WIDE)


def split_feed(total):
    rows, cols = total.shape
    width = rows // 3
    return pl.pallas_call(
        split_kernel,
        grid=(cols // LANES,),
        in_specs=[pl.BlockSpec((rows, LANES), lambda i: (0, i))],
        out_specs=[
            pl.BlockSpec((width, 2, LANES), lambda i: (0, 0, i)),
            pl.BlockSpec((width, LANES), lambda i: (0, i)),
        ],
        out_shape=[like((width, 2, cols), WIDE), like((width, cols), WIDE)],
        compiler_params=params(24),
        name="split_feed",
    )(total)


def other_core(value):
    return lax.ppermute(value, "mp", [(0, 1), (1, 0)])


def to_neighbours(first, last):
    peers = lax.axis_size("seq")
    up = [(i, i + 1) for i in range(peers - 1)]
    down = [(i + 1, i) for i in range(peers - 1)]
    return lax.ppermute(last, "seq", up), lax.ppermute(first, "seq", down)


def exchange(pairs):
    return lax.all_to_all(pairs, "seq", split_axis=0, concat_axis=0, tiled=True)


def by_kind(weights):
    return weights.transpose(1, 0, 2)


def shards(
    tokens,
    out_grad,
    gains,
    routers,
    light_query_key_value_weight,
    light_attention_output_weight,
    heavy_qkv,
    heavy_out,
    light_feedforward_input_weight,
    light_feedforward_output_weight,
    heavy_mlp_in,
    heavy_mlp_out,
    routed_queries,
    routed_keys,
    routed_mlp,
    block_counts,
):
    seq_count, local_len, width = tokens.shape
    seq_devices = lax.axis_size("seq")
    row_base = lax.axis_index("seq") * local_len
    capacity = routed_queries.shape[1]
    light_cols = light_query_key_value_weight.shape[2]
    gain_rows, router_rows = gains.T, routers.T
    slot_ids = jnp.arange(capacity, dtype=jnp.int32)[None, :, None]
    rows = jnp.stack([routed_queries, routed_keys, routed_mlp], axis=2) - row_base
    valid = (slot_ids < block_counts).astype(jnp.int32)
    slots = jnp.concatenate([rows, valid], axis=2)
    place = jnp.stack([row_base, jnp.int32(seq_devices * local_len)]).astype(jnp.int32)[None, :]
    core = lax.axis_index("mp").astype(jnp.int32).reshape(1, 1)
    light_weights = by_kind(light_query_key_value_weight)
    heavy_weights_qkv = by_kind(heavy_qkv)

    before, behind = to_neighbours(tokens[:, :WIN], tokens[:, local_len - WIN :])
    low, qkv, pairs, raw, gate = front(
        tokens, gain_rows, router_rows, slots, light_weights, heavy_weights_qkv, seq_devices
    )
    pair = exchange(after(pairs, before, behind)).reshape(seq_devices * capacity, -1)
    mix, attn, lse, query, window = light_forward(
        place, qkv, before, behind, gain_rows, light_weights, light_attention_output_weight
    )
    kept, pair_mix = heavy_forward(after(pair, attn))
    mix_pairs = exchange(pair_mix.reshape(seq_devices, capacity, LANES))
    light_in = by_kind(after(light_feedforward_input_weight, kept))
    heavy_in = by_kind(after(heavy_mlp_in, kept))
    own, heavy_mix = combine(after(mix_pairs, light_in, heavy_in), attn, heavy_out, slots, gate)
    other = other_core(own)
    low_two, rows, slot, ship, gate_two = mlp_slots(
        core, tokens, own, other, out_grad, gain_rows, router_rows, slots
    )
    all_slots = seq_count * capacity * seq_devices
    gather_heavy = 2 * all_slots * width < 4 * (heavy_mlp_in.size + heavy_mlp_out.size)
    here = lax.all_gather(ship, "seq", axis=1, tiled=True) if gather_heavy else ship
    part, feed_grads, mlp = feed(
        low_two, rows, slot, gate_two, out_grad, slots, light_in, light_feedforward_output_weight,
        heavy_in, heavy_mlp_out,
    )
    beyond, mlp_other = other_core(part), other_core(mlp)
    mixed, middle_grad, mix_grad, grad_pairs, out_grads, small, query_logit = middle_back(
        tokens, own, other, part, beyond, out_grad, gain_rows, router_rows, slots, gate, mlp,
        mlp_other, mix, heavy_mix, light_attention_output_weight, heavy_out, seq_devices,
    )
    feed_sum = lax.psum(feed_grads.reshape(3 * width, -1), "seq")
    pair_grad = exchange(grad_pairs).reshape(seq_devices * capacity, -1)
    local, early, late = light_backward(place, query, window, lse, mix_grad)
    lead, tail = to_neighbours(early, late)
    triple = heavy_backward(pair, kept, after(pair_grad, local))
    triple_pairs = exchange(after(triple, lead, tail).reshape(seq_devices, capacity, -1))
    light_grads, light_part = light_project(after(local, triple), lead, tail, low, light_weights)
    triple_pairs = after(triple_pairs, light_part)
    heavy_grads, low_part, logit = heavy_project(
        light_part, low, triple_pairs, heavy_weights_qkv, slots, gate, raw, query_logit
    )
    low_other, logit_other = other_core(low_part), other_core(logit)
    input_grad, small = input_back(
        low_part, low_other, logit, logit_other, gate, slots, tokens, gain_rows, router_rows,
        middle_grad, small,
    )
    small_rows = small.astype(LOW).reshape(-1, light_cols)
    small_rows = jnp.pad(small_rows, ((0, 256 - small_rows.shape[0]), (0, 0)))
    parts = [
        light_grads.reshape(-1, light_cols),
        heavy_grads.reshape(-1, light_cols),
        jnp.concatenate([out_grads.reshape(-1, light_cols), small_rows]),
    ]
    here = after(here, light_part)
    there = other_core(here).reshape(-1, width)
    here = here.reshape(-1, width)
    steps = len(stage_orders()[0])
    pieces = 4
    heavy_sums = []

    def heavy_piece(parts, piece):
        heavy_sums[:] = heavy_weights(
            core, after(here, *parts), there, heavy_in, heavy_mlp_out, piece, pieces, heavy_sums
        )

    def joined(parts):
        kept_all = lax.optimization_barrier(tuple(parts) + tuple(heavy_sums))
        heavy_sums[:] = kept_all[len(parts) :]
        return list(kept_all[: len(parts)])

    for step in range(steps):
        started = parts
        parts = scatter_all(parts, step)
        if step < 2:
            heavy_piece(started if step else [input_grad], step)
            parts = joined(parts)
    for step in reversed(range(1, steps)):
        started = parts
        parts = gather_all(parts, step)
        if step == 1:
            heavy_piece(started, 2)
            parts = joined(parts)
    halves = [
        (p, lax.ppermute(p, "seq", bit_pairs(order[0]))) for p, order in zip(parts, stage_orders())
    ]
    heavy_piece(parts, 3)
    halves = [tuple(joined(pair)) for pair in halves]
    heavy_in_grad, heavy_out_grad = heavy_sums
    if not gather_heavy:
        sums = [heavy_in_grad[:, 0], heavy_in_grad[:, 1], heavy_out_grad]
        sums = [p.astype(LOW) for p in sums]
        for step in range(steps):
            sums = scatter_all(sums, step)
        for step in reversed(range(steps)):
            sums = gather_all(sums, step)
        heavy_in_grad = jnp.stack(sums[:2], axis=1).astype(WIDE)
        heavy_out_grad = sums[2].astype(WIDE)
    light_sum, heavy_sum, rest = [
        widen(bit_here(order[0]), *pair) for pair, order in zip(halves, stage_orders())
    ]
    feed_in, feed_out = split_feed(after(feed_sum, light_sum, heavy_sum, rest))
    small_sum = rest[2 * width : 2 * width + 8 * width // light_cols].reshape(8, width)
    return (
        mixed,
        input_grad,
        light_sum.reshape(3, width, light_cols).transpose(1, 0, 2),
        rest[:width],
        heavy_sum.reshape(3, width, light_cols).transpose(1, 0, 2),
        rest[width : 2 * width],
        feed_in,
        feed_out,
        heavy_in_grad,
        heavy_out_grad,
        jnp.stack([small_sum[2], small_sum[0]], axis=1),
        jnp.stack([small_sum[3], small_sum[4], small_sum[1]], axis=1),
    )


def solution(mesh):
    rows = P(None, "seq", None)
    by_column = P(None, None, "mp")
    by_hidden = P(None, "mp")
    slots = P(None, "seq")
    weights = (by_column, by_hidden) * 4
    return jax.shard_map(
        shards,
        mesh=mesh,
        in_specs=(rows, rows, P(), P()) + weights + (slots, slots, slots, rows),
        out_specs=(rows, rows) + weights + (P(), P()),
        check_vma=False,
    )
```

time: 2390 us -> 480 us (0.20)
  waiting for transfers between devices: 1470 us -> 114 us
  blocking collectives: 365 us -> 26.9 us
  Pallas kernels: 0 us -> 231 us
  other arithmetic: 213 us -> 8.59 us
  local copies, waits for them, and re-layouts: 169 us -> 25.9 us
  matrix products: 129 us -> 0 us
  starting transfers between devices: 17.2 us -> 50.5 us
    reduce_scatter x8 -> x0, waiting for transfers between devices: 1000 us -> none  [the longest x1 208 us: shards(): lax.psum_scatter(heavy_mlp_in_grad, 'seq', scatter_dimension=0, tiled=True)]
    all_gather x8 -> x0, blocking collectives: 360 us -> none  [the longest x1 65.8 us: shards(): lax.all_gather(heavy_delta, 'seq', axis=2, tiled=True)]
    all_gather x9 -> x1, waiting for transfers between devices: 306 us -> 0.01 us  [shards(): lax.all_gather(ship, 'seq', axis=1, tiled=True)]
    pallas_call x0 -> x20, Pallas kernels: none -> 231 us  [the longest x4 99.1 us: heavy_weights(): pl.pallas_call(lambda *refs: heavy_weights_kernel(tile, *refs), grid=(ste...]
    unnamed x24 -> x2, waiting for transfers between devices: 162 us -> 0.03 us
    dot_general x46 -> x0, matrix products: 129 us -> none  [the longest x2 8.66 us: heavy_scores(): jnp.einsum('sqhd,skhd->shqk', queries, key_heads, preferred_element_type=...]
    scatter-add x10 -> x0, other arithmetic: 124 us -> none  [the longest x8 121 us: add_rows(): return target.at[seq_ids, where_rows].add(values)]
    ppermute x4 -> x34, waiting for transfers between devices: 0.01 us -> 108 us  [the longest x12 51.8 us: scatter_stage(): got = lax.ppermute(sent, 'seq', bit_pairs(bit))]
  transfers between devices with their start and end apart: 26 -> 39, of which waited for: 17 -> 21; matrix products, arithmetic and copies ran while one was open for 14% -> 5% of each run, Pallas kernels for 0% -> 45%
where the time goes in v2:
time: 480 us; the launch traced here: 471 us
  Pallas kernels  231 us (48%)
  waiting for transfers between devices  114 us (24%)
  starting transfers between devices  50.5 us (11%)
  blocking collectives  26.9 us (6%)
  local copies, waits for them, and re-layouts  25.9 us (5%)
  between operations  15.1 us (3%)
  other arithmetic  8.59 us (2%)
    pallas_call x4, Pallas kernels, heavy_weights(): pl.pallas_call(lambda *refs: heavy_weights_kernel(tile, *refs), grid=(ste...  99.1 us
    ppermute x12, waiting for transfers between devices, scatter_stage(): got = lax.ppermute(sent, 'seq', bit_pairs(bit))  51.8 us
    ppermute x9, waiting for transfers between devices, gather_stage(): got = lax.ppermute(value, 'seq', bit_pairs(bit))  29.7 us
    all_to_all x1, blocking collectives, exchange(): return lax.all_to_all(pairs, 'seq', split_axis=0, concat_axis=0, tiled=True)  26.9 us
    pallas_call x1, Pallas kernels, feed(): pl.pallas_call(feed_kernel, grid=(heavy_out.shape[1] // cols,), in_specs=...  20.6 us
    ppermute x4, waiting for transfers between devices, to_neighbours(): return (lax.ppermute(last, 'seq', up), lax.ppermute(first, 'seq', down))  18.8 us
    all_to_all x3, starting transfers between devices, exchange(): return lax.all_to_all(pairs, 'seq', split_axis=0, concat_axis=0, tiled=True)  16.4 us
    pallas_call x1, Pallas kernels, light_forward(): pl.pallas_call(lambda *refs: light_forward_kernel(1.0 / math.sqrt(LHD), *...  15.1 us
  transfers between devices with their start and end apart: 39, of which 21 were waited for; matrix products, arithmetic and copies ran while one was open for 5% of the time, Pallas kernels for 45%

profile of v2, /device:TPU:0, one launch (start us, length us, event | category | flops | bytes accessed | tf_op | source)
XLA Modules:
  0.0 471.2 jit_solution(9295795010079501206)
XLA Ops:
  8.4 4.9 %collective-permute-start = (bf16[2,128,768]{2,1,0:T(8,128)(2,1)S(1)}, bf16[2,128,768]{2,1,0:T(8,128)(2,1)S(1)}, u32[]{:S(2)}, u32[]{:S(2)}) collective-permute-start(bf16[2,128,768]{2,1,0:T(8,128)(2,1)S(1)} %get-tuple-element.202), channel_id=1, source_target_pairs={{0,2},{2,4},{4,6},{6,8},{8,10},{10,12},{12,14},{14,16},{16,18},{18... | collective-permute-start | bytes 1179656 | tf_op jit(solution)/shard_map/ppermute | solution.py:1065
  16.9 8.1 %front.1 = (bf16[2,384,768]{2,1,0:T(8,128)(2,1)}, bf16[2,3,384,384]{3,2,1,0:T(8,128)(2,1)}, bf16[16,96,256]{2,1,0:T(8,128)(2,1)}, f32[2,96,384]{2,1,0:T(8,128)}, f32[2,96,128]{2,1,0:T(8,128)}) custom-call(bf16[2,384,768]{2,1,0:T(8,128)(2,1)} %tokens_ref.7, f32[2,768]{1,0:T(2,128)} %bitcast.184, f32[3,768]{1,0:T(4,128)} %bitcast.180, ...), custom_call_target="tpu_custom_call" | custom-call | tf_op jit(solution)/shard_map/front/pallas_call | solution.py:205
  24.9 5.0 %collective-permute-done.refs_2_ = bf16[2,128,768]{2,1,0:T(8,128)(2,1)S(1)} collective-permute-done((bf16[2,128,768]{2,1,0:T(8,128)(2,1)S(1)}, bf16[2,128,768]{2,1,0:T(8,128)(2,1)S(1)}, u32[]{:S(2)}, u32[]{:S(2)}) %collective-permute-start) | collective-permute-done | bytes 393248 | tf_op jit(solution)/shard_map/ppermute | solution.py:1065
  30.0 1.9 collective-permute-done.1.refs_3_
  31.9 5.9 %all-to-all-start = ((bf16[16,96,256]{2,1,0:T(8,128)(2,1)}), bf16[16,96,256]{2,1,0:T(8,128)(2,1)S(1)}, u32[]{:S(2)}, u32[]{:S(2)}) async-start(bf16[16,96,256]{2,1,0:T(8,128)(2,1)} %get-tuple-element.104), calls=%async_computation | async-start | bytes 1572864 | tf_op jit(solution)/shard_map/all_to_all | solution.py:1069
  38.4 15.1 %light_forward.1 = (bf16[2,384,384]{2,1,0:T(8,128)(2,1)}, f32[2,384,768]{2,1,0:T(8,128)}, f32[2,384,128]{2,1,0:T(8,128)}, bf16[2,384,512]{2,1,0:T(8,128)(2,1)}, bf16[2,2,640,512]{3,2,1,0:T(8,128)(2,1)}) custom-call(s32[1,2]{1,0:T(1,128)} %add_bitcast_fusion.refs_0_, bf16[2,3,384,384]{3,2,1,0:T(8,128)(2,1)} %get-tuple-element.105.refs_1_, ...), custom_call_target="tpu_custom_call" | custom-call | tf_op jit(solution)/shard_map/light_forward/pallas_call | solution.py:271
  53.5 4.1 all-to-all-done
  58.6 7.3 %heavy_forward.1 = (f32[1536,128]{1,0:T(8,128)}, bf16[1536,128]{1,0:T(8,128)(2,1)}) custom-call(bf16[1536,256]{1,0:T(8,128)(2,1)} %bitcast.144), custom_call_target="tpu_custom_call" | custom-call | tf_op jit(solution)/shard_map/heavy_forward/pallas_call | solution.py:427
  65.9 4.9 %all-to-all-start.1 = ((bf16[16,96,128]{2,1,0:T(8,128)(2,1)}), bf16[16,96,128]{2,1,0:T(8,128)(2,1)S(1)}, u32[]{:S(2)}, u32[]{:S(2)}) async-start(bf16[16,96,128]{2,1,0:T(8,128)(2,1)} %bitcast.177), calls=%async_computation.1 | async-start | bytes 786432 | tf_op jit(solution)/shard_map/all_to_all | solution.py:1069
  70.9 8.4 %copy.58 = bf16[768,2,2048]{2,0,1:T(8,128)(2,1)} copy(bf16[768,2,2048]{2,1,0:T(2,128)(2,1)} %param.26) | data formatting | bytes 12582912 | tf_op jit(solution)/shard_map/optimization_barrier | solution.py:1002
  83.0 4.5 combine.1
  87.6 3.0 collective-permute-done.2.other_ref
  91.6 4.8 %mlp_slots.1 = (bf16[2,384,768]{2,1,0:T(8,128)(2,1)}, bf16[2,96,768]{2,1,0:T(8,128)(2,1)}, bf16[2,96,768]{2,1,0:T(8,128)(2,1)}, bf16[2,96,768]{2,1,0:T(8,128)(2,1)}, f32[2,96,128]{2,1,0:T(8,128)}) custom-call(s32[1,1]{1,0:T(1,128)} %bitcast.14.core_ref.refs_0_, bf16[2,384,768]{2,1,0:T(8,128)(2,1)} %tokens_ref.7, ...), custom_call_target="tpu_custom_call" | custom-call | tf_op jit(solution)/shard_map/mlp_slots/pallas_call | solution.py:522
  96.4 20.6 %feed.1 = (bf16[2,2,384,768]{3,2,1,0:T(8,128)(2,1)}, bf16[3,768,512]{2,1,0:T(8,128)(2,1)}, f32[2,96,128]{2,1,0:T(8,128)}) custom-call(bf16[2,384,768]{2,1,0:T(8,128)(2,1)} %get-tuple-element.115.low_ref, bf16[192,768]{1,0:T(8,128)(2,1)} %bitcast.178, bf16[192,768]{1,0:T(8,128)(2,1)} %bitcast.179, f32[2,96,128]{2,1,0:T(8,128)} %get-tuple-element.118.kept_ref, ...), custom_call_target="tpu_custom_call" | custom-call | tf_op jit(solution)/shard_map/feed/pallas_call | solution.py:605
  117.5 4.4 collective-permute-done.4.mlp_other_ref
  123.4 11.4 %middle_back.1 = (bf16[2,384,768]{2,1,0:T(8,128)(2,1)}, f32[2,384,768]{2,1,0:T(8,128)}, bf16[2,384,384]{2,1,0:T(8,128)(2,1)}, bf16[16,96,128]{2,1,0:T(8,128)(2,1...) custom-call(bf16[2,384,768]{2,1,0:T(8,128)(2,1)} %tokens_ref.7, ...), custom_call_target="tpu_custom_call" | custom-call | tf_op jit(solution)/shard_map/middle_back/pallas_call | solution.py:707
  134.8 5.6 %all-to-all-start.2 = ((bf16[16,96,128]{2,1,0:T(8,128)(2,1)}), bf16[16,96,128]{2,1,0:T(8,128)(2,1)S(1)}, u32[]{:S(2)}, u32[]{:S(2)}) async-start(bf16[16,96,128]{2,1,0:T(8,128)(2,1)} %get-tuple-element.129), calls=%async_computation.2 | async-start | bytes 786432 | tf_op jit(solution)/shard_map/all_to_all | solution.py:1069
  140.5 14.3 %light_backward.1 = (bf16[2,3,384,384]{3,2,1,0:T(8,128)(2,1)}, bf16[2,2,128,384]{3,2,1,0:T(8,128)(2,1)}, bf16[2,2,128,384]{3,2,1,0:T(8,128)(2,1)}) custom-call(s32[1,2]{1,0:T(1,128)} %add_bitcast_fusion.refs_0_, bf16[2,384,512]{2,1,0:T(8,128)(2,1)} %get-tuple-element.124.refs_1_, bf16[2,2,640,512]{3,2,1,0:T(8,128)(2,1)} %get-tuple-element.125.refs_2_, ...), custom_call_target="tpu_custom_call" | custom-call | tf_op jit(solution)/shard_map/light_backward/pallas_call | solution.py:330
  154.8 3.9 collective-permute-start.5
  160.7 10.8 %heavy_backward.1 = bf16[1536,256]{1,0:T(8,128)(2,1)} custom-call(bf16[1536,256]{1,0:T(8,128)(2,1)} %bitcast.145, f32[1536,128]{1,0:T(8,128)} %get-tuple-element.109.refs_1_, bf16[1536,128]{1,0:T(8,128)(2,1)} %bitcast.167), custom_call_target="tpu_custom_call" | custom-call | tf_op jit(solution)/shard_map/heavy_backward/pallas_call | solution.py:443
  171.5 9.9 %collective-permute-done.5.lead_ref = bf16[2,2,128,384]{3,2,1,0:T(8,128)(2,1)S(1)} collective-permute-done((bf16[2,2,128,384]{3,2,1,0:T(8,128)(2,1)}, bf16[2,2,128,384]{3,2,1,0:T(8,128)(2,1)S(1)}, u32[]{:S(2)}, u32[]{:S(2)}) %collective-permute-start.5) | collective-permute-done | bytes 393248 | tf_op jit(solution)/shard_map/ppermute | solution.py:1065
  181.3 2.0 collective-permute-done.6.tail_ref
  184.1 8.7 %light_project.1 = (bf16[3,768,384]{2,1,0:T(8,128)(2,1)}, f32[2,384,768]{2,1,0:T(8,128)}) custom-call(bf16[2,3,384,384]{3,2,1,0:T(8,128)(2,1)} %get-tuple-element.131.local_ref, bf16[2,2,128,384]{3,2,1,0:T(8,128)(2,1)} %copy-done.14, bf16[2,2,128,384]{3,2,1,0:T(8,128)(2,1)} %copy-done.15, bf16[2,384,768]{2,1,0:T(8,128)(2,1)} %get-tuple-element.134.low_ref, ...), custom_call_target="tpu_custom_call" | custom-call | tf_op jit(solution)/shard_map/light_project/pallas_call | solution.py:757
  192.8 26.9 %all_to_all.20.pairs_ref = bf16[16,96,256]{2,1,0:T(8,128)(2,1)} all-to-all(bf16[16,96,256]{2,1,0:T(8,128)(2,1)S(1)} %bitcast.155), channel_id=1, replica_groups=mesh['seq'=16,'mp'=2] {'seq'}, dimensions={0} | all-to-all | bytes 1572864 | tf_op jit(solution)/shard_map/all_to_all | solution.py:1069
  219.7 8.7 %heavy_project.1 = (bf16[3,768,384]{2,1,0:T(8,128)(2,1)}, bf16[2,384,768]{2,1,0:T(8,128)(2,1)}, f32[2,96,128]{2,1,0:T(8,128)}) custom-call(f32[2,384,768]{2,1,0:T(8,128)} %get-tuple-element.135.light_part_ref, bf16[2,384,768]{2,1,0:T(8,128)(2,1)} %get-tuple-element.134.low_ref, bf16[16,96,256]{2,1,0:T(8,128)(2,1)} %all_to_all.20.pairs_ref, ...), custom_call_target="tpu_custom_call" | custom-call | tf_op jit(solution)/shard_map/heavy_project/pallas_call | solution.py:812
  232.8 6.9 %input_back.1 = (f32[2,384,768]{2,1,0:T(8,128)}, f32[8,768]{1,0:T(8,128)}) custom-call(bf16[2,384,768]{2,1,0:T(8,128)(2,1)} %get-tuple-element.140.part_ref, bf16[2,384,768]{2,1,0:T(8,128)(2,1)} %collective-permute-done.7.other_ref, f32[2,96,128]{2,1,0:T(8,128)} %get-tuple-element.141.logit_ref, f32[2,96,128]{2,1,0:T(8,128)} %copy-done.17, ...), custom_call_target="tpu_custom_call" | custom-call | tf_op jit(solution)/shard_map/input_back/pallas_call | solution.py:865
  241.1 17.1 %collective-permute-done.9 = bf16[1152,384]{1,0:T(8,128)(2,1)} collective-permute-done((bf16[1152,384]{1,0:T(8,128)(2,1)}, bf16[1152,384]{1,0:T(8,128)(2,1)}, u32[]{:S(2)}, u32[]{:S(2)}) %collective-permute-start.9) | collective-permute-done | bytes 884768 | tf_op jit(solution)/shard_map/ppermute | solution.py:971
  261.4 8.9 %collective-permute-done.11 = bf16[896,384]{1,0:T(8,128)(2,1)S(1)} collective-permute-done((bf16[896,384]{1,0:T(8,128)(2,1)S(1)}, bf16[896,384]{1,0:T(8,128)(2,1)S(1)}, u32[]{:S(2)}, u32[]{:S(2)}) %collective-permute-start.11) | collective-permute-done | bytes 688160 | tf_op jit(solution)/shard_map/ppermute | solution.py:971
  270.5 24.9 %heavy_weights.4 = (f32[768,2,2048]{2,1,0:T(2,128)}, f32[768,2048]{1,0:T(8,128)}) custom-call(s32[1,1]{1,0:T(1,128)} %bitcast.14.core_ref.refs_0_, bf16[3072,768]{1,0:T(8,128)(2,1)} %bitcast.198, bf16[3072,768]{1,0:T(8,128)(2,1)} %bitcast.31.refs_2_, bf16[2,768,2048]{2,1,0:T(8,128)(2,1)} %bitcast.135, bf16[768,2048]{1,0:T(8,128)(2,1)} %refs_4_.7), custom_call_target="tpu_custom_call" | custom-call | flops 14495514624 | bytes 16777216 | tf_op jit(solution)/shard_map/heavy_weights/pallas_call | solution.py:933
  300.6 24.7 %heavy_weights.5 = (f32[768,2,2048]{2,1,0:T(2,128)}, f32[768,2048]{1,0:T(8,128)}) custom-call(s32[1,1]{1,0:T(1,128)} %bitcast.14.core_ref.refs_0_, bf16[3072,768]{1,0:T(8,128)(2,1)} %bitcast.199, bf16[3072,768]{1,0:T(8,128)(2,1)} %bitcast.31.refs_2_, bf16[2,768,2048]{2,1,0:T(8,128)(2,1)} %bitcast.136, ...), custom_call_target="tpu_custom_call", output_to_operand_aliasing={{0}: (5, {}), {1}: (6, {})} | custom-call | flops 14495514624 | bytes 16777216 | tf_op jit(solution)/shard_map/heavy_weights/pallas_call | solution.py:933
  326.9 1.8 collective-permute-start.16
  328.6 2.6 collective-permute-done.26
  331.3 2.3 collective-permute-start.27
  333.6 6.1 %collective-permute-done.21 = bf16[288,384]{1,0:T(8,128)(2,1)S(1)} collective-permute-done((bf16[288,384]{1,0:T(8,128)(2,1)S(1)}, bf16[288,384]{1,0:T(8,128)(2,1)S(1)}, u32[]{:S(2)}, u32[]{:S(2)}) %collective-permute-start.21) | collective-permute-done | bytes 221216 | tf_op jit(solution)/shard_map/ppermute | solution.py:971
  339.9 4.6 collective-permute-done.16
  347.7 7.5 %collective-permute-done.22 = bf16[144,384]{1,0:T(8,128)(2,1)S(1)} collective-permute-done((bf16[144,384]{1,0:T(8,128)(2,1)S(1)}, bf16[144,384]{1,0:T(8,128)(2,1)S(1)}, u32[]{:S(2)}, u32[]{:S(2)}) %collective-permute-start.22) | collective-permute-done | bytes 110624 | tf_op jit(solution)/shard_map/ppermute | solution.py:971
  355.3 4.6 collective-permute-done.17
  360.0 3.0 collective-permute-done.28
  363.1 1.7 collective-permute-start.29
  364.8 5.3 %collective-permute-done.23 = bf16[144,384]{1,0:T(8,128)(2,1)S(1)} collective-permute-done((bf16[144,384]{1,0:T(8,128)(2,1)S(1)}, bf16[144,384]{1,0:T(8,128)(2,1)S(1)}, u32[]{:S(2)}, u32[]{:S(2)}) %collective-permute-start.23) | collective-permute-done | bytes 110624 | tf_op jit(solution)/shard_map/ppermute | solution.py:976
  370.2 5.0 %collective-permute-done.18 = bf16[144,384]{1,0:T(8,128)(2,1)S(1)} collective-permute-done((bf16[144,384]{1,0:T(8,128)(2,1)S(1)}, bf16[144,384]{1,0:T(8,128)(2,1)S(1)}, u32[]{:S(2)}, u32[]{:S(2)}) %collective-permute-start.18) | collective-permute-done | bytes 110624 | tf_op jit(solution)/shard_map/ppermute | solution.py:976
  376.9 12.1 %collective-permute-done.24 = bf16[288,384]{1,0:T(8,128)(2,1)S(1)} collective-permute-done((bf16[288,384]{1,0:T(8,128)(2,1)S(1)}, bf16[288,384]{1,0:T(8,128)(2,1)S(1)}, u32[]{:S(2)}, u32[]{:S(2)}) %collective-permute-start.24) | collective-permute-done | bytes 221216 | tf_op jit(solution)/shard_map/ppermute | solution.py:976
  390.4 4.3 collective-permute-done.19
  396.4 24.7 %heavy_weights.6 = (f32[768,2,2048]{2,1,0:T(2,128)}, f32[768,2048]{1,0:T(8,128)}) custom-call(s32[1,1]{1,0:T(1,128)} %bitcast.14.core_ref.refs_0_, bf16[3072,768]{1,0:T(8,128)(2,1)} %bitcast.200, bf16[3072,768]{1,0:T(8,128)(2,1)} %bitcast.31.refs_2_, bf16[2,768,2048]{2,1,0:T(8,128)(2,1)} %bitcast.137, ...), custom_call_target="tpu_custom_call", output_to_operand_aliasing={{0}: (5, {}), {1}: (6, {})} | custom-call | flops 14495514624 | bytes 16777216 | tf_op jit(solution)/shard_map/heavy_weights/pallas_call | solution.py:933
  424.3 24.8 %heavy_weights.7 = (f32[768,2,2048]{2,1,0:T(2,128)}, f32[768,2048]{1,0:T(8,128)}) custom-call(s32[1,1]{1,0:T(1,128)} %bitcast.14.core_ref.refs_0_, bf16[3072,768]{1,0:T(8,128)(2,1)} %bitcast.201, bf16[3072,768]{1,0:T(8,128)(2,1)} %bitcast.31.refs_2_, bf16[2,768,2048]{2,1,0:T(8,128)(2,1)} %bitcast.138, ...), custom_call_target="tpu_custom_call", output_to_operand_aliasing={{0}: (5, {}), {1}: (6, {})} | custom-call | flops 14495514624 | bytes 16777216 | tf_op jit(solution)/shard_map/heavy_weights/pallas_call | solution.py:933
  449.9 3.5 widen.5
  453.4 2.4 widen.3
  459.0 3.7 split_feed.1
  (143 shorter events, 48.5 us)
Async XLA Ops:
  8.4 21.6 %collective-permute-start = (bf16[2,128,768]{2,1,0:T(8,128)(2,1)S(1)}, bf16[2,128,768]{2,1,0:T(8,128)(2,1)S(1)}, u32[]{:S(2)}, u32[]{:S(2)}) collective-permute-start(bf16[2,128,768]{2,1,0:T(8,128)(2,1)S(1)} %get-tuple-element.202), channel_id=1, source_target_pairs={{0,2},{2,4},{4,6},{6,8},{8,10},{10,12},{12,14},{14,16},{16,18},{18... | collective-permute-start | bytes 1179656 | tf_op jit(solution)/shard_map/ppermute | solution.py:1065
  13.2 18.7 %collective-permute-start.1 = (bf16[2,128,768]{2,1,0:T(8,128)(2,1)S(1)}, bf16[2,128,768]{2,1,0:T(8,128)(2,1)S(1)}, u32[]{:S(2)}, u32[]{:S(2)}) collective-permute-start(bf16[2,128,768]{2,1,0:T(8,128)(2,1)S(1)} %get-tuple-element.201), channel_id=1, source_target_pairs={{2,0},{4,2},{6,4},{8,6},{10,8},{12,10},{14,12},{16,14},{18,16},{20... | collective-permute-start | bytes 1179656 | tf_op jit(solution)/shard_map/ppermute | solution.py:1065
  30.0 8.5 %copy-start.12 = (bf16[2,128,768]{2,1,0:T(8,128)(2,1)}, bf16[2,128,768]{2,1,0:T(8,128)(2,1)S(1)}, u32[]{:S(2)}) copy-start(bf16[2,128,768]{2,1,0:T(8,128)(2,1)S(1)} %collective-permute-done.refs_2_) | copy-start | bytes 1179652
  31.9 6.5 %copy-start.13 = (bf16[2,128,768]{2,1,0:T(8,128)(2,1)}, bf16[2,128,768]{2,1,0:T(8,128)(2,1)S(1)}, u32[]{:S(2)}) copy-start(bf16[2,128,768]{2,1,0:T(8,128)(2,1)S(1)} %collective-permute-done.1.refs_3_) | copy-start | bytes 1179652
  31.9 25.8 %all-to-all-start = ((bf16[16,96,256]{2,1,0:T(8,128)(2,1)}), bf16[16,96,256]{2,1,0:T(8,128)(2,1)S(1)}, u32[]{:S(2)}, u32[]{:S(2)}) async-start(bf16[16,96,256]{2,1,0:T(8,128)(2,1)} %get-tuple-element.104), calls=%async_computation | async-start | bytes 1572864 | tf_op jit(solution)/shard_map/all_to_all | solution.py:1069
  65.9 16.4 %all-to-all-start.1 = ((bf16[16,96,128]{2,1,0:T(8,128)(2,1)}), bf16[16,96,128]{2,1,0:T(8,128)(2,1)S(1)}, u32[]{:S(2)}, u32[]{:S(2)}) async-start(bf16[16,96,128]{2,1,0:T(8,128)(2,1)} %bitcast.177), calls=%async_computation.1 | async-start | bytes 786432 | tf_op jit(solution)/shard_map/all_to_all | solution.py:1069
  70.8 122.0 %all-gather.2.cloned.1.call-start = ((), (), s32[]{:S(2)}) async-start(), calls=%async_computation.4 | async-start | bytes 5013504 | tf_op jit(solution)/shard_map/all_gather | solution.py:1128
  70.9 8.4 %copy-start.8 = (bf16[768,2,512]{2,1,0:T(2,128)(2,1)S(1)}, bf16[768,2,512]{2,1,0:T(2,128)(2,1)}, u32[]{:S(2)}) copy-start(bf16[768,2,512]{2,1,0:T(2,128)(2,1)} %param.24) | copy-start | bytes 4718596
  87.5 3.1 collective-permute-start.2
  117.0 4.9 %collective-permute-start.3 = (bf16[2,2,384,768]{3,2,1,0:T(8,128)(2,1)}, bf16[2,2,384,768]{3,2,1,0:T(8,128)(2,1)S(1)}, u32[]{:S(2)}, u32[]{:S(2)}) collective-permute-start(bf16[2,2,384,768]{3,2,1,0:T(8,128)(2,1)} %get-tuple-element.119.part_ref), channel_id=1, source_target_pairs={{0,1},{1,0},{2,3},{3,2},{4,5},{5,4},{6,7},{7,6},{8,9},{9,8},{10,11... | collective-permute-start | bytes 7077896 | tf_op jit(solution)/shard_map/ppermute | solution.py:1058
  117.2 4.7 %collective-permute-start.4 = (f32[2,96,128]{2,1,0:T(8,128)}, f32[2,96,128]{2,1,0:T(8,128)S(1)}, u32[]{:S(2)}, u32[]{:S(2)}) collective-permute-start(f32[2,96,128]{2,1,0:T(8,128)} %get-tuple-element.120.mlp_ref), channel_id=1, source_target_pairs={{0,1},{1,0},{2,3},{3,2},{4,5},{5,4},{6,7},{7,6},{8,9},{9,8},{10,11... | collective-permute-start | bytes 294920 | tf_op jit(solution)/shard_map/ppermute | solution.py:1058
  134.8 25.1 %all-to-all-start.2 = ((bf16[16,96,128]{2,1,0:T(8,128)(2,1)}), bf16[16,96,128]{2,1,0:T(8,128)(2,1)S(1)}, u32[]{:S(2)}, u32[]{:S(2)}) async-start(bf16[16,96,128]{2,1,0:T(8,128)(2,1)} %get-tuple-element.129), calls=%async_computation.2 | async-start | bytes 786432 | tf_op jit(solution)/shard_map/all_to_all | solution.py:1069
  140.4 316.9 %all-reduce.3.cloned.1.call-start = ((), (), s32[]{:S(2)}) async-start(), calls=%async_computation.5 | async-start | bytes 4718592 | tf_op jit(solution)/shard_map/psum | solution.py:1138
  154.8 26.6 %collective-permute-start.5 = (bf16[2,2,128,384]{3,2,1,0:T(8,128)(2,1)}, bf16[2,2,128,384]{3,2,1,0:T(8,128)(2,1)S(1)}, u32[]{:S(2)}, u32[]{:S(2)}) collective-permute-start(bf16[2,2,128,384]{3,2,1,0:T(8,128)(2,1)} %get-tuple-element.132), channel_id=1, source_target_pairs={{0,2},{2,4},{4,6},{6,8},{8,10},{10,12},{12,14},{14,16},{16,18},{18... | collective-permute-start | bytes 1179656 | tf_op jit(solution)/shard_map/ppermute | solution.py:1065
  158.6 24.7 %collective-permute-start.6 = (bf16[2,2,128,384]{3,2,1,0:T(8,128)(2,1)}, bf16[2,2,128,384]{3,2,1,0:T(8,128)(2,1)S(1)}, u32[]{:S(2)}, u32[]{:S(2)}) collective-permute-start(bf16[2,2,128,384]{3,2,1,0:T(8,128)(2,1)} %get-tuple-element.133), channel_id=1, source_target_pairs={{2,0},{4,2},{6,4},{8,6},{10,8},{12,10},{14,12},{16,14},{18,16},{20... | collective-permute-start | bytes 1179656 | tf_op jit(solution)/shard_map/ppermute | solution.py:1065
  181.3 2.0 copy-start.14
  184.1 8.7 %copy-start.3 = (bf16[1536,256]{1,0:T(8,128)(2,1)S(1)}, bf16[1536,256]{1,0:T(8,128)(2,1)}, u32[]{:S(2)}) copy-start(bf16[1536,256]{1,0:T(8,128)(2,1)} %heavy_backward.1) | copy-start | bytes 2359300
  192.8 77.7 %collective-permute-start.12 = (bf16[2,1536,768]{2,1,0:T(8,128)(2,1)}, bf16[2,1536,768]{2,1,0:T(8,128)(2,1)}, u32[]{:S(2)}, u32[]{:S(2)}) collective-permute-start(bf16[2,1536,768]{2,1,0:T(8,128)(2,1)} %all-gather.2.cloned.1.call-done), channel_id=1, source_target_pairs={{0,1},{1,0},{2,3},{3,2},{4,5},{5,4},{6,7},{7,6},{8,9},{9,8},{10,11... | collective-permute-start | bytes 14155784 | tf_op jit(solution)/shard_map/ppermute | solution.py:1058
  219.7 8.8 %copy-start.5 = (bf16[3,768,384]{2,1,0:T(8,128)(2,1)S(1)}, bf16[3,768,384]{2,1,0:T(8,128)(2,1)}, u32[]{:S(2)}) copy-start(bf16[3,768,384]{2,1,0:T(8,128)(2,1)} %get-tuple-element.145) | copy-start | bytes 5308420
  228.4 3.7 collective-permute-start.7
  228.5 1.9 copy-start.6
  229.5 28.7 %collective-permute-start.9 = (bf16[1152,384]{1,0:T(8,128)(2,1)}, bf16[1152,384]{1,0:T(8,128)(2,1)}, u32[]{:S(2)}, u32[]{:S(2)}) collective-permute-start(bf16[1152,384]{1,0:T(8,128)(2,1)} %dynamic-slice_bitcast_fusion.1), channel_id=1, source_target_pairs={{0,2},{2,0},{4,6},{6,4},{8,10},{10,8},{12,14},{14,12},{16,18},{18,... | collective-permute-start | bytes 2654216 | tf_op jit(solution)/shard_map/ppermute | solution.py:971
  230.1 2.0 collective-permute-start.8
  231.4 28.6 %collective-permute-start.10 = (bf16[1152,384]{1,0:T(8,128)(2,1)}, bf16[1152,384]{1,0:T(8,128)(2,1)}, u32[]{:S(2)}, u32[]{:S(2)}) collective-permute-start(bf16[1152,384]{1,0:T(8,128)(2,1)} %dynamic-slice_bitcast_fusion), channel_id=1, source_target_pairs={{0,4},{2,6},{4,0},{6,2},{8,12},{10,14},{12,8},{14,10},{16,20},{18,... | collective-permute-start | bytes 2654216 | tf_op jit(solution)/shard_map/ppermute | solution.py:971
  232.8 7.7 %copy-start.11 = (bf16[2,768,384]{2,1,0:T(8,128)(2,1)S(1)}, bf16[2,768,384]{2,1,0:T(8,128)(2,1)}, u32[]{:S(2)}) copy-start(bf16[2,768,384]{2,1,0:T(8,128)(2,1)} %get-tuple-element.147) | copy-start | bytes 3538948
  240.6 19.4 %copy-start.7 = (bf16[3,768,384]{2,1,0:T(8,128)(2,1)S(1)}, bf16[3,768,384]{2,1,0:T(8,128)(2,1)}, u32[]{:S(2)}) copy-start(bf16[3,768,384]{2,1,0:T(8,128)(2,1)} %get-tuple-element.146) | copy-start | bytes 5308420
  240.7 29.7 %collective-permute-start.11 = (bf16[896,384]{1,0:T(8,128)(2,1)S(1)}, bf16[896,384]{1,0:T(8,128)(2,1)S(1)}, u32[]{:S(2)}, u32[]{:S(2)}) collective-permute-start(bf16[896,384]{1,0:T(8,128)(2,1)S(1)} %dynamic-slice_bitcast_fusion.2), channel_id=1, source_target_pairs={{0,8},{2,10},{4,12},{6,14},{8,0},{10,2},{12,4},{14,6},{16,24},{18,... | collective-permute-start | bytes 2064392 | tf_op jit(solution)/shard_map/ppermute | solution.py:971
  295.5 29.8 %collective-permute-start.15 = (bf16[448,384]{1,0:T(8,128)(2,1)S(1)}, bf16[448,384]{1,0:T(8,128)(2,1)S(1)}, u32[]{:S(2)}, u32[]{:S(2)}) collective-permute-start(bf16[448,384]{1,0:T(8,128)(2,1)S(1)} %dynamic-slice_bitcast_fusion.5), channel_id=1, source_target_pairs={{0,2},{2,0},{4,6},{6,4},{8,10},{10,8},{12,14},{14,12},{16,18},{18,... | collective-permute-start | bytes 1032200 | tf_op jit(solution)/shard_map/ppermute | solution.py:971
  297.8 27.7 %collective-permute-start.14 = (bf16[576,384]{1,0:T(8,128)(2,1)}, bf16[576,384]{1,0:T(8,128)(2,1)S(1)}, u32[]{:S(2)}, u32[]{:S(2)}) collective-permute-start(bf16[576,384]{1,0:T(8,128)(2,1)} %dynamic-slice_bitcast_fusion.3), channel_id=1, source_target_pairs={{0,2},{2,0},{4,6},{6,4},{8,10},{10,8},{12,14},{14,12},{16,18},{18,... | collective-permute-start | bytes 1327112 | tf_op jit(solution)/shard_map/ppermute | solution.py:971
  299.2 26.4 %collective-permute-start.13 = (bf16[576,384]{1,0:T(8,128)(2,1)}, bf16[576,384]{1,0:T(8,128)(2,1)S(1)}, u32[]{:S(2)}, u32[]{:S(2)}) collective-permute-start(bf16[576,384]{1,0:T(8,128)(2,1)} %dynamic-slice_bitcast_fusion.4), channel_id=1, source_target_pairs={{0,4},{2,6},{4,0},{6,2},{8,12},{10,14},{12,8},{14,10},{16,20},{18,... | collective-permute-start | bytes 1327112 | tf_op jit(solution)/shard_map/ppermute | solution.py:971
  325.8 5.5 %collective-permute-start.26 = (bf16[224,384]{1,0:T(8,128)(2,1)S(1)}, bf16[224,384]{1,0:T(8,128)(2,1)S(1)}, u32[]{:S(2)}, u32[]{:S(2)}) collective-permute-start(bf16[224,384]{1,0:T(8,128)(2,1)S(1)} %dynamic-slice_bitcast_fusion.8), channel_id=1, source_target_pairs={{0,4},{2,6},{4,0},{6,2},{8,12},{10,14},{12,8},{14,10},{16,20},{18,... | collective-permute-start | bytes 516104 | tf_op jit(solution)/shard_map/ppermute | solution.py:971
  326.5 13.2 %collective-permute-start.21 = (bf16[288,384]{1,0:T(8,128)(2,1)S(1)}, bf16[288,384]{1,0:T(8,128)(2,1)S(1)}, u32[]{:S(2)}, u32[]{:S(2)}) collective-permute-start(bf16[288,384]{1,0:T(8,128)(2,1)S(1)} %dynamic-slice_bitcast_fusion.6), channel_id=1, source_target_pairs={{0,8},{2,10},{4,12},{6,14},{8,0},{10,2},{12,4},{14,6},{16,24},{18,... | collective-permute-start | bytes 663560 | tf_op jit(solution)/shard_map/ppermute | solution.py:971
  326.9 17.6 %collective-permute-start.16 = (bf16[288,384]{1,0:T(8,128)(2,1)S(1)}, bf16[288,384]{1,0:T(8,128)(2,1)S(1)}, u32[]{:S(2)}, u32[]{:S(2)}) collective-permute-start(bf16[288,384]{1,0:T(8,128)(2,1)S(1)} %dynamic-slice_bitcast_fusion.7), channel_id=1, source_target_pairs={{0,8},{2,10},{4,12},{6,14},{8,0},{10,2},{12,4},{14,6},{16,24},{18,... | collective-permute-start | bytes 663560 | tf_op jit(solution)/shard_map/ppermute | solution.py:971
  331.3 14.8 %collective-permute-start.27 = (bf16[112,384]{1,0:T(8,128)(2,1)S(1)}, bf16[112,384]{1,0:T(8,128)(2,1)S(1)}, u32[]{:S(2)}, u32[]{:S(2)}) collective-permute-start(bf16[112,384]{1,0:T(8,128)(2,1)S(1)} %dynamic-slice_bitcast_fusion.11), channel_id=1, source_target_pairs={{0,16},{2,18},{4,20},{6,22},{8,24},{10,26},{12,28},{14,30},{16,0},... | collective-permute-start | bytes 258056 | tf_op jit(solution)/shard_map/ppermute | solution.py:971
  339.8 15.4 %collective-permute-start.22 = (bf16[144,384]{1,0:T(8,128)(2,1)S(1)}, bf16[144,384]{1,0:T(8,128)(2,1)S(1)}, u32[]{:S(2)}, u32[]{:S(2)}) collective-permute-start(bf16[144,384]{1,0:T(8,128)(2,1)S(1)} %dynamic-slice_bitcast_fusion.9), channel_id=1, source_target_pairs={{0,16},{2,18},{4,20},{6,22},{8,24},{10,26},{12,28},{14,30},{16,0},... | collective-permute-start | bytes 331784 | tf_op jit(solution)/shard_map/ppermute | solution.py:971
  344.6 15.3 %collective-permute-start.17 = (bf16[144,384]{1,0:T(8,128)(2,1)S(1)}, bf16[144,384]{1,0:T(8,128)(2,1)S(1)}, u32[]{:S(2)}, u32[]{:S(2)}) collective-permute-start(bf16[144,384]{1,0:T(8,128)(2,1)S(1)} %dynamic-slice_bitcast_fusion.10), channel_id=1, source_target_pairs={{0,16},{2,18},{4,20},{6,22},{8,24},{10,26},{12,28},{14,30},{16,0},... | collective-permute-start | bytes 331784 | tf_op jit(solution)/shard_map/ppermute | solution.py:971
  346.1 16.9 %collective-permute-start.28 = (bf16[112,384]{1,0:T(8,128)(2,1)S(1)}, bf16[112,384]{1,0:T(8,128)(2,1)S(1)}, u32[]{:S(2)}, u32[]{:S(2)}) collective-permute-start(bf16[112,384]{1,0:T(8,128)(2,1)S(1)} %fusion.13), channel_id=1, source_target_pairs={{0,16},{2,18},{4,20},{6,22},{8,24},{10,26},{12,28},{14,30},{16,0},... | collective-permute-start | bytes 258056 | tf_op jit(solution)/shard_map/ppermute | solution.py:976
  355.2 14.8 %collective-permute-start.23 = (bf16[144,384]{1,0:T(8,128)(2,1)S(1)}, bf16[144,384]{1,0:T(8,128)(2,1)S(1)}, u32[]{:S(2)}, u32[]{:S(2)}) collective-permute-start(bf16[144,384]{1,0:T(8,128)(2,1)S(1)} %fusion.11), channel_id=1, source_target_pairs={{0,16},{2,18},{4,20},{6,22},{8,24},{10,26},{12,28},{14,30},{16,0},... | collective-permute-start | bytes 331784 | tf_op jit(solution)/shard_map/ppermute | solution.py:976
  359.9 15.2 %collective-permute-start.18 = (bf16[144,384]{1,0:T(8,128)(2,1)S(1)}, bf16[144,384]{1,0:T(8,128)(2,1)S(1)}, u32[]{:S(2)}, u32[]{:S(2)}) collective-permute-start(bf16[144,384]{1,0:T(8,128)(2,1)S(1)} %fusion.12), channel_id=1, source_target_pairs={{0,16},{2,18},{4,20},{6,22},{8,24},{10,26},{12,28},{14,30},{16,0},... | collective-permute-start | bytes 331784 | tf_op jit(solution)/shard_map/ppermute | solution.py:976
  363.1 12.2 %collective-permute-start.29 = (bf16[224,384]{1,0:T(8,128)(2,1)S(1)}, bf16[224,384]{1,0:T(8,128)(2,1)S(1)}, u32[]{:S(2)}, u32[]{:S(2)}) collective-permute-start(bf16[224,384]{1,0:T(8,128)(2,1)S(1)} %maximum_select_fusion.8), channel_id=1, source_target_pairs={{0,4},{2,6},{4,0},{6,2},{8,12},{10,14},{12,8},{14,10},{16,20},{18,... | collective-permute-start | bytes 516104 | tf_op jit(solution)/shard_map/ppermute | solution.py:976
  370.1 18.8 %collective-permute-start.24 = (bf16[288,384]{1,0:T(8,128)(2,1)S(1)}, bf16[288,384]{1,0:T(8,128)(2,1)S(1)}, u32[]{:S(2)}, u32[]{:S(2)}) collective-permute-start(bf16[288,384]{1,0:T(8,128)(2,1)S(1)} %maximum_select_fusion.7), channel_id=1, source_target_pairs={{0,8},{2,10},{4,12},{6,14},{8,0},{10,2},{12,4},{14,6},{16,24},{18,... | collective-permute-start | bytes 663560 | tf_op jit(solution)/shard_map/ppermute | solution.py:976
  375.2 19.6 %collective-permute-start.19 = (bf16[288,384]{1,0:T(8,128)(2,1)S(1)}, bf16[288,384]{1,0:T(8,128)(2,1)S(1)}, u32[]{:S(2)}, u32[]{:S(2)}) collective-permute-start(bf16[288,384]{1,0:T(8,128)(2,1)S(1)} %maximum_select_fusion.6), channel_id=1, source_target_pairs={{0,8},{2,10},{4,12},{6,14},{8,0},{10,2},{12,4},{14,6},{16,24},{18,... | collective-permute-start | bytes 663560 | tf_op jit(solution)/shard_map/ppermute | solution.py:976
  375.4 45.8 %collective-permute-start.30 = (bf16[448,384]{1,0:T(8,128)(2,1)S(1)}, bf16[448,384]{1,0:T(8,128)(2,1)S(1)}, u32[]{:S(2)}, u32[]{:S(2)}) collective-permute-start(bf16[448,384]{1,0:T(8,128)(2,1)S(1)} %maximum_select_fusion.5), channel_id=1, source_target_pairs={{0,2},{2,0},{4,6},{6,4},{8,10},{10,8},{12,14},{14,12},{16,18},{18,... | collective-permute-start | bytes 1032200 | tf_op jit(solution)/shard_map/ppermute | solution.py:976
  389.1 32.4 %collective-permute-start.25 = (bf16[576,384]{1,0:T(8,128)(2,1)S(1)}, bf16[576,384]{1,0:T(8,128)(2,1)S(1)}, u32[]{:S(2)}, u32[]{:S(2)}) collective-permute-start(bf16[576,384]{1,0:T(8,128)(2,1)S(1)} %maximum_select_fusion.4), channel_id=1, source_target_pairs={{0,2},{2,0},{4,6},{6,4},{8,10},{10,8},{12,14},{14,12},{16,18},{18,... | collective-permute-start | bytes 1327112 | tf_op jit(solution)/shard_map/ppermute | solution.py:976
  394.9 26.9 %collective-permute-start.20 = (bf16[576,384]{1,0:T(8,128)(2,1)S(1)}, bf16[576,384]{1,0:T(8,128)(2,1)S(1)}, u32[]{:S(2)}, u32[]{:S(2)}) collective-permute-start(bf16[576,384]{1,0:T(8,128)(2,1)S(1)} %maximum_select_fusion.3), channel_id=1, source_target_pairs={{0,4},{2,6},{4,0},{6,2},{8,12},{10,14},{12,8},{14,10},{16,20},{18,... | collective-permute-start | bytes 1327112 | tf_op jit(solution)/shard_map/ppermute | solution.py:976
  422.2 26.9 %collective-permute-start.31 = (bf16[1152,384]{1,0:T(8,128)(2,1)S(1)}, bf16[1152,384]{1,0:T(8,128)(2,1)S(1)}, u32[]{:S(2)}, u32[]{:S(2)}) collective-permute-start(bf16[1152,384]{1,0:T(8,128)(2,1)S(1)} %maximum_select_fusion.mine_ref), channel_id=1, source_target_pairs={{0,2},{2,0},{4,6},{6,4},{8,10},{10,8},{12,14},{14,12},{16,18},{18,... | collective-permute-start | bytes 2654216 | tf_op jit(solution)/shard_map/ppermute | solution.py:1191
  423.7 25.3 %collective-permute-start.33 = (bf16[1152,384]{1,0:T(8,128)(2,1)S(1)}, bf16[1152,384]{1,0:T(8,128)(2,1)}, u32[]{:S(2)}, u32[]{:S(2)}) collective-permute-start(bf16[1152,384]{1,0:T(8,128)(2,1)S(1)} %maximum_select_fusion.1.mine_ref), channel_id=1, source_target_pairs={{0,4},{2,6},{4,0},{6,2},{8,12},{10,14},{12,8},{14,10},{16,20},{18,... | collective-permute-start | bytes 2654216 | tf_op jit(solution)/shard_map/ppermute | solution.py:1191
  424.3 24.8 %collective-permute-start.32 = (bf16[896,384]{1,0:T(8,128)(2,1)S(1)}, bf16[896,384]{1,0:T(8,128)(2,1)S(1)}, u32[]{:S(2)}, u32[]{:S(2)}) collective-permute-start(bf16[896,384]{1,0:T(8,128)(2,1)S(1)} %maximum_select_fusion.2.mine_ref), channel_id=1, source_target_pairs={{0,8},{2,10},{4,12},{6,14},{8,0},{10,2},{12,4},{14,6},{16,24},{18,... | collective-permute-start | bytes 2064392 | tf_op jit(solution)/shard_map/ppermute | solution.py:1191
  (9 other events, 8.5 us)
Sparse Core Ops, SparseCore 0:
  96.5 90.1 all-gather.1
  230.2 163.2 all-reduce.2
